TPU v7x, 32 devices: a whole 2x2x4 slice. The times are simulated.
32 devices in a mesh: tm: 2 (over x), lon: 16 (over z, y, core).
Axes of the slice: x: 2, y: 2, z: 4, core: 2. Of those that a mesh axis runs over, the one named last changes fastest.
Arguments:
- snapshots: bfloat16 [2048, 128, 256], P('lon', 'tm'), may hold values from -6 to 6
- test_matrix: float32 [128, 64], replicated, may hold values from -6 to 6
Outputs:
- pod_modes: float32 [64, 327680], P(None, ('lon', 'tm'))
All inputs are finite; a program needn't handle non-finite values.
Results may differ from a plain program's by a relative error of at most 0.0003.
Values may be sent and summed in bfloat16 or wider, within the bound.
No kernel may reach another device: no remote copies, remote signals or barrier semaphores. Data moves between devices by JAX's collectives and lax.ppermute only.
A program may use at most 128 MiB of HBM per device.

v0:
```python
import math

import jax
import jax.numpy as jnp
from jax import lax
from jax.sharding import PartitionSpec as P

NPH = 2048
MMAX = 640
NTH = 256


highest = lax.Precision.HIGHEST


def swapped(array, axis, distance):
    return lax.ppermute(array, axis, [(i, i ^ 1 << distance) for i in range(lax.axis_size(axis))])


def matmul(first_op, second_op):
    return jnp.dot(first_op, second_op, precision=highest, preferred_element_type=jnp.float32)


def spectral_table(points, wave_count):
    lon_ids = jnp.arange(points, dtype=jnp.int32)
    col_ids = jnp.arange(2 * wave_count, dtype=jnp.int32)
    wavenumber = jnp.where(col_ids < wave_count, col_ids, col_ids - wave_count + 1)
    phase_index = lon_ids[:, None] * wavenumber[None, :] % points
    angles = 2.0 * math.pi / points * phase_index.astype(jnp.float32)
    trig_value = jnp.where(col_ids[None, :] < wave_count, jnp.cos(angles), jnp.sin(angles))
    col_scale = math.sqrt(2.0 / points) / jnp.sqrt(
        1.0 + 4.0 * wavenumber.astype(jnp.float32) / wave_count
    )
    return trig_value * col_scale[None, :]


def area_weight(start_row, row_count, total_rows):
    row_ids = start_row + jnp.arange(row_count, dtype=jnp.int32)
    colatitude = math.pi * (row_ids.astype(jnp.float32) + 0.5) / (2.0 * total_rows)
    return jnp.sqrt(jnp.sin(colatitude))


def merge_gram(gram_matrix, test_matrix):
    sketch = matmul(gram_matrix, test_matrix)
    sketch_gram = matmul(sketch.T, gram_matrix)
    power_gram = matmul(sketch_gram, sketch)
    power_gram = 0.5 * (power_gram + power_gram.T)
    chol_first = jnp.linalg.cholesky(power_gram)
    projected = lax.linalg.triangular_solve(chol_first, sketch_gram, left_side=True, lower=True)
    proj_gram = matmul(projected, projected.T)
    chol_second = jnp.linalg.cholesky(0.5 * (proj_gram + proj_gram.T))
    unmixed = lax.linalg.triangular_solve(chol_first, sketch.T, left_side=True, lower=True)
    mixing = matmul(chol_second.T, unmixed)
    return (mixing, matmul(chol_second.T, chol_second))


def block_gram(low_energy, cross_term, high_energy):
    top_rows = jnp.concatenate([low_energy, cross_term], axis=1)
    bottom_rows = jnp.concatenate([cross_term.T, high_energy], axis=1)
    return jnp.concatenate([top_rows, bottom_rows], axis=0)


def combine_pair(mixing, low_modes, high_modes):
    rank_rows = low_modes.shape[0]
    return matmul(mixing[:, :rank_rows], low_modes) + matmul(mixing[:, rank_rows:], high_modes)


def own_columns(modes_flat, group_index, group_count):
    col_count = modes_flat.shape[1] // group_count
    return lax.dynamic_slice_in_dim(modes_flat, group_index * col_count, col_count, 1)


def local(snapshots, test_matrix):
    dev_rows = NTH // lax.axis_size("lon")
    dft_table = spectral_table(NPH, MMAX)
    row_weight = area_weight(lax.axis_index("lon") * dev_rows, dev_rows, NTH)
    spectra = jnp.einsum(
        "pst,pk->stk",
        lax.all_to_all(snapshots, "lon", split_axis=2, concat_axis=0, tiled=True).astype(
            jnp.float32
        ),
        dft_table,
        precision=highest,
    )
    spectra = spectra * row_weight[None, :, None]
    rank_rows = spectra.shape[0]
    modes_now = spectra.reshape(rank_rows, -1)
    levels_count = lax.axis_size("tm").bit_length() - 1
    group_index = lax.axis_index("tm")
    group_count = lax.axis_size("tm")
    energy = lax.psum(matmul(modes_now, modes_now.T), "lon")
    start_level = 0
    for tree_level in range(start_level, levels_count):
        partner_modes, partner_energy = swapped((modes_now, energy), "tm", tree_level)
        is_upper = group_index // 2**tree_level % 2 == 1
        low_modes = jnp.where(is_upper, partner_modes, modes_now)
        high_modes = jnp.where(is_upper, modes_now, partner_modes)
        low_energy = jnp.where(is_upper, partner_energy, energy)
        high_energy = jnp.where(is_upper, energy, partner_energy)
        cross_term = lax.psum(matmul(low_modes, high_modes.T), "lon")
        mixing, energy = merge_gram(block_gram(low_energy, cross_term, high_energy), test_matrix)
        modes_now = combine_pair(mixing, low_modes, high_modes)
    return own_columns(modes_now, group_index, group_count)


def solution(mesh):
    return jax.shard_map(
        local,
        mesh=mesh,
        in_specs=(P("lon", "tm", None), P()),
        out_specs=P(None, ("lon", "tm")),
        check_vma=False,
    )
```

profile of v0, /device:TPU:0, one launch (start us, length us, event | category | flops | bytes accessed | tf_op | source)
XLA Modules:
  0.0 359.0 jit_solution(2334400126653114431)
XLA Ops:
  0.0 0.0 copy-start
  0.0 7.4 %copy.17 = bf16[128,64,256]{0,1,2:T(8,128)(2,1)} copy(bf16[128,64,256]{2,1,0:T(8,128)(2,1)} %param.5) | data formatting | bytes 8388608 | tf_op args[0]
  7.4 7.4 %all-to-all-start = ((bf16[128,64,256]{0,1,2:T(8,128)(2,1)}), bf16[128,64,256]{0,1,2:T(8,128)(2,1)}, u32[]{:S(2)}, u32[]{:S(2)}) async-start(bf16[128,64,256]{0,1,2:T(8,128)(2,1)} %copy.17), calls=%async_computation | async-start | bytes 8388608 | tf_op jit(solution)/shard_map/all_to_all | solution.py:79
  14.9 43.2 %fusion.77 = f32[2048,1280,1]{1,0,2:T(8,128)} fusion(f32[1280]{0:T(1024)S(1)} %rsqrt_multiply_fusion, s32[1280]{0:T(1024)S(1)} %add_select_fusion.1, pred[1280]{0:T(1024)(128)(4,1)S(1)} %iota_compare_fusion.3), kind=kLoop, calls=%fused_computation.7.clone.1 | loop fusion | flops 41943040 | bytes 10497280 | tf_op jit(solution)/shard_map/pst,pk->stk/dot_general | solution.py:77
  58.2 34.3 %all-to-all-done = bf16[128,64,256]{0,1,2:T(8,128)(2,1)} async-done(((bf16[128,64,256]{0,1,2:T(8,128)(2,1)}), bf16[128,64,256]{0,1,2:T(8,128)(2,1)}, u32[]{:S(2)}, u32[]{:S(2)}) %all-to-all-start) | async-done | bytes 4194336 | tf_op jit(solution)/shard_map/all_to_all | solution.py:79
  92.5 21.6 %fusion.3 = f32[1280,64,16]{0,1,2:T(8,128)S(1)} fusion(bf16[16,16,8,8,128]{4,3,2,1,0:T(8,128)(2,1)} %bitcast.16, f32[2048,1280,1]{1,0,2:T(8,128)} %fusion.77), kind=kOutput, calls=%fused_computation.6 | convolution fusion | flops 32212254720 | bytes 19922944 | tf_op jit(solution)/shard_map/pst,pk->stk/dot_general | solution.py:77
  114.1 0.0 copy-start.1
  114.1 0.6 multiply_bitcast_fusion
  114.7 1.8 copy-done.1
  116.5 2.8 copy.28
  119.2 1.5 collective-permute-start.1
  120.7 8.9 %fusion.31 = f32[64,64]{1,0:T(8,128)S(1)} fusion(f32[1280,64,16]{0,1,2:T(8,128)} %copy-done.1, f32[16]{0:T(128)S(1)} %sine_sqrt_fusion), kind=kOutput, calls=%fused_computation.35 | convolution fusion | flops 1007943680 | bytes 5259328 | tf_op jit(solution)/shard_map/dot_general | solution.py:21
  129.6 105.7 %collective-permute-done.1 = f32[64,20480]{1,0:T(8,128)} collective-permute-done((f32[64,20480]{1,0:T(8,128)}, f32[64,20480]{1,0:T(8,128)}, u32[]{:S(2)}, u32[]{:S(2)}) %collective-permute-start.1) | collective-permute-done | bytes 5242912 | tf_op jit(solution)/shard_map/ppermute | solution.py:17
  235.3 8.7 %fusion.29 = f32[64,64]{1,0:T(8,128)S(1)} fusion(f32[64,20480]{1,0:T(8,128)} %collective-permute-done.1, f32[64,20480]{1,0:T(8,128)} %bitcast.19, pred[]{:T(512)S(6)} %eq.7), kind=kOutput, calls=%fused_computation.33 | convolution fusion | flops 1009254400 | bytes 10502145 | tf_op jit(solution)/shard_map/dot_general | solution.py:21
  244.0 74.5 %all-reduce = (f32[64,64]{1,0:T(8,128)S(1)}, f32[64,64]{1,0:T(8,128)S(1)}) all-reduce(f32[64,64]{1,0:T(8,128)S(1)} %fusion.31, f32[64,64]{1,0:T(8,128)S(1)} %fusion.29), channel_id=1, replica_groups=mesh['tm'=2,'lon'=16] {'lon'}, use_global_device_ids=true, to_apply=%region_0.1 | all-reduce | flops 8192 | bytes 65536 | tf_op jit(solution)/shard_map/psum | solution.py:91
  318.5 1.5 collective-permute-start
  320.0 0.1 copy.21
  320.0 2.3 collective-permute-done
  322.4 0.0 copy-done
  322.4 0.3 fusion.55
  322.7 0.3 fusion.54
  323.0 0.2 fusion.64
  323.2 0.1 copy.22
  323.3 0.1 copy.23
  323.4 5.8 %cholesky.44 = f32[64,64]{1,0:T(8,128)S(1)} custom-call(f32[64,64]{1,0:T(8,128)S(1)} %fusion.44), custom_call_target="Cholesky" | custom-call | tf_op jit(solution)/shard_map/jit(cholesky)/cholesky | solution.py:48
  329.3 0.6 compare_reduce_fusion.1
  329.9 0.7 fusion.34
  330.6 4.9 %custom-call.6 = f32[1,64,64]{1,2,0:T(8,128)S(1)} custom-call(f32[1,64,64]{2,1,0:T(8,128)S(1)} %fusion.34), custom_call_target="InvertDiagBlocksLowerTriangular" | custom-call | tf_op jit(solution)/shard_map/triangular_solve/custom-call.0 | solution.py:49
  335.5 0.3 fusion.37
  335.7 0.2 fusion.42
  336.0 0.2 fusion.65
  336.1 0.1 copy.24
  336.2 0.1 copy.25
  336.3 5.8 %cholesky.55 = f32[64,64]{1,0:T(8,128)S(1)} custom-call(f32[64,64]{1,0:T(8,128)S(1)} %fusion.39), custom_call_target="Cholesky" | custom-call | tf_op jit(solution)/shard_map/jit(cholesky)/cholesky | solution.py:51
  342.2 0.6 compare_reduce_fusion
  342.9 0.9 fusion.46
  343.7 6.9 %fusion.30 = f32[64,20480]{1,0:T(8,128)S(1)} fusion(f32[64,20480]{1,0:T(8,128)} %bitcast.19, f32[64,20480]{1,0:T(8,128)} %collective-permute-done.1, pred[]{:T(512)S(6)} %eq.7, f32[64,128]{1,0:T(8,128)S(1)} %fusion.46), kind=kOutput, calls=%fused_computation.34 | convolution fusion | flops 1007943680 | bytes 15761409 | tf_op jit(solution)/shard_map/dot_general | solution.py:21
  350.7 6.5 %fusion.28 = f32[64,20480]{1,0:T(8,128)S(1)} fusion(f32[64,20480]{1,0:T(8,128)} %collective-permute-done.1, f32[64,20480]{1,0:T(8,128)} %bitcast.19, pred[]{:T(512)S(6)} %eq.7, f32[64,128]{1,0:T(8,128)S(1)} %fusion.46), kind=kOutput, calls=%fused_computation.32 | convolution fusion | flops 1007943680 | bytes 15761409 | tf_op jit(solution)/shard_map/dot_general | solution.py:21
  357.2 1.8 dynamic-slice_add_fusion
  (11 shorter events, 0.2 us)
Async XLA Ops:
  0.0 322.4 %copy-start = (f32[128,64]{0,1:T(8,128)S(1)}, f32[128,64]{0,1:T(8,128)}, u32[]{:S(2)}) copy-start(f32[128,64]{0,1:T(8,128)} %param.6) | copy-start | bytes 98308
  7.4 85.1 %all-to-all-start = ((bf16[128,64,256]{0,1,2:T(8,128)(2,1)}), bf16[128,64,256]{0,1,2:T(8,128)(2,1)}, u32[]{:S(2)}, u32[]{:S(2)}) async-start(bf16[128,64,256]{0,1,2:T(8,128)(2,1)} %copy.17), calls=%async_computation | async-start | bytes 8388608 | tf_op jit(solution)/shard_map/all_to_all | solution.py:79
  114.1 2.4 copy-start.1
  119.2 116.0 %collective-permute-start.1 = (f32[64,20480]{1,0:T(8,128)}, f32[64,20480]{1,0:T(8,128)}, u32[]{:S(2)}, u32[]{:S(2)}) collective-permute-start(f32[64,20480]{1,0:T(8,128)} %bitcast.19), channel_id=1, source_target_pairs={{0,16},{16,0},{1,17},{17,1},{2,18},{18,2},{3,19},{19,3},{4,20},{20... | collective-permute-start | bytes 15728648 | tf_op jit(solution)/shard_map/ppermute | solution.py:17
  318.5 3.9 %collective-permute-start = (f32[64,64]{1,0:T(8,128)S(1)}, f32[64,64]{1,0:T(8,128)S(1)}, u32[]{:S(2)}, u32[]{:S(2)}) collective-permute-start(f32[64,64]{1,0:T(8,128)S(1)} %get-tuple-element.6), channel_id=1, source_target_pairs={{0,16},{16,0},{1,17},{17,1},{2,18},{18,2},{3,19},{19,3},{4,20},{20... | collective-permute-start | bytes 49160 | tf_op jit(solution)/shard_map/ppermute | solution.py:17
where the time goes:
time: 359 us
  waiting for transfers between devices  142 us (40%)
  blocking collectives  74.5 us (21%)
  other arithmetic  64.3 us (18%)
  matrix products  54.9 us (15%)
  local copies, waits for them, and re-layouts  12.3 us (3%)
  starting transfers between devices  10.4 us (3%)
    ppermute x2, waiting for transfers between devices, swapped(): lax.ppermute(array, axis, [(i, i ^ 1 << distance) for i in range(lax.axis...  108 us
    psum x1, blocking collectives, local(): energy = lax.psum(matmul(modes_now, modes_now.T), 'lon')  74.5 us
    dot_general x1, other arithmetic, local(): jnp.einsum('pst,pk->stk', lax.all_to_all(snapshots, 'lon', split_axis=2,...  43.2 us
    all_to_all x1, waiting for transfers between devices, local(): lax.all_to_all(snapshots, 'lon', split_axis=2, concat_axis=0, tiled=True)  34.3 us
    dot_general x9, matrix products, matmul(): jnp.dot(first_op, second_op, precision=highest, preferred_element_type=jn...  32.8 us
    dot_general x1, matrix products, local(): jnp.einsum('pst,pk->stk', lax.all_to_all(snapshots, 'lon', split_axis=2,...  21.6 us
    unnamed x5, local copies, waits for them, and re-layouts  9.16 us
    all_to_all x1, starting transfers between devices, local(): lax.all_to_all(snapshots, 'lon', split_axis=2, concat_axis=0, tiled=True)  7.44 us
  transfers between devices with their start and end apart: 3, of which 3 were waited for; matrix products, arithmetic and copies ran while one was open for 15% of the time, Pallas kernels for 0%

commit v1 on v0

--- a/solution.py
+++ b/solution.py
@@ -1,16 +1,21 @@
+import functools
 import math
 
 import jax
 import jax.numpy as jnp
 from jax import lax
+from jax.experimental import pallas as pl
+from jax.experimental.pallas import tpu as pltpu
 from jax.sharding import PartitionSpec as P
 
 NPH = 2048
 MMAX = 640
 NTH = 256
+COL_TILE = 256
 
 
 highest = lax.Precision.HIGHEST
+NT_DIMS = (((1,), (1,)), ((), ()))
 
 
 def swapped(array, axis, distance):
@@ -70,7 +75,7 @@
     return lax.dynamic_slice_in_dim(modes_flat, group_index * col_count, col_count, 1)
 
 
-def local(snapshots, test_matrix):
+def local_tree(snapshots, test_matrix):
     dev_rows = NTH // lax.axis_size("lon")
     dft_table = spectral_table(NPH, MMAX)
     row_weight = area_weight(lax.axis_index("lon") * dev_rows, dev_rows, NTH)
@@ -103,9 +108,182 @@
     return own_columns(modes_now, group_index, group_count)
 
 
+def split_table(points, wave_count):
+    table = spectral_table(points, wave_count)
+    high = lax.reduce_precision(table, 8, 7)
+    return high.astype(jnp.bfloat16), (table - high).astype(jnp.bfloat16)
+
+
+def spectra_kernel(weight_ref, x_ref, high_ref, low_ref, xh_ref, xl_ref, gram_ref, lhs, acc):
+    sources, groups, rows, rank_rows, points = x_ref.shape
+    step = pl.program_id(0)
+
+    @pl.when(step == 0)
+    def _():
+        acc[...] = jnp.zeros_like(acc)
+        for src in range(sources):
+            for grp in range(groups):
+                for row in range(rows):
+                    start = (row * groups + grp) * rank_rows
+                    lhs[start : start + rank_rows, src * points : (src + 1) * points] = x_ref[
+                        src, grp, row
+                    ]
+
+    span = groups * rank_rows
+    block_rows = min(rows, 2) * span
+    for start in range(0, rows * span, block_rows):
+        values = lhs[start : start + block_rows, :]
+        spectra = jnp.dot(values, high_ref[...], preferred_element_type=jnp.float32)
+        spectra += jnp.dot(values, low_ref[...], preferred_element_type=jnp.float32)
+        for part in range(0, block_rows, span):
+            row = (start + part) // span
+            scaled = spectra[part : part + span] * weight_ref[0, row]
+            top = scaled.astype(jnp.bfloat16)
+            rest = (scaled - top.astype(jnp.float32)).astype(jnp.bfloat16)
+            xh_ref[row] = top
+            xl_ref[row] = rest
+            acc[...] += lax.dot_general(
+                jnp.concatenate([top, rest], axis=0), top, NT_DIMS, preferred_element_type=jnp.float32
+            )
+
+    @pl.when(step == pl.num_programs(0) - 1)
+    def _():
+        cross = acc[span:, :]
+        gram_ref[...] = acc[:span, :] + (cross + cross.T)
+
+
+def spectra_and_gram(blocks, row_weight, table_high, table_low):
+    sources, groups, rows, rank_rows, points = blocks.shape
+    lons, cols = table_high.shape
+    span = groups * rank_rows
+    modes = jax.ShapeDtypeStruct((rows, span, cols), jnp.bfloat16)
+    return pl.pallas_call(
+        spectra_kernel,
+        grid=(cols // COL_TILE,),
+        in_specs=[
+            pl.BlockSpec(memory_space=pltpu.SMEM),
+            pl.BlockSpec(blocks.shape, lambda i: (0, 0, 0, 0, 0)),
+            pl.BlockSpec((lons, COL_TILE), lambda i: (0, i)),
+            pl.BlockSpec((lons, COL_TILE), lambda i: (0, i)),
+        ],
+        out_specs=[
+            pl.BlockSpec((rows, span, COL_TILE), lambda i: (0, 0, i)),
+            pl.BlockSpec((rows, span, COL_TILE), lambda i: (0, 0, i)),
+            pl.BlockSpec((span, span), lambda i: (0, 0)),
+        ],
+        out_shape=[modes, modes, jax.ShapeDtypeStruct((span, span), jnp.float32)],
+        scratch_shapes=[
+            pltpu.VMEM((rows * span, lons), jnp.bfloat16),
+            pltpu.VMEM((2 * span, span), jnp.float32),
+        ],
+        compiler_params=pltpu.CompilerParams(vmem_limit_bytes=48 * 2**20),
+        cost_estimate=pl.CostEstimate(
+            flops=4 * rows * span * lons * cols,
+            bytes_accessed=2 * blocks.size + 4 * lons * cols + 4 * rows * span * cols,
+            transcendentals=0,
+        ),
+    )(row_weight.reshape(1, rows), blocks, table_high, table_low)
+
+
+def dot_full(first, second, dims=(((1,), (0,)), ((), ()))):
+    return lax.dot_general(
+        first, second, dims, precision=highest, preferred_element_type=jnp.float32
+    )
+
+
+def eliminate(work, size):
+    height, width = work.shape
+    row_ids = lax.broadcasted_iota(jnp.int32, (height, width), 0)
+    result = jnp.zeros_like(work)
+    for col in range(size):
+        pivot = work[col : col + 1, :]
+        inverse = lax.rsqrt(work[col : col + 1, col : col + 1])
+        scaled_row = pivot * inverse
+        factor = work[:, col : col + 1] * inverse
+        result = jnp.where(row_ids == col, scaled_row, result)
+        work = work - factor * scaled_row
+    return result
+
+
+def merge_kernel(gram_ref, test_ref, xh_ref, xl_ref, out_ref, mix_ref):
+    rank = test_ref.shape[1]
+    row = pl.program_id(0)
+
+    @pl.when(row == 0)
+    def _():
+        gram = gram_ref[...]
+        test = test_ref[...]
+        sketch = dot_full(gram, test)
+        sketch_t = dot_full(test, gram, (((0,), (0,)), ((), ())))
+        sketch_gram = dot_full(sketch_t, gram)
+        power = dot_full(sketch_gram, sketch)
+        power = 0.5 * (power + power.T)
+        solved = eliminate(jnp.concatenate([power, jnp.zeros_like(power), sketch_gram, sketch_t], axis=1), rank)
+        projected = solved[:, 2 * rank : 4 * rank]
+        unmixed = solved[:, 4 * rank : 6 * rank]
+        inner = dot_full(projected, projected, NT_DIMS)
+        upper = eliminate(0.5 * (inner + inner.T), rank)
+        col_ids = lax.broadcasted_iota(jnp.int32, upper.shape, 1)
+        row_ids = lax.broadcasted_iota(jnp.int32, upper.shape, 0)
+        mixing = dot_full(jnp.where(col_ids >= row_ids, upper, 0.0), unmixed)
+        top = mixing.astype(jnp.bfloat16)
+        rest = (mixing - top.astype(jnp.float32)).astype(jnp.bfloat16)
+        mix_ref[:rank, : 2 * rank] = top
+        mix_ref[:rank, 2 * rank :] = top
+        mix_ref[rank:, : 2 * rank] = rest
+        mix_ref[rank:, 2 * rank :] = jnp.zeros_like(rest)
+
+    stacked = jnp.concatenate([xh_ref[0], xl_ref[0]], axis=0)
+    both = jnp.dot(mix_ref[...], stacked, preferred_element_type=jnp.float32)
+    out_ref[...] = both[:rank] + both[rank:]
+
+
+def merge_and_mix(gram, test_matrix, modes_high, modes_low):
+    rows, span, cols = modes_high.shape
+    rank = test_matrix.shape[1]
+    return pl.pallas_call(
+        merge_kernel,
+        grid=(rows,),
+        in_specs=[
+            pl.BlockSpec(gram.shape, lambda i: (0, 0)),
+            pl.BlockSpec(test_matrix.shape, lambda i: (0, 0)),
+            pl.BlockSpec((1, span, cols), lambda i: (i, 0, 0)),
+            pl.BlockSpec((1, span, cols), lambda i: (i, 0, 0)),
+        ],
+        out_specs=pl.BlockSpec((rank, cols), lambda i: (0, i)),
+        out_shape=jax.ShapeDtypeStruct((rank, rows * cols), jnp.float32),
+        scratch_shapes=[pltpu.VMEM((2 * rank, 2 * span), jnp.bfloat16)],
+        compiler_params=pltpu.CompilerParams(vmem_limit_bytes=32 * 2**20),
+    )(gram, test_matrix, modes_high, modes_low)
+
+
+def summed(array, axes):
+    for axis in axes:
+        for distance in range(lax.axis_size(axis).bit_length() - 1):
+            array = array + swapped(array, axis, distance)
+    return array
+
+
+def local_pair(snapshots, test_matrix):
+    points, rank_rows, total_rows = snapshots.shape
+    lon_count, group_count = lax.axis_size("lon"), lax.axis_size("tm")
+    dev_rows = total_rows // (lon_count * group_count)
+    first_row = (lax.axis_index("lon") * group_count + lax.axis_index("tm")) * dev_rows
+    row_weight = area_weight(first_row, dev_rows, NTH)
+    table_high, table_low = split_table(NPH, MMAX)
+    blocks = lax.all_to_all(
+        snapshots.transpose(2, 1, 0), ("lon", "tm"), split_axis=0, concat_axis=0, tiled=True
+    ).reshape(lon_count, group_count, dev_rows, rank_rows, points)
+    modes_high, modes_low, gram = spectra_and_gram(blocks, row_weight, table_high, table_low)
+    gram = summed(gram, ("lon", "tm"))
+    return merge_and_mix(gram, test_matrix, modes_high, modes_low)
+
+
 def solution(mesh):
+    lon_count, group_count = mesh.shape["lon"], mesh.shape["tm"]
+    whole_rows = NTH % (lon_count * group_count) == 0
     return jax.shard_map(
-        local,
+        local_pair if group_count == 2 and whole_rows else local_tree,
         mesh=mesh,
         in_specs=(P("lon", "tm", None), P()),
         out_specs=P(None, ("lon", "tm")),

time: 359 us -> 174 us (0.48)
  waiting for transfers between devices: 142 us -> 65.1 us
  blocking collectives: 74.5 us -> 0 us
  matrix products: 54.9 us -> 0 us
  Pallas kernels: 0 us -> 41.6 us
  other arithmetic: 64.3 us -> 44.7 us
    ppermute x2 -> x5, waiting for transfers between devices: 108 us -> 16.1 us  [swapped(): lax.ppermute(array, axis, [(i, i ^ 1 << distance) for i in range(lax.axis...]
    psum x1 -> x0, blocking collectives: 74.5 us -> none  [local(): energy = lax.psum(matmul(modes_now, modes_now.T), 'lon')]
    dot_general x10 -> x0, matrix products: 54.4 us -> none  [the longest x9 32.8 us: matmul(): jnp.dot(first_op, second_op, precision=highest, preferred_element_type=jn...]
    convert_element_type x0 -> x1, other arithmetic: none -> 44.6 us  [split_table(): return (high.astype(jnp.bfloat16), (table - high).astype(jnp.bfloat16))]
    dot_general x1 -> x0, other arithmetic: 43.2 us -> none  [local(): jnp.einsum('pst,pk->stk', lax.all_to_all(snapshots, 'lon', split_axis=2,...]
    pallas_call x0 -> x2, Pallas kernels: none -> 41.6 us  [the longest x1 25.7 us: spectra_and_gram(): pl.pallas_call(spectra_kernel, grid=(cols // COL_TILE,), in_specs=[pl.Blo...]
    another operation x8 -> x0, other arithmetic: 18.6 us -> none  [the longest x3 6.52 us: merge_gram(): chol_first = jnp.linalg.cholesky(power_gram)]
    all_to_all x1, waiting for transfers between devices: 34.3 us -> 49 us  [local_pair(): lax.all_to_all(snapshots.transpose(2, 1, 0), ('lon', 'tm'), split_axis=0,...]
  transfers between devices with their start and end apart: 3 -> 6, of which waited for: 3 -> 6; matrix products, arithmetic and copies ran while one was open for 15% -> 26% of each run, Pallas kernels for 0% -> 0%
where the time goes in v1:
time: 174 us
  waiting for transfers between devices  65.1 us (37%)
  other arithmetic  44.7 us (26%)
  Pallas kernels  41.6 us (24%)
  starting transfers between devices  11.4 us (7%)
  local copies, waits for them, and re-layouts  10.7 us (6%)
    all_to_all x1, waiting for transfers between devices, local_pair(): lax.all_to_all(snapshots.transpose(2, 1, 0), ('lon', 'tm'), split_axis=0,...  49 us
    convert_element_type x1, other arithmetic, split_table(): return (high.astype(jnp.bfloat16), (table - high).astype(jnp.bfloat16))  44.6 us
    pallas_call x1, Pallas kernels, spectra_and_gram(): pl.pallas_call(spectra_kernel, grid=(cols // COL_TILE,), in_specs=[pl.Blo...  25.7 us
    ppermute x5, waiting for transfers between devices, swapped(): lax.ppermute(array, axis, [(i, i ^ 1 << distance) for i in range(lax.axis...  16.1 us
    pallas_call x1, Pallas kernels, merge_and_mix(): pl.pallas_call(merge_kernel, grid=(rows,), in_specs=[pl.BlockSpec(gram.sh...  15.9 us
    unnamed x8, local copies, waits for them, and re-layouts  10.7 us
    all_to_all x1, starting transfers between devices, local_pair(): lax.all_to_all(snapshots.transpose(2, 1, 0), ('lon', 'tm'), split_axis=0,...  7.43 us
    ppermute x5, starting transfers between devices, swapped(): lax.ppermute(array, axis, [(i, i ^ 1 << distance) for i in range(lax.axis...  3.96 us
  transfers between devices with their start and end apart: 6, of which 6 were waited for; matrix products, arithmetic and copies ran while one was open for 26% of the time, Pallas kernels for 0%

profile of v1, /device:TPU:0, one launch (start us, length us, event | category | flops | bytes accessed | tf_op | source)
XLA Modules:
  0.0 173.6 jit_solution(9378399458139835626)
XLA Ops:
  0.0 7.4 %copy.8 = bf16[128,64,256]{0,1,2:T(8,128)(2,1)} copy(bf16[128,64,256]{2,1,0:T(8,128)(2,1)} %param.2) | data formatting | bytes 8388608 | tf_op args[0]
  7.4 7.4 %all-to-all-start = ((bf16[256,64,128]{2,1,0:T(8,128)(2,1)}), bf16[256,64,128]{2,1,0:T(8,128)(2,1)}, u32[]{:S(2)}, u32[]{:S(2)}) async-start(bf16[256,64,128]{2,1,0:T(8,128)(2,1)} %bitcast.2), calls=%async_computation | async-start | bytes 8388608 | tf_op jit(solution)/shard_map/all_to_all | solution.py:274
  14.9 44.6 %fusion = (bf16[2048,1280]{1,0:T(8,128)(2,1)}, bf16[2048,1280]{1,0:T(8,128)(2,1)}) fusion(f32[1280]{0:T(1024)S(1)} %rsqrt_multiply_fusion, s32[1280]{0:T(1024)S(1)} %add_select_fusion.1, pred[1280]{0:T(1024)(128)(4,1)S(1)} %iota_compare_fusion), kind=kLoop, calls=%fused_computation.5 | loop fusion | flops 52428800 | bytes 10497280 | tf_op jit(solution)/shard_map/convert_element_type | solution.py:114
  59.5 49.0 %all-to-all-done = bf16[256,64,128]{2,1,0:T(8,128)(2,1)} async-done(((bf16[256,64,128]{2,1,0:T(8,128)(2,1)}), bf16[256,64,128]{2,1,0:T(8,128)(2,1)}, u32[]{:S(2)}, u32[]{:S(2)}) %all-to-all-start) | async-done | bytes 4194336 | tf_op jit(solution)/shard_map/all_to_all | solution.py:274
  108.5 0.0 copy-start.2
  108.5 25.7 %shard_map.28 = (bf16[8,128,1280]{2,1,0:T(8,128)(2,1)S(1)}, bf16[8,128,1280]{2,1,0:T(8,128)(2,1)S(1)}, f32[128,128]{1,0:T(8,128)S(1)}) custom-call(f32[1,8]{1,0:T(1,128)S(1)} %sine_sqrt_fusion.weight_ref, bf16[16,2,8,64,128]{4,3,2,1,0:T(8,128)(2,1)} %bitcast.1.x_ref, bf16[2048,1280]{1,0:T(8,128)(2,1)} %get-tuple-element.12.high_ref, ...), custom_call_target="tpu_custom_call" | custom-call | flops 10737418240 | bytes 19922944 | tf_op jit(solution)/shard_map/pallas_call | solution.py:160
  134.3 0.0 copy-start
  134.3 1.5 copy-done
  135.8 0.0 collective-permute-start
  135.8 1.3 collective-permute-done
  137.0 1.4 collective-permute-start.1
  138.5 2.9 %collective-permute-done.1 = f32[128,128]{1,0:T(8,128)S(1)} collective-permute-done((f32[128,128]{1,0:T(8,128)S(1)}, f32[128,128]{1,0:T(8,128)S(1)}, u32[]{:S(2)}, u32[]{:S(2)}) %collective-permute-start.1) | collective-permute-done | bytes 65568 | tf_op jit(solution)/shard_map/ppermute | solution.py:22
  141.4 0.1 collective-permute-start.2
  141.5 4.2 %collective-permute-done.2 = f32[128,128]{1,0:T(8,128)S(1)} collective-permute-done((f32[128,128]{1,0:T(8,128)S(1)}, f32[128,128]{1,0:T(8,128)S(1)}, u32[]{:S(2)}, u32[]{:S(2)}) %collective-permute-start.2) | collective-permute-done | bytes 65568 | tf_op jit(solution)/shard_map/ppermute | solution.py:22
  145.7 1.5 collective-permute-start.3
  147.2 4.4 %collective-permute-done.3 = f32[128,128]{1,0:T(8,128)S(1)} collective-permute-done((f32[128,128]{1,0:T(8,128)S(1)}, f32[128,128]{1,0:T(8,128)S(1)}, u32[]{:S(2)}, u32[]{:S(2)}) %collective-permute-start.3) | collective-permute-done | bytes 65568 | tf_op jit(solution)/shard_map/ppermute | solution.py:22
  151.6 0.9 collective-permute-start.4
  152.5 0.0 copy-done.2
  152.5 0.1 copy.9.test_ref
  152.6 3.3 %collective-permute-done.4 = f32[128,128]{1,0:T(8,128)S(1)} collective-permute-done((f32[128,128]{1,0:T(8,128)S(1)}, f32[128,128]{1,0:T(8,128)S(1)}, u32[]{:S(2)}, u32[]{:S(2)}) %collective-permute-start.4) | collective-permute-done | bytes 65568 | tf_op jit(solution)/shard_map/ppermute | solution.py:22
  155.9 0.0 copy-start.1
  155.9 1.7 copy-done.1
  157.7 15.9 %shard_map.29 = f32[64,10240]{1,0:T(8,128)} custom-call(f32[128,128]{1,0:T(8,128)S(1)} %add.94.gram_ref, f32[128,64]{1,0:T(8,128)S(1)} %copy.9.test_ref, bf16[8,128,1280]{2,1,0:T(8,128)(2,1)S(1)} %get-tuple-element.9.xh_ref, bf16[8,128,1280]{2,1,0:T(8,128)(2,1)S(1)} %copy-done.1), custom_call_target="tpu_custom_call" | custom-call | tf_op jit(solution)/shard_map/pallas_call | solution.py:244
  (9 shorter events, 0.1 us)
Async XLA Ops:
  7.4 101.2 %all-to-all-start = ((bf16[256,64,128]{2,1,0:T(8,128)(2,1)}), bf16[256,64,128]{2,1,0:T(8,128)(2,1)}, u32[]{:S(2)}, u32[]{:S(2)}) async-start(bf16[256,64,128]{2,1,0:T(8,128)(2,1)} %bitcast.2), calls=%async_computation | async-start | bytes 8388608 | tf_op jit(solution)/shard_map/all_to_all | solution.py:274
  108.5 44.0 %copy-start.2 = (f32[128,64]{0,1:T(8,128)S(1)}, f32[128,64]{0,1:T(8,128)}, u32[]{:S(2)}) copy-start(f32[128,64]{0,1:T(8,128)} %param.3) | copy-start | bytes 98308
  134.3 1.5 copy-start
  135.8 1.3 collective-permute-start
  137.0 4.3 %collective-permute-start.1 = (f32[128,128]{1,0:T(8,128)S(1)}, f32[128,128]{1,0:T(8,128)S(1)}, u32[]{:S(2)}, u32[]{:S(2)}) collective-permute-start(f32[128,128]{1,0:T(8,128)S(1)} %add.90), channel_id=1, source_target_pairs={{0,2},{1,3},{2,0},{3,1},{4,6},{5,7},{6,4},{7,5},{8,10},{9,11},{10,... | collective-permute-start | bytes 196616 | tf_op jit(solution)/shard_map/ppermute | solution.py:22
  141.4 4.3 %collective-permute-start.2 = (f32[128,128]{1,0:T(8,128)S(1)}, f32[128,128]{1,0:T(8,128)S(1)}, u32[]{:S(2)}, u32[]{:S(2)}) collective-permute-start(f32[128,128]{1,0:T(8,128)S(1)} %add.91), channel_id=1, source_target_pairs={{0,4},{1,5},{2,6},{3,7},{4,0},{5,1},{6,2},{7,3},{8,12},{9,13},{10,... | collective-permute-start | bytes 196616 | tf_op jit(solution)/shard_map/ppermute | solution.py:22
  145.7 5.9 %collective-permute-start.3 = (f32[128,128]{1,0:T(8,128)S(1)}, f32[128,128]{1,0:T(8,128)S(1)}, u32[]{:S(2)}, u32[]{:S(2)}) collective-permute-start(f32[128,128]{1,0:T(8,128)S(1)} %add.92), channel_id=1, source_target_pairs={{0,8},{1,9},{2,10},{3,11},{4,12},{5,13},{6,14},{7,15},{8,0},{9,1},... | collective-permute-start | bytes 196616 | tf_op jit(solution)/shard_map/ppermute | solution.py:22
  151.6 4.3 %collective-permute-start.4 = (f32[128,128]{1,0:T(8,128)S(1)}, f32[128,128]{1,0:T(8,128)S(1)}, u32[]{:S(2)}, u32[]{:S(2)}) collective-permute-start(f32[128,128]{1,0:T(8,128)S(1)} %add.93), channel_id=1, source_target_pairs={{0,16},{16,0},{1,17},{17,1},{2,18},{18,2},{3,19},{19,3},{4,20},{20... | collective-permute-start | bytes 196616 | tf_op jit(solution)/shard_map/ppermute | solution.py:22
  155.9 1.7 %copy-start.1 = (bf16[8,128,1280]{2,1,0:T(8,128)(2,1)S(1)}, bf16[8,128,1280]{2,1,0:T(8,128)(2,1)}, u32[]{:S(2)}) copy-start(bf16[8,128,1280]{2,1,0:T(8,128)(2,1)} %copy-done) | copy-start | bytes 7864324

commit v2 on v1

--- a/solution.py
+++ b/solution.py
@@ -12,6 +12,9 @@
 MMAX = 640
 NTH = 256
 COL_TILE = 256
+LANES = 128
+PIVOTS = 4
+VMEM_BYTES = 59 * 2**20
 
 
 highest = lax.Precision.HIGHEST
@@ -130,32 +133,36 @@
                     ]
 
     span = groups * rank_rows
-    block_rows = min(rows, 2) * span
-    for start in range(0, rows * span, block_rows):
-        values = lhs[start : start + block_rows, :]
-        spectra = jnp.dot(values, high_ref[...], preferred_element_type=jnp.float32)
-        spectra += jnp.dot(values, low_ref[...], preferred_element_type=jnp.float32)
-        for part in range(0, block_rows, span):
-            row = (start + part) // span
-            scaled = spectra[part : part + span] * weight_ref[0, row]
-            top = scaled.astype(jnp.bfloat16)
-            rest = (scaled - top.astype(jnp.float32)).astype(jnp.bfloat16)
-            xh_ref[row] = top
-            xl_ref[row] = rest
-            acc[...] += lax.dot_general(
-                jnp.concatenate([top, rest], axis=0), top, NT_DIMS, preferred_element_type=jnp.float32
-            )
+    values = lhs[...]
+    spectra = jnp.dot(values, high_ref[...], preferred_element_type=jnp.float32)
+    spectra += jnp.dot(values, low_ref[...], preferred_element_type=jnp.float32)
+    tops, rests = [], []
+    for row in range(rows):
+        scaled = spectra[row * span : (row + 1) * span] * weight_ref[0, row]
+        top = scaled.astype(jnp.bfloat16)
+        rest = (scaled - top.astype(jnp.float32)).astype(jnp.bfloat16)
+        xh_ref[row] = top
+        xl_ref[row] = rest
+        tops.append(top)
+        rests.append(rest)
+    top = jnp.concatenate(tops, axis=1)
+    both = jnp.concatenate([top, jnp.concatenate(rests, axis=1)], axis=0)
+    acc[...] += lax.dot_general(both, top, NT_DIMS, preferred_element_type=jnp.float32)
 
     @pl.when(step == pl.num_programs(0) - 1)
     def _():
         cross = acc[span:, :]
-        gram_ref[...] = acc[:span, :] + (cross + cross.T)
+        gram = acc[:span, :] + (cross + cross.T)
+        gram_ref[:rank_rows, :] = gram[:rank_rows, :]
+        low = gram[rank_rows:, rank_rows:]
+        gram_ref[rank_rows:, :] = jnp.concatenate([low[: rank_rows // 2], low[rank_rows // 2 :]], axis=1)
 
 
 def spectra_and_gram(blocks, row_weight, table_high, table_low):
     sources, groups, rows, rank_rows, points = blocks.shape
     lons, cols = table_high.shape
     span = groups * rank_rows
+    packed = rank_rows + rank_rows // 2
     modes = jax.ShapeDtypeStruct((rows, span, cols), jnp.bfloat16)
     return pl.pallas_call(
         spectra_kernel,
@@ -169,14 +176,14 @@
         out_specs=[
             pl.BlockSpec((rows, span, COL_TILE), lambda i: (0, 0, i)),
             pl.BlockSpec((rows, span, COL_TILE), lambda i: (0, 0, i)),
-            pl.BlockSpec((span, span), lambda i: (0, 0)),
-        ],
-        out_shape=[modes, modes, jax.ShapeDtypeStruct((span, span), jnp.float32)],
+            pl.BlockSpec((packed, span), lambda i: (0, 0)),
+        ],
+        out_shape=[modes, modes, jax.ShapeDtypeStruct((packed, span), jnp.float32)],
         scratch_shapes=[
             pltpu.VMEM((rows * span, lons), jnp.bfloat16),
             pltpu.VMEM((2 * span, span), jnp.float32),
         ],
-        compiler_params=pltpu.CompilerParams(vmem_limit_bytes=48 * 2**20),
+        compiler_params=pltpu.CompilerParams(vmem_limit_bytes=VMEM_BYTES),
         cost_estimate=pl.CostEstimate(
             flops=4 * rows * span * lons * cols,
             bytes_accessed=2 * blocks.size + 4 * lons * cols + 4 * rows * span * cols,
@@ -191,38 +198,72 @@
     )
 
 
-def eliminate(work, size):
+def eliminate(work, size, out_ref):
     height, width = work.shape
-    row_ids = lax.broadcasted_iota(jnp.int32, (height, width), 0)
-    result = jnp.zeros_like(work)
-    for col in range(size):
-        pivot = work[col : col + 1, :]
-        inverse = lax.rsqrt(work[col : col + 1, col : col + 1])
-        scaled_row = pivot * inverse
-        factor = work[:, col : col + 1] * inverse
-        result = jnp.where(row_ids == col, scaled_row, result)
-        work = work - factor * scaled_row
-    return result
-
-
-def merge_kernel(gram_ref, test_ref, xh_ref, xl_ref, out_ref, mix_ref):
+    for col in range(0, size, PIVOTS):
+        base = col // 8 * 8
+        lead = col - base
+        rows = [work[lead + i : lead + i + 1, :] for i in range(PIVOTS)]
+        cols = [
+            jnp.broadcast_to(work[:, col + i : col + i + 1], (height - base, LANES)) for i in range(PIVOTS)
+        ]
+        update = None
+        for i in range(PIVOTS):
+            inverse = lax.rsqrt(cols[i][lead + i : lead + i + 1, :])
+            wide = jnp.concatenate([inverse] * (width // LANES), axis=1)
+            solved = rows[i] * wide
+            out_ref[col + i : col + i + 1, :] = solved
+            factor = cols[i] * inverse
+            for k in range(i + 1, PIVOTS):
+                share = factor[lead + k : lead + k + 1, :]
+                cols[k] = cols[k] - factor * share
+                rows[k] = rows[k] - solved * jnp.concatenate([share] * (width // LANES), axis=1)
+            term = jnp.concatenate([factor] * (width // LANES), axis=1) * solved
+            update = term if update is None else update + term
+        following = (col + PIVOTS) // 8 * 8 - base
+        work = work[following:] - update[following:]
+
+
+def add_up(parts):
+    while len(parts) > 1:
+        parts = [parts[i] + parts[i + 1] for i in range(0, len(parts), 2)]
+    return parts[0]
+
+
+def unpacked(packed):
+    span = packed.shape[1]
+    rank = span // 2
+    low = jnp.concatenate([packed[rank:, :rank], packed[rank:, rank:]], axis=0)
+    square = jnp.concatenate(
+        [packed[:rank], jnp.concatenate([jnp.zeros_like(low), low], axis=1)], axis=0
+    )
+    row_ids = lax.broadcasted_iota(jnp.int32, square.shape, 0)
+    col_ids = lax.broadcasted_iota(jnp.int32, square.shape, 1)
+    return jnp.where((row_ids >= rank) & (col_ids < rank), square.T, square)
+
+
+def merge_kernel(*refs):
+    *part_refs, test_ref, xh_ref, xl_ref, out_ref, mix_ref, first_ref, second_ref = refs
     rank = test_ref.shape[1]
     row = pl.program_id(0)
 
     @pl.when(row == 0)
     def _():
-        gram = gram_ref[...]
+        gram = unpacked(add_up([part[...] for part in part_refs]))
         test = test_ref[...]
         sketch = dot_full(gram, test)
         sketch_t = dot_full(test, gram, (((0,), (0,)), ((), ())))
         sketch_gram = dot_full(sketch_t, gram)
         power = dot_full(sketch_gram, sketch)
         power = 0.5 * (power + power.T)
-        solved = eliminate(jnp.concatenate([power, jnp.zeros_like(power), sketch_gram, sketch_t], axis=1), rank)
-        projected = solved[:, 2 * rank : 4 * rank]
-        unmixed = solved[:, 4 * rank : 6 * rank]
+        pad = jnp.zeros_like(power)
+        eliminate(jnp.concatenate([power, pad, sketch_gram, sketch_t], axis=1), rank, first_ref)
+        projected = first_ref[:, 2 * rank : 4 * rank]
+        unmixed = first_ref[:, 4 * rank : 6 * rank]
         inner = dot_full(projected, projected, NT_DIMS)
-        upper = eliminate(0.5 * (inner + inner.T), rank)
+        inner = 0.5 * (inner + inner.T)
+        eliminate(jnp.concatenate([inner, pad], axis=1), rank, second_ref)
+        upper = second_ref[:, :rank]
         col_ids = lax.broadcasted_iota(jnp.int32, upper.shape, 1)
         row_ids = lax.broadcasted_iota(jnp.int32, upper.shape, 0)
         mixing = dot_full(jnp.where(col_ids >= row_ids, upper, 0.0), unmixed)
@@ -238,30 +279,45 @@
     out_ref[...] = both[:rank] + both[rank:]
 
 
-def merge_and_mix(gram, test_matrix, modes_high, modes_low):
+def merge_and_mix(gram_parts, test_matrix, modes_high, modes_low):
     rows, span, cols = modes_high.shape
     rank = test_matrix.shape[1]
     return pl.pallas_call(
         merge_kernel,
         grid=(rows,),
         in_specs=[
-            pl.BlockSpec(gram.shape, lambda i: (0, 0)),
+            *[pl.BlockSpec(part.shape, lambda i: (0, 0)) for part in gram_parts],
             pl.BlockSpec(test_matrix.shape, lambda i: (0, 0)),
             pl.BlockSpec((1, span, cols), lambda i: (i, 0, 0)),
             pl.BlockSpec((1, span, cols), lambda i: (i, 0, 0)),
         ],
         out_specs=pl.BlockSpec((rank, cols), lambda i: (0, i)),
         out_shape=jax.ShapeDtypeStruct((rank, rows * cols), jnp.float32),
-        scratch_shapes=[pltpu.VMEM((2 * rank, 2 * span), jnp.bfloat16)],
-        compiler_params=pltpu.CompilerParams(vmem_limit_bytes=32 * 2**20),
-    )(gram, test_matrix, modes_high, modes_low)
-
-
-def summed(array, axes):
-    for axis in axes:
-        for distance in range(lax.axis_size(axis).bit_length() - 1):
-            array = array + swapped(array, axis, distance)
-    return array
+        scratch_shapes=[
+            pltpu.VMEM((2 * rank, 2 * span), jnp.bfloat16),
+            pltpu.VMEM((rank, 6 * rank), jnp.float32),
+            pltpu.VMEM((rank, 2 * rank), jnp.float32),
+        ],
+        compiler_params=pltpu.CompilerParams(vmem_limit_bytes=VMEM_BYTES),
+    )(*gram_parts, test_matrix, modes_high, modes_low)
+
+
+def exchanged(array, axes, bits):
+    count = lax.axis_size(axes)
+    masks = [0]
+    for bit in bits:
+        masks += [mask | bit for mask in masks]
+    return [array] + [
+        lax.ppermute(array, axes, [(i, i ^ mask) for i in range(count)]) for mask in masks[1:]
+    ]
+
+
+def sum_parts(array, axes):
+    bits = [1 << k for k in range(lax.axis_size(axes).bit_length() - 1)]
+    parts = exchanged(array, axes, bits[:1])
+    for group in (bits[1:2] + bits[-1:], *[bits[k : k + 2] for k in range(2, len(bits) - 1, 2)]):
+        parts = exchanged(add_up(parts), axes, group)
+    return parts
 
 
 def local_pair(snapshots, test_matrix):
@@ -275,13 +331,14 @@
         snapshots.transpose(2, 1, 0), ("lon", "tm"), split_axis=0, concat_axis=0, tiled=True
     ).reshape(lon_count, group_count, dev_rows, rank_rows, points)
     modes_high, modes_low, gram = spectra_and_gram(blocks, row_weight, table_high, table_low)
-    gram = summed(gram, ("lon", "tm"))
-    return merge_and_mix(gram, test_matrix, modes_high, modes_low)
+    gram_parts = sum_parts(gram, ("tm", "lon"))
+    return merge_and_mix(gram_parts, test_matrix, modes_high, modes_low)
 
 
 def solution(mesh):
     lon_count, group_count = mesh.shape["lon"], mesh.shape["tm"]
-    whole_rows = NTH % (lon_count * group_count) == 0
+    device_count = lon_count * group_count
+    whole_rows = NTH % device_count == 0 and device_count & (device_count - 1) == 0
     return jax.shard_map(
         local_pair if group_count == 2 and whole_rows else local_tree,
         mesh=mesh,

time: 174 us -> 162 us (0.931)
  Pallas kernels: 41.6 us -> 33.3 us
  waiting for transfers between devices: 65.1 us -> 58.2 us
  starting transfers between devices: 11.4 us -> 15.4 us
  local copies, waits for them, and re-layouts: 10.7 us -> 8.69 us
    ppermute x5 -> x7, waiting for transfers between devices: 16.1 us -> 9.78 us  [exchanged(): lax.ppermute(array, axes, [(i, i ^ mask) for i in range(count)])]
    pallas_call x1, Pallas kernels: 25.7 us -> 20.6 us  [spectra_and_gram(): pl.pallas_call(spectra_kernel, grid=(cols // COL_TILE,), in_specs=[pl.Blo...]
    ppermute x5 -> x7, starting transfers between devices: 3.96 us -> 7.95 us  [exchanged(): lax.ppermute(array, axes, [(i, i ^ mask) for i in range(count)])]
    pallas_call x1, Pallas kernels: 15.9 us -> 12.7 us  [merge_and_mix(): pl.pallas_call(merge_kernel, grid=(rows,), in_specs=[*[pl.BlockSpec(part....]
    unnamed x8 -> x12, local copies, waits for them, and re-layouts: 10.7 us -> 8.69 us
  transfers between devices with their start and end apart: 6 -> 8, of which waited for: 6 -> 7; matrix products, arithmetic and copies ran while one was open for 26% -> 28% of each run, Pallas kernels for 0% -> 0%
where the time goes in v2:
time: 162 us
  waiting for transfers between devices  58.2 us (36%)
  other arithmetic  46.1 us (28%)
  Pallas kernels  33.3 us (21%)
  starting transfers between devices  15.4 us (10%)
  local copies, waits for them, and re-layouts  8.69 us (5%)
    all_to_all x1, waiting for transfers between devices, local_pair(): lax.all_to_all(snapshots.transpose(2, 1, 0), ('lon', 'tm'), split_axis=0,...  48.4 us
    convert_element_type x1, other arithmetic, split_table(): return (high.astype(jnp.bfloat16), (table - high).astype(jnp.bfloat16))  44.6 us
    pallas_call x1, Pallas kernels, spectra_and_gram(): pl.pallas_call(spectra_kernel, grid=(cols // COL_TILE,), in_specs=[pl.Blo...  20.6 us
    pallas_call x1, Pallas kernels, merge_and_mix(): pl.pallas_call(merge_kernel, grid=(rows,), in_specs=[*[pl.BlockSpec(part....  12.7 us
    ppermute x7, waiting for transfers between devices, exchanged(): lax.ppermute(array, axes, [(i, i ^ mask) for i in range(count)])  9.78 us
    unnamed x12, local copies, waits for them, and re-layouts  8.69 us
    ppermute x7, starting transfers between devices, exchanged(): lax.ppermute(array, axes, [(i, i ^ mask) for i in range(count)])  7.95 us
    all_to_all x1, starting transfers between devices, local_pair(): lax.all_to_all(snapshots.transpose(2, 1, 0), ('lon', 'tm'), split_axis=0,...  7.43 us
  transfers between devices with their start and end apart: 8, of which 7 were waited for; matrix products, arithmetic and copies ran while one was open for 28% of the time, Pallas kernels for 0%

profile of v2, /device:TPU:0, one launch (start us, length us, event | category | flops | bytes accessed | tf_op | source)
XLA Modules:
  0.0 161.7 jit_solution(1080148361411151187)
XLA Ops:
  0.0 7.4 %copy.8 = bf16[128,64,256]{0,1,2:T(8,128)(2,1)} copy(bf16[128,64,256]{2,1,0:T(8,128)(2,1)} %param.2) | data formatting | bytes 8388608 | tf_op args[0]
  7.4 7.4 %all-to-all-start = ((bf16[256,64,128]{2,1,0:T(8,128)(2,1)}), bf16[256,64,128]{2,1,0:T(8,128)(2,1)}, u32[]{:S(2)}, u32[]{:S(2)}) async-start(bf16[256,64,128]{2,1,0:T(8,128)(2,1)} %bitcast.2), calls=%async_computation | async-start | bytes 8388608 | tf_op jit(solution)/shard_map/all_to_all | solution.py:330
  14.8 0.6 sine_sqrt_fusion.weight_ref
  15.5 44.6 %fusion = (bf16[2048,1280]{1,0:T(8,128)(2,1)}, bf16[2048,1280]{1,0:T(8,128)(2,1)}) fusion(f32[1280]{0:T(1024)S(1)} %rsqrt_multiply_fusion, s32[1280]{0:T(1024)S(1)} %add_select_fusion.1, pred[1280]{0:T(1024)(128)(4,1)S(1)} %iota_compare_fusion), kind=kLoop, calls=%fused_computation.5 | loop fusion | flops 52428800 | bytes 10497280 | tf_op jit(solution)/shard_map/convert_element_type | solution.py:117
  60.1 48.4 %all-to-all-done = bf16[256,64,128]{2,1,0:T(8,128)(2,1)} async-done(((bf16[256,64,128]{2,1,0:T(8,128)(2,1)}), bf16[256,64,128]{2,1,0:T(8,128)(2,1)}, u32[]{:S(2)}, u32[]{:S(2)}) %all-to-all-start) | async-done | bytes 4194336 | tf_op jit(solution)/shard_map/all_to_all | solution.py:330
  108.5 0.0 copy-start.4
  108.5 20.6 %shard_map.28 = (bf16[8,128,1280]{2,1,0:T(8,128)(2,1)}, bf16[8,128,1280]{2,1,0:T(8,128)(2,1)}, f32[96,128]{1,0:T(8,128)}) custom-call(f32[1,8]{1,0:T(1,128)} %sine_sqrt_fusion.weight_ref, bf16[16,2,8,64,128]{4,3,2,1,0:T(8,128)(2,1)} %bitcast.1.x_ref, bf16[2048,1280]{1,0:T(8,128)(2,1)} %get-tuple-element.12.high_ref, bf16[2048,1280]{1,0:T(8,128)(2,1)} %get-tuple-element.11.low_ref), custom_call_target="tpu_custom_call" | custom-call | flops 10737418240 | bytes 19922944 | tf_op jit(solution)/shard_map/pallas_call | solution.py:167
  129.1 0.0 collective-permute-start
  129.2 1.4 collective-permute-done
  130.6 0.8 add.87
  131.4 1.4 collective-permute-start.1
  132.8 1.5 collective-permute-start.2
  134.3 0.6 collective-permute-start.3
  134.9 0.6 collective-permute-done.1
  135.5 1.8 %collective-permute-done.2 = f32[96,128]{1,0:T(8,128)S(1)} collective-permute-done((f32[96,128]{1,0:T(8,128)S(1)}, f32[96,128]{1,0:T(8,128)S(1)}, u32[]{:S(2)}, u32[]{:S(2)}) %collective-permute-start.2) | collective-permute-done | bytes 49184 | tf_op jit(solution)/shard_map/ppermute | solution.py:311
  137.3 2.0 %collective-permute-done.3 = f32[96,128]{1,0:T(8,128)S(1)} collective-permute-done((f32[96,128]{1,0:T(8,128)S(1)}, f32[96,128]{1,0:T(8,128)S(1)}, u32[]{:S(2)}, u32[]{:S(2)}) %collective-permute-start.3) | collective-permute-done | bytes 49184 | tf_op jit(solution)/shard_map/ppermute | solution.py:311
  139.3 0.0 copy-start
  139.4 0.1 collective-permute-start.4
  139.4 3.1 %collective-permute-start.5 = (f32[96,128]{1,0:T(8,128)S(1)}, f32[96,128]{1,0:T(8,128)S(1)}, u32[]{:S(2)}, u32[]{:S(2)}) collective-permute-start(f32[96,128]{1,0:T(8,128)S(1)} %add_add_fusion.refs_0_), channel_id=1, source_target_pairs={{0,8},{1,9},{2,10},{3,11},{4,12},{5,13},{6,14},{7,15},{8,0},{9,1},... | collective-permute-start | bytes 147464 | tf_op jit(solution)/shard_map/ppermute | solution.py:311
  142.6 1.2 collective-permute-start.6
  143.8 0.0 copy-done.4
  143.8 0.7 copy.9.refs_4_
  144.5 0.0 collective-permute-done.4.refs_1_
  144.5 0.0 copy-start.1
  144.5 0.1 collective-permute-done.5.refs_2_
  144.6 0.0 copy-start.2
  144.6 3.8 %collective-permute-done.6.refs_3_ = f32[96,128]{1,0:T(8,128)S(1)} collective-permute-done((f32[96,128]{1,0:T(8,128)S(1)}, f32[96,128]{1,0:T(8,128)S(1)}, u32[]{:S(2)}, u32[]{:S(2)}) %collective-permute-start.6) | collective-permute-done | bytes 49184 | tf_op jit(solution)/shard_map/ppermute | solution.py:311
  148.4 0.0 copy-start.3
  148.4 0.0 copy-done
  148.5 0.0 copy-done.1
  148.5 0.0 copy-done.2
  148.5 0.6 copy-done.3
  149.1 12.7 %shard_map.29 = f32[64,10240]{1,0:T(8,128)} custom-call(f32[96,128]{1,0:T(8,128)} %copy-done, f32[96,128]{1,0:T(8,128)} %copy-done.1, f32[96,128]{1,0:T(8,128)} %copy-done.2, f32[96,128]{1,0:T(8,128)} %copy-done.3, f32[128,64]{1,0:T(8,128)} %copy.9.refs_4_, bf16[8,128,1280]{2,1,0:T(8,128)(2,1)} %get-tuple-element.9.refs_5_, ...), custom_call_target="tpu_custom_call" | custom-call | tf_op jit(solution)/shard_map/pallas_call | solution.py:285
  (4 shorter events, 0.0 us)
Async XLA Ops:
  7.4 101.2 %all-to-all-start = ((bf16[256,64,128]{2,1,0:T(8,128)(2,1)}), bf16[256,64,128]{2,1,0:T(8,128)(2,1)}, u32[]{:S(2)}, u32[]{:S(2)}) async-start(bf16[256,64,128]{2,1,0:T(8,128)(2,1)} %bitcast.2), calls=%async_computation | async-start | bytes 8388608 | tf_op jit(solution)/shard_map/all_to_all | solution.py:330
  108.5 35.3 %copy-start.4 = (f32[128,64]{0,1:T(8,128)S(1)}, f32[128,64]{0,1:T(8,128)}, u32[]{:S(2)}) copy-start(f32[128,64]{0,1:T(8,128)} %param.3) | copy-start | bytes 98308
  129.1 1.4 collective-permute-start
  131.4 4.1 %collective-permute-start.1 = (f32[96,128]{1,0:T(8,128)S(1)}, f32[96,128]{1,0:T(8,128)S(1)}, u32[]{:S(2)}, u32[]{:S(2)}) collective-permute-start(f32[96,128]{1,0:T(8,128)S(1)} %add.87), channel_id=1, source_target_pairs={{0,2},{1,3},{2,0},{3,1},{4,6},{5,7},{6,4},{7,5},{8,10},{9,11},{10,... | collective-permute-start | bytes 147464 | tf_op jit(solution)/shard_map/ppermute | solution.py:311
  132.8 4.5 %collective-permute-start.2 = (f32[96,128]{1,0:T(8,128)S(1)}, f32[96,128]{1,0:T(8,128)S(1)}, u32[]{:S(2)}, u32[]{:S(2)}) collective-permute-start(f32[96,128]{1,0:T(8,128)S(1)} %add.87), channel_id=1, source_target_pairs={{0,16},{1,17},{2,18},{3,19},{4,20},{5,21},{6,22},{7,23},{8,24},{9,... | collective-permute-start | bytes 147464 | tf_op jit(solution)/shard_map/ppermute | solution.py:311
  134.3 5.0 %collective-permute-start.3 = (f32[96,128]{1,0:T(8,128)S(1)}, f32[96,128]{1,0:T(8,128)S(1)}, u32[]{:S(2)}, u32[]{:S(2)}) collective-permute-start(f32[96,128]{1,0:T(8,128)S(1)} %add.87), channel_id=1, source_target_pairs={{0,18},{1,19},{2,16},{3,17},{4,22},{5,23},{6,20},{7,21},{8,26},{9,... | collective-permute-start | bytes 147464 | tf_op jit(solution)/shard_map/ppermute | solution.py:311
  139.3 9.1 %copy-start = (f32[96,128]{1,0:T(8,128)}, f32[96,128]{1,0:T(8,128)S(1)}, u32[]{:S(2)}) copy-start(f32[96,128]{1,0:T(8,128)S(1)} %add_add_fusion.refs_0_) | copy-start | bytes 147460
  139.4 5.2 %collective-permute-start.4 = (f32[96,128]{1,0:T(8,128)S(1)}, f32[96,128]{1,0:T(8,128)S(1)}, u32[]{:S(2)}, u32[]{:S(2)}) collective-permute-start(f32[96,128]{1,0:T(8,128)S(1)} %add_add_fusion.refs_0_), channel_id=1, source_target_pairs={{0,4},{1,5},{2,6},{3,7},{4,0},{5,1},{6,2},{7,3},{8,12},{9,13},{10,... | collective-permute-start | bytes 147464 | tf_op jit(solution)/shard_map/ppermute | solution.py:311
  139.4 5.2 %collective-permute-start.5 = (f32[96,128]{1,0:T(8,128)S(1)}, f32[96,128]{1,0:T(8,128)S(1)}, u32[]{:S(2)}, u32[]{:S(2)}) collective-permute-start(f32[96,128]{1,0:T(8,128)S(1)} %add_add_fusion.refs_0_), channel_id=1, source_target_pairs={{0,8},{1,9},{2,10},{3,11},{4,12},{5,13},{6,14},{7,15},{8,0},{9,1},... | collective-permute-start | bytes 147464 | tf_op jit(solution)/shard_map/ppermute | solution.py:311
  142.6 5.9 %collective-permute-start.6 = (f32[96,128]{1,0:T(8,128)S(1)}, f32[96,128]{1,0:T(8,128)S(1)}, u32[]{:S(2)}, u32[]{:S(2)}) collective-permute-start(f32[96,128]{1,0:T(8,128)S(1)} %add_add_fusion.refs_0_), channel_id=1, source_target_pairs={{0,12},{1,13},{2,14},{3,15},{4,8},{5,9},{6,10},{7,11},{8,4},{9,5},... | collective-permute-start | bytes 147464 | tf_op jit(solution)/shard_map/ppermute | solution.py:311
  144.5 3.9 %copy-start.1 = (f32[96,128]{1,0:T(8,128)}, f32[96,128]{1,0:T(8,128)S(1)}, u32[]{:S(2)}) copy-start(f32[96,128]{1,0:T(8,128)S(1)} %collective-permute-done.4.refs_1_) | copy-start | bytes 147460
  144.6 3.8 %copy-start.2 = (f32[96,128]{1,0:T(8,128)}, f32[96,128]{1,0:T(8,128)S(1)}, u32[]{:S(2)}) copy-start(f32[96,128]{1,0:T(8,128)S(1)} %collective-permute-done.5.refs_2_) | copy-start | bytes 147460
  148.4 0.6 copy-start.3

commit v3 on v2

--- a/solution.py
+++ b/solution.py
@@ -14,7 +14,9 @@
 COL_TILE = 256
 LANES = 128
 PIVOTS = 4
-VMEM_BYTES = 59 * 2**20
+SNAPSHOT_TILE = 16
+EARLY_ROWS = 6
+VMEM_BYTES = 51 * 2**20
 
 
 highest = lax.Precision.HIGHEST
@@ -114,10 +116,37 @@
 def split_table(points, wave_count):
     table = spectral_table(points, wave_count)
     high = lax.reduce_precision(table, 8, 7)
-    return high.astype(jnp.bfloat16), (table - high).astype(jnp.bfloat16)
-
-
-def spectra_kernel(weight_ref, x_ref, high_ref, low_ref, xh_ref, xl_ref, gram_ref, lhs, acc):
+    return jnp.stack([high.astype(jnp.bfloat16), (table - high).astype(jnp.bfloat16)])
+
+
+def relayout_kernel(x_ref, first_ref, last_ref):
+    points, some, total = x_ref.shape
+    devices, split = first_ref.shape[:2]
+    by_snapshot = jnp.transpose(x_ref[...], (1, 0, 2))
+    turned = jnp.stack([by_snapshot[i].T for i in range(some)], axis=0)
+    rows = jnp.transpose(turned, (1, 0, 2)).reshape(devices, total // devices, some, points)
+    first_ref[...] = rows[:, :split]
+    last_ref[...] = rows[:, split:]
+
+
+def relayout(snapshots, devices, split):
+    points, rank_rows, total = snapshots.shape
+    some = SNAPSHOT_TILE
+    cuts = (split, total // devices - split)
+    return pl.pallas_call(
+        relayout_kernel,
+        grid=(rank_rows // some,),
+        in_specs=[pl.BlockSpec((points, some, total), lambda i: (0, i, 0))],
+        out_specs=[pl.BlockSpec((devices, cut, some, points), lambda i: (0, 0, i, 0)) for cut in cuts],
+        out_shape=[
+            jax.ShapeDtypeStruct((devices, cut, rank_rows, points), snapshots.dtype) for cut in cuts
+        ],
+        compiler_params=pltpu.CompilerParams(vmem_limit_bytes=VMEM_BYTES),
+    )(snapshots)
+
+
+def spectra_kernel(*refs, first_row):
+    weight_ref, x_ref, table_ref, *before, modes_ref, gram_ref, lhs, acc = refs
     sources, groups, rows, rank_rows, points = x_ref.shape
     step = pl.program_id(0)
 
@@ -134,15 +163,15 @@
 
     span = groups * rank_rows
     values = lhs[...]
-    spectra = jnp.dot(values, high_ref[...], preferred_element_type=jnp.float32)
-    spectra += jnp.dot(values, low_ref[...], preferred_element_type=jnp.float32)
+    spectra = jnp.dot(values, table_ref[0], preferred_element_type=jnp.float32)
+    spectra += jnp.dot(values, table_ref[1], preferred_element_type=jnp.float32)
     tops, rests = [], []
     for row in range(rows):
-        scaled = spectra[row * span : (row + 1) * span] * weight_ref[0, row]
+        scaled = spectra[row * span : (row + 1) * span] * weight_ref[0, first_row + row]
         top = scaled.astype(jnp.bfloat16)
         rest = (scaled - top.astype(jnp.float32)).astype(jnp.bfloat16)
-        xh_ref[row] = top
-        xl_ref[row] = rest
+        modes_ref[row, :span] = top
+        modes_ref[row, span:] = rest
         tops.append(top)
         rests.append(rest)
     top = jnp.concatenate(tops, axis=1)
@@ -153,32 +182,36 @@
     def _():
         cross = acc[span:, :]
         gram = acc[:span, :] + (cross + cross.T)
-        gram_ref[:rank_rows, :] = gram[:rank_rows, :]
         low = gram[rank_rows:, rank_rows:]
-        gram_ref[rank_rows:, :] = jnp.concatenate([low[: rank_rows // 2], low[rank_rows // 2 :]], axis=1)
-
-
-def spectra_and_gram(blocks, row_weight, table_high, table_low):
+        low = jnp.concatenate([low[: rank_rows // 2], low[rank_rows // 2 :]], axis=1)
+        packed = jnp.concatenate([gram[:rank_rows], low], axis=0)
+        for ref in before:
+            packed += ref[...]
+        gram_ref[...] = packed
+
+
+def spectra_and_gram(blocks, row_weight, table, first_row, *before):
     sources, groups, rows, rank_rows, points = blocks.shape
-    lons, cols = table_high.shape
+    _, lons, cols = table.shape
     span = groups * rank_rows
-    packed = rank_rows + rank_rows // 2
-    modes = jax.ShapeDtypeStruct((rows, span, cols), jnp.bfloat16)
+    packed = (rank_rows + rank_rows // 2, span)
     return pl.pallas_call(
-        spectra_kernel,
+        functools.partial(spectra_kernel, first_row=first_row),
         grid=(cols // COL_TILE,),
         in_specs=[
             pl.BlockSpec(memory_space=pltpu.SMEM),
             pl.BlockSpec(blocks.shape, lambda i: (0, 0, 0, 0, 0)),
-            pl.BlockSpec((lons, COL_TILE), lambda i: (0, i)),
-            pl.BlockSpec((lons, COL_TILE), lambda i: (0, i)),
+            pl.BlockSpec((2, lons, COL_TILE), lambda i: (0, 0, i)),
+            *[pl.BlockSpec(packed, lambda i: (0, 0)) for _ in before],
         ],
         out_specs=[
-            pl.BlockSpec((rows, span, COL_TILE), lambda i: (0, 0, i)),
-            pl.BlockSpec((rows, span, COL_TILE), lambda i: (0, 0, i)),
-            pl.BlockSpec((packed, span), lambda i: (0, 0)),
-        ],
-        out_shape=[modes, modes, jax.ShapeDtypeStruct((packed, span), jnp.float32)],
+            pl.BlockSpec((rows, 2 * span, COL_TILE), lambda i: (0, 0, i)),
+            pl.BlockSpec(packed, lambda i: (0, 0)),
+        ],
+        out_shape=[
+            jax.ShapeDtypeStruct((rows, 2 * span, cols), jnp.bfloat16),
+            jax.ShapeDtypeStruct(packed, jnp.float32),
+        ],
         scratch_shapes=[
             pltpu.VMEM((rows * span, lons), jnp.bfloat16),
             pltpu.VMEM((2 * span, span), jnp.float32),
@@ -189,7 +222,7 @@
             bytes_accessed=2 * blocks.size + 4 * lons * cols + 4 * rows * span * cols,
             transcendentals=0,
         ),
-    )(row_weight.reshape(1, rows), blocks, table_high, table_low)
+    )(row_weight.reshape(1, -1), blocks, table, *before)
 
 
 def dot_full(first, second, dims=(((1,), (0,)), ((), ()))):
@@ -242,17 +275,17 @@
     return jnp.where((row_ids >= rank) & (col_ids < rank), square.T, square)
 
 
-def merge_kernel(*refs):
-    *part_refs, test_ref, xh_ref, xl_ref, out_ref, mix_ref, first_ref, second_ref = refs
-    rank = test_ref.shape[1]
+def merge_kernel(*refs, split):
+    *part_refs, test_ref, early_ref, late_ref, out_ref, mix_ref, first_ref, second_ref = refs
+    rank = test_ref.shape[0]
     row = pl.program_id(0)
 
     @pl.when(row == 0)
     def _():
         gram = unpacked(add_up([part[...] for part in part_refs]))
-        test = test_ref[...]
-        sketch = dot_full(gram, test)
-        sketch_t = dot_full(test, gram, (((0,), (0,)), ((), ())))
+        test_t = test_ref[...]
+        sketch = dot_full(gram, test_t, NT_DIMS)
+        sketch_t = dot_full(test_t, gram)
         sketch_gram = dot_full(sketch_t, gram)
         power = dot_full(sketch_gram, sketch)
         power = 0.5 * (power + power.T)
@@ -274,32 +307,41 @@
         mix_ref[rank:, : 2 * rank] = rest
         mix_ref[rank:, 2 * rank :] = jnp.zeros_like(rest)
 
-    stacked = jnp.concatenate([xh_ref[0], xl_ref[0]], axis=0)
-    both = jnp.dot(mix_ref[...], stacked, preferred_element_type=jnp.float32)
-    out_ref[...] = both[:rank] + both[rank:]
-
-
-def merge_and_mix(gram_parts, test_matrix, modes_high, modes_low):
-    rows, span, cols = modes_high.shape
+    def mix(modes):
+        both = jnp.dot(mix_ref[...], modes, preferred_element_type=jnp.float32)
+        out_ref[...] = both[:rank] + both[rank:]
+
+    @pl.when(row < split)
+    def _():
+        mix(early_ref[0])
+
+    @pl.when(row >= split)
+    def _():
+        mix(late_ref[0])
+
+
+def merge_and_mix(gram_parts, test_matrix, early, late):
+    split, height, cols = early.shape
+    rows = split + late.shape[0]
     rank = test_matrix.shape[1]
     return pl.pallas_call(
-        merge_kernel,
+        functools.partial(merge_kernel, split=split),
         grid=(rows,),
         in_specs=[
             *[pl.BlockSpec(part.shape, lambda i: (0, 0)) for part in gram_parts],
-            pl.BlockSpec(test_matrix.shape, lambda i: (0, 0)),
-            pl.BlockSpec((1, span, cols), lambda i: (i, 0, 0)),
-            pl.BlockSpec((1, span, cols), lambda i: (i, 0, 0)),
+            pl.BlockSpec((rank, 2 * rank), lambda i: (0, 0)),
+            pl.BlockSpec((1, height, cols), lambda i: (jnp.minimum(i, split - 1), 0, 0)),
+            pl.BlockSpec((1, height, cols), lambda i: (jnp.maximum(i - split, 0), 0, 0)),
         ],
         out_specs=pl.BlockSpec((rank, cols), lambda i: (0, i)),
         out_shape=jax.ShapeDtypeStruct((rank, rows * cols), jnp.float32),
         scratch_shapes=[
-            pltpu.VMEM((2 * rank, 2 * span), jnp.bfloat16),
+            pltpu.VMEM((2 * rank, height), jnp.bfloat16),
             pltpu.VMEM((rank, 6 * rank), jnp.float32),
             pltpu.VMEM((rank, 2 * rank), jnp.float32),
         ],
         compiler_params=pltpu.CompilerParams(vmem_limit_bytes=VMEM_BYTES),
-    )(*gram_parts, test_matrix, modes_high, modes_low)
+    )(*gram_parts, test_matrix.T, early, late)
 
 
 def exchanged(array, axes, bits):
@@ -326,13 +368,17 @@
     dev_rows = total_rows // (lon_count * group_count)
     first_row = (lax.axis_index("lon") * group_count + lax.axis_index("tm")) * dev_rows
     row_weight = area_weight(first_row, dev_rows, NTH)
-    table_high, table_low = split_table(NPH, MMAX)
-    blocks = lax.all_to_all(
-        snapshots.transpose(2, 1, 0), ("lon", "tm"), split_axis=0, concat_axis=0, tiled=True
-    ).reshape(lon_count, group_count, dev_rows, rank_rows, points)
-    modes_high, modes_low, gram = spectra_and_gram(blocks, row_weight, table_high, table_low)
-    gram_parts = sum_parts(gram, ("tm", "lon"))
-    return merge_and_mix(gram_parts, test_matrix, modes_high, modes_low)
+    table = split_table(NPH, MMAX)
+    split = EARLY_ROWS * dev_rows // 8
+    early, late = relayout(snapshots, lon_count * group_count, split)
+    late, table = lax.optimization_barrier((late, table))
+    modes, gram = [], []
+    for first, part in ((0, early), (split, late)):
+        blocks = lax.all_to_all(part, ("lon", "tm"), split_axis=0, concat_axis=0, tiled=True)
+        blocks = blocks.reshape(lon_count, group_count, -1, rank_rows, points)
+        spectra, *gram = spectra_and_gram(blocks, row_weight, table, first, *gram)
+        modes.append(spectra)
+    return merge_and_mix(sum_parts(gram[0], ("tm", "lon")), test_matrix, *modes)
 
 
 def solution(mesh):

time: 162 us -> 155 us (0.957)
  waiting for transfers between devices: 58.2 us -> 36.4 us
  Pallas kernels: 33.3 us -> 43 us
  other arithmetic: 46.1 us -> 53.7 us
  local copies, waits for them, and re-layouts: 8.69 us -> 1.62 us
  starting transfers between devices: 15.4 us -> 19.4 us
    all_to_all x1 -> x2, waiting for transfers between devices: 48.4 us -> 27.3 us  [local_pair(): lax.all_to_all(part, ('lon', 'tm'), split_axis=0, concat_axis=0, tiled=True)]
    pallas_call x2 -> x4, Pallas kernels: 33.3 us -> 43 us  [the longest x2 24.9 us: spectra_and_gram(): pl.pallas_call(functools.partial(spectra_kernel, first_row=first_row), gr...]
    another operation x0 -> x1, other arithmetic: none -> 8.99 us  [split_table(): jnp.stack([high.astype(jnp.bfloat16), (table - high).astype(jnp.bfloat16)])]
    unnamed x12 -> x4, local copies, waits for them, and re-layouts: 8.69 us -> 1.62 us
    all_to_all x1 -> x2, starting transfers between devices: 7.43 us -> 11.3 us  [local_pair(): lax.all_to_all(part, ('lon', 'tm'), split_axis=0, concat_axis=0, tiled=True)]
  transfers between devices with their start and end apart: 8 -> 9, of which waited for: 7 -> 8; matrix products, arithmetic and copies ran while one was open for 28% -> 35% of each run, Pallas kernels for 0% -> 11%
where the time goes in v3:
time: 155 us; the launch traced here: 154 us
  other arithmetic  53.7 us (35%)
  Pallas kernels  43 us (28%)
  waiting for transfers between devices  36.4 us (23%)
  starting transfers between devices  19.4 us (13%)
  local copies, waits for them, and re-layouts  1.62 us (1%)
    convert_element_type x1, other arithmetic, split_table(): high.astype(jnp.bfloat16)  44.6 us
    all_to_all x2, waiting for transfers between devices, local_pair(): lax.all_to_all(part, ('lon', 'tm'), split_axis=0, concat_axis=0, tiled=True)  27.3 us
    pallas_call x2, Pallas kernels, spectra_and_gram(): pl.pallas_call(functools.partial(spectra_kernel, first_row=first_row), gr...  24.9 us
    pallas_call x1, Pallas kernels, merge_and_mix(): pl.pallas_call(functools.partial(merge_kernel, split=split), grid=(rows,)...  12.1 us
    all_to_all x2, starting transfers between devices, local_pair(): lax.all_to_all(part, ('lon', 'tm'), split_axis=0, concat_axis=0, tiled=True)  11.3 us
    ppermute x7, waiting for transfers between devices, exchanged(): lax.ppermute(array, axes, [(i, i ^ mask) for i in range(count)])  9.16 us
    another operation x1, other arithmetic, split_table(): jnp.stack([high.astype(jnp.bfloat16), (table - high).astype(jnp.bfloat16)])  8.99 us
    ppermute x7, starting transfers between devices, exchanged(): lax.ppermute(array, axes, [(i, i ^ mask) for i in range(count)])  8.07 us
  transfers between devices with their start and end apart: 9, of which 8 were waited for; matrix products, arithmetic and copies ran while one was open for 35% of the time, Pallas kernels for 11%

profile of v3, /device:TPU:0, one launch (start us, length us, event | category | flops | bytes accessed | tf_op | source)
XLA Modules:
  0.0 154.2 jit_solution(11769120528731791786)
XLA Ops:
  0.0 6.0 %shard_map.28 = (bf16[32,6,64,128]{3,2,1,0:T(8,128)(2,1)}, bf16[32,2,64,128]{3,2,1,0:T(8,128)(2,1)}) custom-call(bf16[128,64,256]{2,1,0:T(8,128)(2,1)} %x_ref.1), custom_call_target="tpu_custom_call" | custom-call | tf_op jit(solution)/shard_map/pallas_call | solution.py:136
  6.0 7.3 %all-to-all-start.1 = ((bf16[32,6,64,128]{3,2,1,0:T(8,128)(2,1)}), bf16[32,6,64,128]{3,2,1,0:T(8,128)(2,1)S(1)}, u32[]{:S(2)}, u32[]{:S(2)}) async-start(bf16[32,6,64,128]{3,2,1,0:T(8,128)(2,1)} %get-tuple-element.16), calls=%async_computation.1 | async-start | bytes 6291456 | tf_op jit(solution)/shard_map/all_to_all | solution.py:377
  13.4 44.6 %reduce-precision_convert_fusion = (bf16[1,2048,1280]{2,1,0:T(8,128)(2,1)}, bf16[1,2048,1280]{2,1,0:T(8,128)(2,1)}) fusion(f32[1280]{0:T(1024)S(1)} %rsqrt_multiply_fusion, s32[1280]{0:T(1024)S(1)} %add_select_fusion.1, pred[1280]{0:T(1024)(128)(4,1)S(1)} %iota_compare_fusion), kind=kLoop, calls=%fused_computation.4 | loop fusion | flops 52428800 | bytes 10497280 | tf_op jit(solution)/shard_map/convert_element_type | solution.py:119
  58.0 9.0 %pad_maximum_fusion.refs_2_ = bf16[2,2048,1280]{2,1,0:T(8,128)(2,1)} fusion(bf16[1,2048,1280]{2,1,0:T(8,128)(2,1)} %get-tuple-element.22, bf16[1,2048,1280]{2,1,0:T(8,128)(2,1)} %get-tuple-element.21), kind=kLoop, calls=%fused_computation.9 | loop fusion | flops 5242880 | bytes 20971520 | tf_op jit(solution)/shard_map/stack | solution.py:119
  67.0 17.6 %all-to-all-done.1 = bf16[32,6,64,128]{3,2,1,0:T(8,128)(2,1)S(1)} async-done(((bf16[32,6,64,128]{3,2,1,0:T(8,128)(2,1)}), bf16[32,6,64,128]{3,2,1,0:T(8,128)(2,1)S(1)}, u32[]{:S(2)}, u32[]{:S(2)}) %all-to-all-start.1) | async-done | bytes 3145760 | tf_op jit(solution)/shard_map/all_to_all | solution.py:377
  84.6 0.0 copy-start.1
  84.6 1.6 %copy-done.1 = bf16[32,6,64,128]{3,2,1,0:T(8,128)(2,1)} copy-done((bf16[32,6,64,128]{3,2,1,0:T(8,128)(2,1)}, bf16[32,6,64,128]{3,2,1,0:T(8,128)(2,1)S(1)}, u32[]{:S(2)}) %copy-start.1) | copy-done | bytes 3145752
  86.2 4.0 %all-to-all-start = ((bf16[32,2,64,128]{3,2,1,0:T(8,128)(2,1)}), bf16[32,2,64,128]{3,2,1,0:T(8,128)(2,1)S(1)}, u32[]{:S(2)}, u32[]{:S(2)}) async-start(bf16[32,2,64,128]{3,2,1,0:T(8,128)(2,1)} %get-tuple-element.14), calls=%async_computation | async-start | bytes 2097152 | tf_op jit(solution)/shard_map/all_to_all | solution.py:377
  90.2 16.5 %shard_map.29 = (bf16[6,256,1280]{2,1,0:T(8,128)(2,1)}, f32[96,128]{1,0:T(8,128)S(1)}) custom-call(f32[1,8]{1,0:T(1,128)S(1)} %sine_sqrt_fusion.refs_0_, bf16[16,2,6,64,128]{4,3,2,1,0:T(8,128)(2,1)} %bitcast.5, bf16[2,2048,1280]{2,1,0:T(8,128)(2,1)} %pad_maximum_fusion.refs_2_), custom_call_target="tpu_custom_call" | custom-call | flops 8053063680 | bytes 17563648 | tf_op jit(solution)/shard_map/pallas_call | solution.py:198
  106.7 0.0 copy-start
  106.7 9.7 %all-to-all-done = bf16[32,2,64,128]{3,2,1,0:T(8,128)(2,1)S(1)} async-done(((bf16[32,2,64,128]{3,2,1,0:T(8,128)(2,1)}), bf16[32,2,64,128]{3,2,1,0:T(8,128)(2,1)S(1)}, u32[]{:S(2)}, u32[]{:S(2)}) %all-to-all-start) | async-done | bytes 1048608 | tf_op jit(solution)/shard_map/all_to_all | solution.py:377
  116.4 8.4 %shard_map.30 = (bf16[2,256,1280]{2,1,0:T(8,128)(2,1)S(1)}, f32[96,128]{1,0:T(8,128)S(1)}) custom-call(f32[1,8]{1,0:T(1,128)S(1)} %sine_sqrt_fusion.refs_0_, bf16[16,2,2,64,128]{4,3,2,1,0:T(8,128)(2,1)S(1)} %bitcast.3, bf16[2,2048,1280]{2,1,0:T(8,128)(2,1)} %pad_maximum_fusion.refs_2_, f32[96,128]{1,0:T(8,128)S(1)} %get-tuple-element.17.refs_3_), custom_call_target="tpu_custom_call" | custom-call | flops 2684354560 | bytes 12845056 | tf_op jit(solution)/shard_map/pallas_call | solution.py:198
  124.8 0.1 collective-permute-start
  124.9 1.2 collective-permute-done
  126.1 1.5 collective-permute-start.1
  127.7 1.5 collective-permute-start.2
  129.2 0.5 collective-permute-start.3
  129.7 0.6 collective-permute-done.1
  130.3 2.0 %collective-permute-done.2 = f32[96,128]{1,0:T(8,128)S(1)} collective-permute-done((f32[96,128]{1,0:T(8,128)S(1)}, f32[96,128]{1,0:T(8,128)S(1)}, u32[]{:S(2)}, u32[]{:S(2)}) %collective-permute-start.2) | collective-permute-done | bytes 49184 | tf_op jit(solution)/shard_map/ppermute | solution.py:353
  132.3 1.9 %collective-permute-done.3 = f32[96,128]{1,0:T(8,128)S(1)} collective-permute-done((f32[96,128]{1,0:T(8,128)S(1)}, f32[96,128]{1,0:T(8,128)S(1)}, u32[]{:S(2)}, u32[]{:S(2)}) %collective-permute-start.3) | collective-permute-done | bytes 49184 | tf_op jit(solution)/shard_map/ppermute | solution.py:353
  134.2 0.1 collective-permute-start.4
  134.2 2.0 %collective-permute-start.5 = (f32[96,128]{1,0:T(8,128)S(1)}, f32[96,128]{1,0:T(8,128)S(1)}, u32[]{:S(2)}, u32[]{:S(2)}) collective-permute-start(f32[96,128]{1,0:T(8,128)S(1)} %add_add_fusion.refs_0_), channel_id=1, source_target_pairs={{0,8},{1,9},{2,10},{3,11},{4,12},{5,13},{6,14},{7,15},{8,0},{9,1},... | collective-permute-start | bytes 147464 | tf_op jit(solution)/shard_map/ppermute | solution.py:353
  136.2 2.4 %collective-permute-start.6 = (f32[96,128]{1,0:T(8,128)S(1)}, f32[96,128]{1,0:T(8,128)S(1)}, u32[]{:S(2)}, u32[]{:S(2)}) collective-permute-start(f32[96,128]{1,0:T(8,128)S(1)} %add_add_fusion.refs_0_), channel_id=1, source_target_pairs={{0,12},{1,13},{2,14},{3,15},{4,8},{5,9},{6,10},{7,11},{8,4},{9,5},... | collective-permute-start | bytes 147464 | tf_op jit(solution)/shard_map/ppermute | solution.py:353
  138.6 0.0 collective-permute-done.4.refs_1_
  138.6 0.9 collective-permute-done.5.refs_2_
  139.5 2.6 %collective-permute-done.6.refs_3_ = f32[96,128]{1,0:T(8,128)S(1)} collective-permute-done((f32[96,128]{1,0:T(8,128)S(1)}, f32[96,128]{1,0:T(8,128)S(1)}, u32[]{:S(2)}, u32[]{:S(2)}) %collective-permute-start.6) | collective-permute-done | bytes 49184 | tf_op jit(solution)/shard_map/ppermute | solution.py:353
  142.1 0.0 copy-done
  142.1 12.1 %shard_map.31 = f32[64,10240]{1,0:T(8,128)} custom-call(f32[96,128]{1,0:T(8,128)S(1)} %add_add_fusion.refs_0_, f32[96,128]{1,0:T(8,128)S(1)} %collective-permute-done.4.refs_1_, f32[96,128]{1,0:T(8,128)S(1)} %collective-permute-done.5.refs_2_, f32[96,128]{1,0:T(8,128)S(1)} %collective-permute-done.6.refs_3_, f32[64,128]{1,0:T(8,128)S(1)} %bitcast.4, ...), custom_call_target="tpu_custom_call" | custom-call | tf_op jit(solution)/shard_map/pallas_call | solution.py:327
  (6 shorter events, 0.1 us)
Async XLA Ops:
  6.0 78.5 %all-to-all-start.1 = ((bf16[32,6,64,128]{3,2,1,0:T(8,128)(2,1)}), bf16[32,6,64,128]{3,2,1,0:T(8,128)(2,1)S(1)}, u32[]{:S(2)}, u32[]{:S(2)}) async-start(bf16[32,6,64,128]{3,2,1,0:T(8,128)(2,1)} %get-tuple-element.16), calls=%async_computation.1 | async-start | bytes 6291456 | tf_op jit(solution)/shard_map/all_to_all | solution.py:377
  84.6 1.6 %copy-start.1 = (bf16[32,6,64,128]{3,2,1,0:T(8,128)(2,1)}, bf16[32,6,64,128]{3,2,1,0:T(8,128)(2,1)S(1)}, u32[]{:S(2)}) copy-start(bf16[32,6,64,128]{3,2,1,0:T(8,128)(2,1)S(1)} %all-to-all-done.1) | copy-start | bytes 9437188
  86.2 30.3 %all-to-all-start = ((bf16[32,2,64,128]{3,2,1,0:T(8,128)(2,1)}), bf16[32,2,64,128]{3,2,1,0:T(8,128)(2,1)S(1)}, u32[]{:S(2)}, u32[]{:S(2)}) async-start(bf16[32,2,64,128]{3,2,1,0:T(8,128)(2,1)} %get-tuple-element.14), calls=%async_computation | async-start | bytes 2097152 | tf_op jit(solution)/shard_map/all_to_all | solution.py:377
  106.7 35.4 %copy-start = (f32[128,64]{0,1:T(8,128)S(1)}, f32[128,64]{0,1:T(8,128)}, u32[]{:S(2)}) copy-start(f32[128,64]{0,1:T(8,128)} %param.3) | copy-start | bytes 98308
  124.8 1.3 collective-permute-start
  126.1 4.2 %collective-permute-start.1 = (f32[96,128]{1,0:T(8,128)S(1)}, f32[96,128]{1,0:T(8,128)S(1)}, u32[]{:S(2)}, u32[]{:S(2)}) collective-permute-start(f32[96,128]{1,0:T(8,128)S(1)} %add.98), channel_id=1, source_target_pairs={{0,2},{1,3},{2,0},{3,1},{4,6},{5,7},{6,4},{7,5},{8,10},{9,11},{10,... | collective-permute-start | bytes 147464 | tf_op jit(solution)/shard_map/ppermute | solution.py:353
  127.7 4.6 %collective-permute-start.2 = (f32[96,128]{1,0:T(8,128)S(1)}, f32[96,128]{1,0:T(8,128)S(1)}, u32[]{:S(2)}, u32[]{:S(2)}) collective-permute-start(f32[96,128]{1,0:T(8,128)S(1)} %add.98), channel_id=1, source_target_pairs={{0,16},{1,17},{2,18},{3,19},{4,20},{5,21},{6,22},{7,23},{8,24},{9,... | collective-permute-start | bytes 147464 | tf_op jit(solution)/shard_map/ppermute | solution.py:353
  129.2 5.0 %collective-permute-start.3 = (f32[96,128]{1,0:T(8,128)S(1)}, f32[96,128]{1,0:T(8,128)S(1)}, u32[]{:S(2)}, u32[]{:S(2)}) collective-permute-start(f32[96,128]{1,0:T(8,128)S(1)} %add.98), channel_id=1, source_target_pairs={{0,18},{1,19},{2,16},{3,17},{4,22},{5,23},{6,20},{7,21},{8,26},{9,... | collective-permute-start | bytes 147464 | tf_op jit(solution)/shard_map/ppermute | solution.py:353
  134.2 4.5 %collective-permute-start.4 = (f32[96,128]{1,0:T(8,128)S(1)}, f32[96,128]{1,0:T(8,128)S(1)}, u32[]{:S(2)}, u32[]{:S(2)}) collective-permute-start(f32[96,128]{1,0:T(8,128)S(1)} %add_add_fusion.refs_0_), channel_id=1, source_target_pairs={{0,4},{1,5},{2,6},{3,7},{4,0},{5,1},{6,2},{7,3},{8,12},{9,13},{10,... | collective-permute-start | bytes 147464 | tf_op jit(solution)/shard_map/ppermute | solution.py:353
  134.2 5.3 %collective-permute-start.5 = (f32[96,128]{1,0:T(8,128)S(1)}, f32[96,128]{1,0:T(8,128)S(1)}, u32[]{:S(2)}, u32[]{:S(2)}) collective-permute-start(f32[96,128]{1,0:T(8,128)S(1)} %add_add_fusion.refs_0_), channel_id=1, source_target_pairs={{0,8},{1,9},{2,10},{3,11},{4,12},{5,13},{6,14},{7,15},{8,0},{9,1},... | collective-permute-start | bytes 147464 | tf_op jit(solution)/shard_map/ppermute | solution.py:353
  136.2 5.9 %collective-permute-start.6 = (f32[96,128]{1,0:T(8,128)S(1)}, f32[96,128]{1,0:T(8,128)S(1)}, u32[]{:S(2)}, u32[]{:S(2)}) collective-permute-start(f32[96,128]{1,0:T(8,128)S(1)} %add_add_fusion.refs_0_), channel_id=1, source_target_pairs={{0,12},{1,13},{2,14},{3,15},{4,8},{5,9},{6,10},{7,11},{8,4},{9,5},... | collective-permute-start | bytes 147464 | tf_op jit(solution)/shard_map/ppermute | solution.py:353

commit v4 on v3

--- a/solution.py
+++ b/solution.py
@@ -16,7 +16,8 @@
 PIVOTS = 4
 SNAPSHOT_TILE = 16
 EARLY_ROWS = 6
-VMEM_BYTES = 51 * 2**20
+VMEM_BYTES = 52 * 2**20
+MERGE_VMEM_BYTES = 61000 * 2**10
 
 
 highest = lax.Precision.HIGHEST
@@ -31,8 +32,8 @@
     return jnp.dot(first_op, second_op, precision=highest, preferred_element_type=jnp.float32)
 
 
-def spectral_table(points, wave_count):
-    lon_ids = jnp.arange(points, dtype=jnp.int32)
+def spectral_table(points, wave_count, row_count):
+    lon_ids = jnp.arange(row_count, dtype=jnp.int32)
     col_ids = jnp.arange(2 * wave_count, dtype=jnp.int32)
     wavenumber = jnp.where(col_ids < wave_count, col_ids, col_ids - wave_count + 1)
     phase_index = lon_ids[:, None] * wavenumber[None, :] % points
@@ -82,7 +83,7 @@
 
 def local_tree(snapshots, test_matrix):
     dev_rows = NTH // lax.axis_size("lon")
-    dft_table = spectral_table(NPH, MMAX)
+    dft_table = spectral_table(NPH, MMAX, NPH)
     row_weight = area_weight(lax.axis_index("lon") * dev_rows, dev_rows, NTH)
     spectra = jnp.einsum(
         "pst,pk->stk",
@@ -114,7 +115,7 @@
 
 
 def split_table(points, wave_count):
-    table = spectral_table(points, wave_count)
+    table = spectral_table(points, wave_count, points // 2)
     high = lax.reduce_precision(table, 8, 7)
     return jnp.stack([high.astype(jnp.bfloat16), (table - high).astype(jnp.bfloat16)])
 
@@ -154,17 +155,22 @@
     def _():
         acc[...] = jnp.zeros_like(acc)
         for src in range(sources):
-            for grp in range(groups):
-                for row in range(rows):
-                    start = (row * groups + grp) * rank_rows
-                    lhs[start : start + rank_rows, src * points : (src + 1) * points] = x_ref[
+            half, place = divmod(src, sources // 2)
+            for row in range(rows):
+                for grp in range(groups):
+                    start = ((half * rows + row) * groups + grp) * rank_rows
+                    lhs[start : start + rank_rows, place * points : (place + 1) * points] = x_ref[
                         src, grp, row
                     ]
 
     span = groups * rank_rows
     values = lhs[...]
-    spectra = jnp.dot(values, table_ref[0], preferred_element_type=jnp.float32)
-    spectra += jnp.dot(values, table_ref[1], preferred_element_type=jnp.float32)
+    halves = jnp.dot(values, table_ref[0], preferred_element_type=jnp.float32)
+    halves += jnp.dot(values, table_ref[1], preferred_element_type=jnp.float32)
+    col_ids = step * COL_TILE + lax.broadcasted_iota(jnp.int32, (1, COL_TILE), 1)
+    wavenumber = jnp.where(col_ids < MMAX, col_ids, col_ids - MMAX + 1)
+    turned = (1 - 2 * (wavenumber & 1)).astype(jnp.float32)
+    spectra = halves[: rows * span] + turned * halves[rows * span :]
     tops, rests = [], []
     for row in range(rows):
         scaled = spectra[row * span : (row + 1) * span] * weight_ref[0, first_row + row]
@@ -192,7 +198,7 @@
 
 def spectra_and_gram(blocks, row_weight, table, first_row, *before):
     sources, groups, rows, rank_rows, points = blocks.shape
-    _, lons, cols = table.shape
+    _, half_lons, cols = table.shape
     span = groups * rank_rows
     packed = (rank_rows + rank_rows // 2, span)
     return pl.pallas_call(
@@ -201,7 +207,7 @@
         in_specs=[
             pl.BlockSpec(memory_space=pltpu.SMEM),
             pl.BlockSpec(blocks.shape, lambda i: (0, 0, 0, 0, 0)),
-            pl.BlockSpec((2, lons, COL_TILE), lambda i: (0, 0, i)),
+            pl.BlockSpec((2, half_lons, COL_TILE), lambda i: (0, 0, i)),
             *[pl.BlockSpec(packed, lambda i: (0, 0)) for _ in before],
         ],
         out_specs=[
@@ -213,13 +219,13 @@
             jax.ShapeDtypeStruct(packed, jnp.float32),
         ],
         scratch_shapes=[
-            pltpu.VMEM((rows * span, lons), jnp.bfloat16),
+            pltpu.VMEM((2 * rows * span, half_lons), jnp.bfloat16),
             pltpu.VMEM((2 * span, span), jnp.float32),
         ],
         compiler_params=pltpu.CompilerParams(vmem_limit_bytes=VMEM_BYTES),
         cost_estimate=pl.CostEstimate(
-            flops=4 * rows * span * lons * cols,
-            bytes_accessed=2 * blocks.size + 4 * lons * cols + 4 * rows * span * cols,
+            flops=8 * rows * span * half_lons * cols,
+            bytes_accessed=2 * blocks.size + 4 * half_lons * cols + 4 * rows * span * cols,
             transcendentals=0,
         ),
     )(row_weight.reshape(1, -1), blocks, table, *before)
@@ -276,12 +282,18 @@
 
 
 def merge_kernel(*refs, split):
-    *part_refs, test_ref, early_ref, late_ref, out_ref, mix_ref, first_ref, second_ref = refs
+    *part_refs, test_ref, early_ref, late_ref, out_ref, mix_ref, first_ref, second_ref, held, sems = refs
     rank = test_ref.shape[0]
     row = pl.program_id(0)
+    fetches = [
+        pltpu.make_async_copy(early_ref, held.at[pl.ds(0, split)], sems.at[0]),
+        pltpu.make_async_copy(late_ref, held.at[pl.ds(split, late_ref.shape[0])], sems.at[1]),
+    ]
 
     @pl.when(row == 0)
     def _():
+        for fetch in fetches:
+            fetch.start()
         gram = unpacked(add_up([part[...] for part in part_refs]))
         test_t = test_ref[...]
         sketch = dot_full(gram, test_t, NT_DIMS)
@@ -307,17 +319,11 @@
         mix_ref[rank:, : 2 * rank] = rest
         mix_ref[rank:, 2 * rank :] = jnp.zeros_like(rest)
 
-    def mix(modes):
-        both = jnp.dot(mix_ref[...], modes, preferred_element_type=jnp.float32)
-        out_ref[...] = both[:rank] + both[rank:]
-
-    @pl.when(row < split)
-    def _():
-        mix(early_ref[0])
-
-    @pl.when(row >= split)
-    def _():
-        mix(late_ref[0])
+        for fetch in fetches:
+            fetch.wait()
+
+    both = jnp.dot(mix_ref[...], held[row], preferred_element_type=jnp.float32)
+    out_ref[...] = both[:rank] + both[rank:]
 
 
 def merge_and_mix(gram_parts, test_matrix, early, late):
@@ -330,8 +336,8 @@
         in_specs=[
             *[pl.BlockSpec(part.shape, lambda i: (0, 0)) for part in gram_parts],
             pl.BlockSpec((rank, 2 * rank), lambda i: (0, 0)),
-            pl.BlockSpec((1, height, cols), lambda i: (jnp.minimum(i, split - 1), 0, 0)),
-            pl.BlockSpec((1, height, cols), lambda i: (jnp.maximum(i - split, 0), 0, 0)),
+            pl.BlockSpec(memory_space=pl.ANY),
+            pl.BlockSpec(memory_space=pl.ANY),
         ],
         out_specs=pl.BlockSpec((rank, cols), lambda i: (0, i)),
         out_shape=jax.ShapeDtypeStruct((rank, rows * cols), jnp.float32),
@@ -339,8 +345,10 @@
             pltpu.VMEM((2 * rank, height), jnp.bfloat16),
             pltpu.VMEM((rank, 6 * rank), jnp.float32),
             pltpu.VMEM((rank, 2 * rank), jnp.float32),
-        ],
-        compiler_params=pltpu.CompilerParams(vmem_limit_bytes=VMEM_BYTES),
+            pltpu.VMEM((rows, height, cols), jnp.bfloat16),
+            pltpu.SemaphoreType.DMA((2,)),
+        ],
+        compiler_params=pltpu.CompilerParams(vmem_limit_bytes=MERGE_VMEM_BYTES),
     )(*gram_parts, test_matrix.T, early, late)
 
 

time: 155 us -> 153 us (0.987)
  waiting for transfers between devices: 36.4 us -> 65.8 us
  other arithmetic: 53.7 us -> 24.6 us
  Pallas kernels: 43 us -> 40.9 us
    all_to_all x2, waiting for transfers between devices: 27.3 us -> 56.6 us  [local_pair(): lax.all_to_all(part, ('lon', 'tm'), split_axis=0, concat_axis=0, tiled=True)]
    convert_element_type x1, other arithmetic: 44.6 us -> 21.7 us  [split_table(): high.astype(jnp.bfloat16)]
    another operation x1, other arithmetic: 8.99 us -> 2.76 us  [split_table(): jnp.stack([high.astype(jnp.bfloat16), (table - high).astype(jnp.bfloat16)])]
    pallas_call x1, Pallas kernels: 12.1 us -> 10.5 us  [merge_and_mix(): pl.pallas_call(functools.partial(merge_kernel, split=split), grid=(rows,)...]
  transfers between devices with their start and end apart: 9 -> 9, of which waited for: 8 -> 8; matrix products, arithmetic and copies ran while one was open for 35% -> 16% of each run, Pallas kernels for 11% -> 11%
where the time goes in v4:
time: 153 us
  waiting for transfers between devices  65.8 us (43%)
  Pallas kernels  40.9 us (27%)
  other arithmetic  24.6 us (16%)
  starting transfers between devices  19.3 us (13%)
  local copies, waits for them, and re-layouts  2.24 us (1%)
    all_to_all x2, waiting for transfers between devices, local_pair(): lax.all_to_all(part, ('lon', 'tm'), split_axis=0, concat_axis=0, tiled=True)  56.6 us
    pallas_call x2, Pallas kernels, spectra_and_gram(): pl.pallas_call(functools.partial(spectra_kernel, first_row=first_row), gr...  24.4 us
    convert_element_type x1, other arithmetic, split_table(): high.astype(jnp.bfloat16)  21.7 us
    all_to_all x2, starting transfers between devices, local_pair(): lax.all_to_all(part, ('lon', 'tm'), split_axis=0, concat_axis=0, tiled=True)  11.3 us
    pallas_call x1, Pallas kernels, merge_and_mix(): pl.pallas_call(functools.partial(merge_kernel, split=split), grid=(rows,)...  10.5 us
    ppermute x7, waiting for transfers between devices, exchanged(): lax.ppermute(array, axes, [(i, i ^ mask) for i in range(count)])  9.16 us
    ppermute x7, starting transfers between devices, exchanged(): lax.ppermute(array, axes, [(i, i ^ mask) for i in range(count)])  8.01 us
    pallas_call x1, Pallas kernels, relayout(): pl.pallas_call(relayout_kernel, grid=(rank_rows // some,), in_specs=[pl.B...  6.06 us
  transfers between devices with their start and end apart: 9, of which 8 were waited for; matrix products, arithmetic and copies ran while one was open for 16% of the time, Pallas kernels for 11%

profile of v4, /device:TPU:0, one launch (start us, length us, event | category | flops | bytes accessed | tf_op | source)
XLA Modules:
  0.0 153.0 jit_solution(376570207101178044)
XLA Ops:
  0.0 6.1 %shard_map.28 = (bf16[32,6,64,128]{3,2,1,0:T(8,128)(2,1)}, bf16[32,2,64,128]{3,2,1,0:T(8,128)(2,1)}) custom-call(bf16[128,64,256]{2,1,0:T(8,128)(2,1)} %x_ref.1), custom_call_target="tpu_custom_call" | custom-call | tf_op jit(solution)/shard_map/pallas_call | solution.py:137
  6.1 7.3 %all-to-all-start.1 = ((bf16[32,6,64,128]{3,2,1,0:T(8,128)(2,1)}), bf16[32,6,64,128]{3,2,1,0:T(8,128)(2,1)S(1)}, u32[]{:S(2)}, u32[]{:S(2)}) async-start(bf16[32,6,64,128]{3,2,1,0:T(8,128)(2,1)} %get-tuple-element.16), calls=%async_computation.1 | async-start | bytes 6291456 | tf_op jit(solution)/shard_map/all_to_all | solution.py:385
  13.4 21.7 %reduce-precision_convert_fusion = (bf16[1,1024,1280]{2,1,0:T(8,128)(2,1)S(1)}, bf16[1,1024,1280]{2,1,0:T(8,128)(2,1)S(1)}) fusion(f32[1280]{0:T(1024)S(1)} %rsqrt_multiply_fusion, s32[1280]{0:T(1024)S(1)} %add_select_fusion.1, pred[1280]{0:T(1024)(128)(4,1)S(1)} %iota_compare_fusion), kind=kLoop, calls=%fused_computation.4 | loop fusion | flops 26214400 | bytes 5254400 | tf_op jit(solution)/shard_map/convert_element_type | solution.py:120
  35.1 2.8 %pad_maximum_fusion.refs_2_ = bf16[2,1024,1280]{2,1,0:T(8,128)(2,1)} fusion(bf16[1,1024,1280]{2,1,0:T(8,128)(2,1)S(1)} %get-tuple-element.22, bf16[1,1024,1280]{2,1,0:T(8,128)(2,1)S(1)} %get-tuple-element.21), kind=kLoop, calls=%fused_computation.9 | loop fusion | flops 2621440 | bytes 10485760 | tf_op jit(solution)/shard_map/stack | solution.py:120
  37.9 46.7 %all-to-all-done.1 = bf16[32,6,64,128]{3,2,1,0:T(8,128)(2,1)S(1)} async-done(((bf16[32,6,64,128]{3,2,1,0:T(8,128)(2,1)}), bf16[32,6,64,128]{3,2,1,0:T(8,128)(2,1)S(1)}, u32[]{:S(2)}, u32[]{:S(2)}) %all-to-all-start.1) | async-done | bytes 3145760 | tf_op jit(solution)/shard_map/all_to_all | solution.py:385
  84.6 0.0 copy-start
  84.6 1.6 %copy-done = bf16[32,6,64,128]{3,2,1,0:T(8,128)(2,1)} copy-done((bf16[32,6,64,128]{3,2,1,0:T(8,128)(2,1)}, bf16[32,6,64,128]{3,2,1,0:T(8,128)(2,1)S(1)}, u32[]{:S(2)}) %copy-start) | copy-done | bytes 3145752
  86.2 4.0 %all-to-all-start = ((bf16[32,2,64,128]{3,2,1,0:T(8,128)(2,1)}), bf16[32,2,64,128]{3,2,1,0:T(8,128)(2,1)S(1)}, u32[]{:S(2)}, u32[]{:S(2)}) async-start(bf16[32,2,64,128]{3,2,1,0:T(8,128)(2,1)} %get-tuple-element.14), calls=%async_computation | async-start | bytes 2097152 | tf_op jit(solution)/shard_map/all_to_all | solution.py:385
  90.3 16.2 %shard_map.29 = (bf16[6,256,1280]{2,1,0:T(8,128)(2,1)}, f32[96,128]{1,0:T(8,128)S(1)}) custom-call(f32[1,8]{1,0:T(1,128)S(1)} %sine_sqrt_fusion.refs_0_, bf16[16,2,6,64,128]{4,3,2,1,0:T(8,128)(2,1)} %bitcast.4, bf16[2,1024,1280]{2,1,0:T(8,128)(2,1)} %pad_maximum_fusion.refs_2_), custom_call_target="tpu_custom_call" | custom-call | flops 8053063680 | bytes 12320768 | tf_op jit(solution)/shard_map/pallas_call | solution.py:204
  106.5 10.0 %all-to-all-done = bf16[32,2,64,128]{3,2,1,0:T(8,128)(2,1)S(1)} async-done(((bf16[32,2,64,128]{3,2,1,0:T(8,128)(2,1)}), bf16[32,2,64,128]{3,2,1,0:T(8,128)(2,1)S(1)}, u32[]{:S(2)}, u32[]{:S(2)}) %all-to-all-start) | async-done | bytes 1048608 | tf_op jit(solution)/shard_map/all_to_all | solution.py:385
  116.5 8.1 %shard_map.30 = (bf16[2,256,1280]{2,1,0:T(8,128)(2,1)}, f32[96,128]{1,0:T(8,128)S(1)}) custom-call(f32[1,8]{1,0:T(1,128)S(1)} %sine_sqrt_fusion.refs_0_, bf16[16,2,2,64,128]{4,3,2,1,0:T(8,128)(2,1)S(1)} %bitcast.3, bf16[2,1024,1280]{2,1,0:T(8,128)(2,1)} %pad_maximum_fusion.refs_2_, f32[96,128]{1,0:T(8,128)S(1)} %get-tuple-element.17.refs_3_), custom_call_target="tpu_custom_call" | custom-call | flops 2684354560 | bytes 7602176 | tf_op jit(solution)/shard_map/pallas_call | solution.py:204
  124.6 0.0 collective-permute-start
  124.6 1.2 collective-permute-done
  125.9 1.6 %collective-permute-start.1 = (f32[96,128]{1,0:T(8,128)S(1)}, f32[96,128]{1,0:T(8,128)S(1)}, u32[]{:S(2)}, u32[]{:S(2)}) collective-permute-start(f32[96,128]{1,0:T(8,128)S(1)} %add.98), channel_id=1, source_target_pairs={{0,2},{1,3},{2,0},{3,1},{4,6},{5,7},{6,4},{7,5},{8,10},{9,11},{10,... | collective-permute-start | bytes 147464 | tf_op jit(solution)/shard_map/ppermute | solution.py:361
  127.4 1.5 collective-permute-start.2
  128.9 0.5 collective-permute-start.3
  129.4 0.6 collective-permute-done.1
  130.0 2.0 %collective-permute-done.2 = f32[96,128]{1,0:T(8,128)S(1)} collective-permute-done((f32[96,128]{1,0:T(8,128)S(1)}, f32[96,128]{1,0:T(8,128)S(1)}, u32[]{:S(2)}, u32[]{:S(2)}) %collective-permute-start.2) | collective-permute-done | bytes 49184 | tf_op jit(solution)/shard_map/ppermute | solution.py:361
  132.0 1.8 %collective-permute-done.3 = f32[96,128]{1,0:T(8,128)S(1)} collective-permute-done((f32[96,128]{1,0:T(8,128)S(1)}, f32[96,128]{1,0:T(8,128)S(1)}, u32[]{:S(2)}, u32[]{:S(2)}) %collective-permute-start.3) | collective-permute-done | bytes 49184 | tf_op jit(solution)/shard_map/ppermute | solution.py:361
  133.9 0.0 copy-start.1
  133.9 0.1 collective-permute-start.4
  134.0 2.0 %collective-permute-start.5 = (f32[96,128]{1,0:T(8,128)S(1)}, f32[96,128]{1,0:T(8,128)S(1)}, u32[]{:S(2)}, u32[]{:S(2)}) collective-permute-start(f32[96,128]{1,0:T(8,128)S(1)} %add_add_fusion.refs_0_), channel_id=1, source_target_pairs={{0,8},{1,9},{2,10},{3,11},{4,12},{5,13},{6,14},{7,15},{8,0},{9,1},... | collective-permute-start | bytes 147464 | tf_op jit(solution)/shard_map/ppermute | solution.py:361
  136.0 2.4 %collective-permute-start.6 = (f32[96,128]{1,0:T(8,128)S(1)}, f32[96,128]{1,0:T(8,128)S(1)}, u32[]{:S(2)}, u32[]{:S(2)}) collective-permute-start(f32[96,128]{1,0:T(8,128)S(1)} %add_add_fusion.refs_0_), channel_id=1, source_target_pairs={{0,12},{1,13},{2,14},{3,15},{4,8},{5,9},{6,10},{7,11},{8,4},{9,5},... | collective-permute-start | bytes 147464 | tf_op jit(solution)/shard_map/ppermute | solution.py:361
  138.4 0.0 collective-permute-done.4.refs_1_
  138.4 0.0 copy-start.2
  138.4 0.9 collective-permute-done.5.refs_2_
  139.2 0.0 copy-start.3
  139.3 2.6 %collective-permute-done.6.refs_3_ = f32[96,128]{1,0:T(8,128)S(1)} collective-permute-done((f32[96,128]{1,0:T(8,128)S(1)}, f32[96,128]{1,0:T(8,128)S(1)}, u32[]{:S(2)}, u32[]{:S(2)}) %collective-permute-start.6) | collective-permute-done | bytes 49184 | tf_op jit(solution)/shard_map/ppermute | solution.py:361
  141.9 0.0 copy-start.4
  141.9 0.0 copy-done.1
  141.9 0.0 copy-done.2
  141.9 0.0 copy-done.3
  141.9 0.6 copy-done.4
  142.5 10.5 %shard_map.31 = f32[64,10240]{1,0:T(8,128)} custom-call(f32[96,128]{1,0:T(8,128)} %copy-done.1, f32[96,128]{1,0:T(8,128)} %copy-done.2, f32[96,128]{1,0:T(8,128)} %copy-done.3, f32[96,128]{1,0:T(8,128)} %copy-done.4, f32[64,128]{1,0:T(8,128)} %bitcast.5, bf16[6,256,1280]{2,1,0:T(8,128)(2,1)} %get-tuple-element.19.refs_5_, ...), custom_call_target="tpu_custom_call" | custom-call | tf_op jit(solution)/shard_map/pallas_call | solution.py:333
  (6 shorter events, 0.1 us)
Async XLA Ops:
  6.1 78.5 %all-to-all-start.1 = ((bf16[32,6,64,128]{3,2,1,0:T(8,128)(2,1)}), bf16[32,6,64,128]{3,2,1,0:T(8,128)(2,1)S(1)}, u32[]{:S(2)}, u32[]{:S(2)}) async-start(bf16[32,6,64,128]{3,2,1,0:T(8,128)(2,1)} %get-tuple-element.16), calls=%async_computation.1 | async-start | bytes 6291456 | tf_op jit(solution)/shard_map/all_to_all | solution.py:385
  84.6 1.6 %copy-start = (bf16[32,6,64,128]{3,2,1,0:T(8,128)(2,1)}, bf16[32,6,64,128]{3,2,1,0:T(8,128)(2,1)S(1)}, u32[]{:S(2)}) copy-start(bf16[32,6,64,128]{3,2,1,0:T(8,128)(2,1)S(1)} %all-to-all-done.1) | copy-start | bytes 9437188
  86.2 30.3 %all-to-all-start = ((bf16[32,2,64,128]{3,2,1,0:T(8,128)(2,1)}), bf16[32,2,64,128]{3,2,1,0:T(8,128)(2,1)S(1)}, u32[]{:S(2)}, u32[]{:S(2)}) async-start(bf16[32,2,64,128]{3,2,1,0:T(8,128)(2,1)} %get-tuple-element.14), calls=%async_computation | async-start | bytes 2097152 | tf_op jit(solution)/shard_map/all_to_all | solution.py:385
  124.6 1.2 collective-permute-start
  125.9 4.1 %collective-permute-start.1 = (f32[96,128]{1,0:T(8,128)S(1)}, f32[96,128]{1,0:T(8,128)S(1)}, u32[]{:S(2)}, u32[]{:S(2)}) collective-permute-start(f32[96,128]{1,0:T(8,128)S(1)} %add.98), channel_id=1, source_target_pairs={{0,2},{1,3},{2,0},{3,1},{4,6},{5,7},{6,4},{7,5},{8,10},{9,11},{10,... | collective-permute-start | bytes 147464 | tf_op jit(solution)/shard_map/ppermute | solution.py:361
  127.4 4.6 %collective-permute-start.2 = (f32[96,128]{1,0:T(8,128)S(1)}, f32[96,128]{1,0:T(8,128)S(1)}, u32[]{:S(2)}, u32[]{:S(2)}) collective-permute-start(f32[96,128]{1,0:T(8,128)S(1)} %add.98), channel_id=1, source_target_pairs={{0,16},{1,17},{2,18},{3,19},{4,20},{5,21},{6,22},{7,23},{8,24},{9,... | collective-permute-start | bytes 147464 | tf_op jit(solution)/shard_map/ppermute | solution.py:361
  128.9 5.0 %collective-permute-start.3 = (f32[96,128]{1,0:T(8,128)S(1)}, f32[96,128]{1,0:T(8,128)S(1)}, u32[]{:S(2)}, u32[]{:S(2)}) collective-permute-start(f32[96,128]{1,0:T(8,128)S(1)} %add.98), channel_id=1, source_target_pairs={{0,18},{1,19},{2,16},{3,17},{4,22},{5,23},{6,20},{7,21},{8,26},{9,... | collective-permute-start | bytes 147464 | tf_op jit(solution)/shard_map/ppermute | solution.py:361
  133.9 8.0 %copy-start.1 = (f32[96,128]{1,0:T(8,128)}, f32[96,128]{1,0:T(8,128)S(1)}, u32[]{:S(2)}) copy-start(f32[96,128]{1,0:T(8,128)S(1)} %add_add_fusion.refs_0_) | copy-start | bytes 147460
  133.9 4.5 %collective-permute-start.4 = (f32[96,128]{1,0:T(8,128)S(1)}, f32[96,128]{1,0:T(8,128)S(1)}, u32[]{:S(2)}, u32[]{:S(2)}) collective-permute-start(f32[96,128]{1,0:T(8,128)S(1)} %add_add_fusion.refs_0_), channel_id=1, source_target_pairs={{0,4},{1,5},{2,6},{3,7},{4,0},{5,1},{6,2},{7,3},{8,12},{9,13},{10,... | collective-permute-start | bytes 147464 | tf_op jit(solution)/shard_map/ppermute | solution.py:361
  134.0 5.3 %collective-permute-start.5 = (f32[96,128]{1,0:T(8,128)S(1)}, f32[96,128]{1,0:T(8,128)S(1)}, u32[]{:S(2)}, u32[]{:S(2)}) collective-permute-start(f32[96,128]{1,0:T(8,128)S(1)} %add_add_fusion.refs_0_), channel_id=1, source_target_pairs={{0,8},{1,9},{2,10},{3,11},{4,12},{5,13},{6,14},{7,15},{8,0},{9,1},... | collective-permute-start | bytes 147464 | tf_op jit(solution)/shard_map/ppermute | solution.py:361
  136.0 5.9 %collective-permute-start.6 = (f32[96,128]{1,0:T(8,128)S(1)}, f32[96,128]{1,0:T(8,128)S(1)}, u32[]{:S(2)}, u32[]{:S(2)}) collective-permute-start(f32[96,128]{1,0:T(8,128)S(1)} %add_add_fusion.refs_0_), channel_id=1, source_target_pairs={{0,12},{1,13},{2,14},{3,15},{4,8},{5,9},{6,10},{7,11},{8,4},{9,5},... | collective-permute-start | bytes 147464 | tf_op jit(solution)/shard_map/ppermute | solution.py:361
  138.4 3.5 %copy-start.2 = (f32[96,128]{1,0:T(8,128)}, f32[96,128]{1,0:T(8,128)S(1)}, u32[]{:S(2)}) copy-start(f32[96,128]{1,0:T(8,128)S(1)} %collective-permute-done.4.refs_1_) | copy-start | bytes 147460
  139.2 2.6 %copy-start.3 = (f32[96,128]{1,0:T(8,128)}, f32[96,128]{1,0:T(8,128)S(1)}, u32[]{:S(2)}) copy-start(f32[96,128]{1,0:T(8,128)S(1)} %collective-permute-done.5.refs_2_) | copy-start | bytes 147460
  141.9 0.6 copy-start.4

commit v5 on v4

--- a/solution.py
+++ b/solution.py
@@ -16,8 +16,8 @@
 PIVOTS = 4
 SNAPSHOT_TILE = 16
 EARLY_ROWS = 6
-VMEM_BYTES = 52 * 2**20
-MERGE_VMEM_BYTES = 61000 * 2**10
+VMEM_BYTES = 50 * 2**20
+RELAYOUT_VMEM_BYTES = 58 * 2**20
 
 
 highest = lax.Precision.HIGHEST
@@ -116,8 +116,9 @@
 
 def split_table(points, wave_count):
     table = spectral_table(points, wave_count, points // 2)
+    table = table.reshape(points // 2, -1, COL_TILE).transpose(1, 0, 2)
     high = lax.reduce_precision(table, 8, 7)
-    return jnp.stack([high.astype(jnp.bfloat16), (table - high).astype(jnp.bfloat16)])
+    return jnp.stack([high.astype(jnp.bfloat16), (table - high).astype(jnp.bfloat16)], axis=1)
 
 
 def relayout_kernel(x_ref, first_ref, last_ref):
@@ -142,78 +143,80 @@
         out_shape=[
             jax.ShapeDtypeStruct((devices, cut, rank_rows, points), snapshots.dtype) for cut in cuts
         ],
-        compiler_params=pltpu.CompilerParams(vmem_limit_bytes=VMEM_BYTES),
+        compiler_params=pltpu.CompilerParams(vmem_limit_bytes=RELAYOUT_VMEM_BYTES),
     )(snapshots)
 
 
 def spectra_kernel(*refs, first_row):
-    weight_ref, x_ref, table_ref, *before, modes_ref, gram_ref, lhs, acc = refs
+    weight_ref, x_ref, table_ref, *before, modes_ref, gram_ref, lhs, acc, held, sems = refs
     sources, groups, rows, rank_rows, points = x_ref.shape
-    step = pl.program_id(0)
-
-    @pl.when(step == 0)
-    def _():
-        acc[...] = jnp.zeros_like(acc)
-        for src in range(sources):
-            half, place = divmod(src, sources // 2)
-            for row in range(rows):
-                for grp in range(groups):
-                    start = ((half * rows + row) * groups + grp) * rank_rows
-                    lhs[start : start + rank_rows, place * points : (place + 1) * points] = x_ref[
-                        src, grp, row
-                    ]
-
+    tiles = table_ref.shape[0]
     span = groups * rank_rows
-    values = lhs[...]
-    halves = jnp.dot(values, table_ref[0], preferred_element_type=jnp.float32)
-    halves += jnp.dot(values, table_ref[1], preferred_element_type=jnp.float32)
-    col_ids = step * COL_TILE + lax.broadcasted_iota(jnp.int32, (1, COL_TILE), 1)
-    wavenumber = jnp.where(col_ids < MMAX, col_ids, col_ids - MMAX + 1)
-    turned = (1 - 2 * (wavenumber & 1)).astype(jnp.float32)
-    spectra = halves[: rows * span] + turned * halves[rows * span :]
-    tops, rests = [], []
-    for row in range(rows):
-        scaled = spectra[row * span : (row + 1) * span] * weight_ref[0, first_row + row]
-        top = scaled.astype(jnp.bfloat16)
-        rest = (scaled - top.astype(jnp.float32)).astype(jnp.bfloat16)
-        modes_ref[row, :span] = top
-        modes_ref[row, span:] = rest
-        tops.append(top)
-        rests.append(rest)
-    top = jnp.concatenate(tops, axis=1)
-    both = jnp.concatenate([top, jnp.concatenate(rests, axis=1)], axis=0)
-    acc[...] += lax.dot_general(both, top, NT_DIMS, preferred_element_type=jnp.float32)
-
-    @pl.when(step == pl.num_programs(0) - 1)
-    def _():
-        cross = acc[span:, :]
-        gram = acc[:span, :] + (cross + cross.T)
-        low = gram[rank_rows:, rank_rows:]
-        low = jnp.concatenate([low[: rank_rows // 2], low[rank_rows // 2 :]], axis=1)
-        packed = jnp.concatenate([gram[:rank_rows], low], axis=0)
-        for ref in before:
-            packed += ref[...]
-        gram_ref[...] = packed
+
+    def fetch(step):
+        return pltpu.make_async_copy(table_ref.at[step], held.at[step], sems.at[step])
+
+    for step in range(tiles):
+        fetch(step).start()
+    acc[...] = jnp.zeros_like(acc)
+    for src in range(sources):
+        half, place = divmod(src, sources // 2)
+        for row in range(rows):
+            for grp in range(groups):
+                start = ((half * rows + row) * groups + grp) * rank_rows
+                lhs[start : start + rank_rows, place * points : (place + 1) * points] = x_ref[
+                    src, grp, row
+                ]
+
+    @pl.loop(0, tiles)
+    def _(step):
+        fetch(step).wait()
+        tile = pl.ds(pl.multiple_of(step * COL_TILE, COL_TILE), COL_TILE)
+        values = lhs[...]
+        halves = jnp.dot(values, held[step, 0], preferred_element_type=jnp.float32)
+        halves += jnp.dot(values, held[step, 1], preferred_element_type=jnp.float32)
+        col_ids = step * COL_TILE + lax.broadcasted_iota(jnp.int32, (1, COL_TILE), 1)
+        wavenumber = jnp.where(col_ids < MMAX, col_ids, col_ids - MMAX + 1)
+        turned = (1 - 2 * (wavenumber & 1)).astype(jnp.float32)
+        spectra = halves[: rows * span] + turned * halves[rows * span :]
+        tops, rests = [], []
+        for row in range(rows):
+            scaled = spectra[row * span : (row + 1) * span] * weight_ref[0, first_row + row]
+            top = scaled.astype(jnp.bfloat16)
+            rest = (scaled - top.astype(jnp.float32)).astype(jnp.bfloat16)
+            modes_ref[row, :span, tile] = top
+            modes_ref[row, span:, tile] = rest
+            tops.append(top)
+            rests.append(rest)
+        top = jnp.concatenate(tops, axis=1)
+        both = jnp.concatenate([top, jnp.concatenate(rests, axis=1)], axis=0)
+        acc[...] += lax.dot_general(both, top, NT_DIMS, preferred_element_type=jnp.float32)
+
+    cross = acc[span:, :]
+    gram = acc[:span, :] + (cross + cross.T)
+    low = gram[rank_rows:, rank_rows:]
+    low = jnp.concatenate([low[: rank_rows // 2], low[rank_rows // 2 :]], axis=1)
+    packed = jnp.concatenate([gram[:rank_rows], low], axis=0)
+    for ref in before:
+        packed += ref[...]
+    gram_ref[...] = packed
 
 
 def spectra_and_gram(blocks, row_weight, table, first_row, *before):
     sources, groups, rows, rank_rows, points = blocks.shape
-    _, half_lons, cols = table.shape
+    tiles, _, half_lons, _ = table.shape
+    cols = tiles * COL_TILE
     span = groups * rank_rows
     packed = (rank_rows + rank_rows // 2, span)
     return pl.pallas_call(
         functools.partial(spectra_kernel, first_row=first_row),
-        grid=(cols // COL_TILE,),
         in_specs=[
             pl.BlockSpec(memory_space=pltpu.SMEM),
-            pl.BlockSpec(blocks.shape, lambda i: (0, 0, 0, 0, 0)),
-            pl.BlockSpec((2, half_lons, COL_TILE), lambda i: (0, 0, i)),
-            *[pl.BlockSpec(packed, lambda i: (0, 0)) for _ in before],
-        ],
-        out_specs=[
-            pl.BlockSpec((rows, 2 * span, COL_TILE), lambda i: (0, 0, i)),
-            pl.BlockSpec(packed, lambda i: (0, 0)),
-        ],
+            pl.BlockSpec(memory_space=pltpu.VMEM),
+            pl.BlockSpec(memory_space=pl.ANY),
+            *[pl.BlockSpec(memory_space=pltpu.VMEM) for _ in before],
+        ],
+        out_specs=[pl.BlockSpec(memory_space=pltpu.VMEM)] * 2,
         out_shape=[
             jax.ShapeDtypeStruct((rows, 2 * span, cols), jnp.bfloat16),
             jax.ShapeDtypeStruct(packed, jnp.float32),
@@ -221,6 +224,8 @@
         scratch_shapes=[
             pltpu.VMEM((2 * rows * span, half_lons), jnp.bfloat16),
             pltpu.VMEM((2 * span, span), jnp.float32),
+            pltpu.VMEM(table.shape, table.dtype),
+            pltpu.SemaphoreType.DMA((tiles,)),
         ],
         compiler_params=pltpu.CompilerParams(vmem_limit_bytes=VMEM_BYTES),
         cost_estimate=pl.CostEstimate(
@@ -348,7 +353,7 @@
             pltpu.VMEM((rows, height, cols), jnp.bfloat16),
             pltpu.SemaphoreType.DMA((2,)),
         ],
-        compiler_params=pltpu.CompilerParams(vmem_limit_bytes=MERGE_VMEM_BYTES),
+        compiler_params=pltpu.CompilerParams(vmem_limit_bytes=VMEM_BYTES),
     )(*gram_parts, test_matrix.T, early, late)
 
 

time: 153 us -> 150 us (0.980)
  local copies, waits for them, and re-layouts: 2.24 us -> 0.01 us
  Pallas kernels: 40.9 us -> 38.8 us
    unnamed x10 -> x2, local copies, waits for them, and re-layouts: 2.24 us -> 0.01 us
  transfers between devices with their start and end apart: 9 -> 9, of which waited for: 8 -> 8; matrix products, arithmetic and copies ran while one was open for 16% -> 16% of each run, Pallas kernels for 11% -> 10%
where the time goes in v5:
time: 150 us
  waiting for transfers between devices  66.7 us (44%)
  Pallas kernels  38.8 us (26%)
  other arithmetic  24.6 us (16%)
  starting transfers between devices  19.5 us (13%)
    all_to_all x2, waiting for transfers between devices, local_pair(): lax.all_to_all(part, ('lon', 'tm'), split_axis=0, concat_axis=0, tiled=True)  57.6 us
    pallas_call x2, Pallas kernels, spectra_and_gram(): pl.pallas_call(functools.partial(spectra_kernel, first_row=first_row), in...  23 us
    convert_element_type x1, other arithmetic, split_table(): high.astype(jnp.bfloat16)  21.7 us
    all_to_all x2, starting transfers between devices, local_pair(): lax.all_to_all(part, ('lon', 'tm'), split_axis=0, concat_axis=0, tiled=True)  11.4 us
    pallas_call x1, Pallas kernels, merge_and_mix(): pl.pallas_call(functools.partial(merge_kernel, split=split), grid=(rows,)...  9.72 us
    ppermute x7, waiting for transfers between devices, exchanged(): lax.ppermute(array, axes, [(i, i ^ mask) for i in range(count)])  9.16 us
    ppermute x7, starting transfers between devices, exchanged(): lax.ppermute(array, axes, [(i, i ^ mask) for i in range(count)])  8.07 us
    pallas_call x1, Pallas kernels, relayout(): pl.pallas_call(relayout_kernel, grid=(rank_rows // some,), in_specs=[pl.B...  6.06 us
  transfers between devices with their start and end apart: 9, of which 8 were waited for; matrix products, arithmetic and copies ran while one was open for 16% of the time, Pallas kernels for 10%

profile of v5, /device:TPU:0, one launch (start us, length us, event | category | flops | bytes accessed | tf_op | source)
XLA Modules:
  0.0 149.7 jit_solution(15182237817838732011)
XLA Ops:
  0.0 6.1 %shard_map.28 = (bf16[32,6,64,128]{3,2,1,0:T(8,128)(2,1)}, bf16[32,2,64,128]{3,2,1,0:T(8,128)(2,1)}) custom-call(bf16[128,64,256]{2,1,0:T(8,128)(2,1)} %x_ref.1), custom_call_target="tpu_custom_call" | custom-call | tf_op jit(solution)/shard_map/pallas_call | solution.py:138
  6.1 7.3 %all-to-all-start.1 = ((bf16[32,6,64,128]{3,2,1,0:T(8,128)(2,1)}), bf16[32,6,64,128]{3,2,1,0:T(8,128)(2,1)S(1)}, u32[]{:S(2)}, u32[]{:S(2)}) async-start(bf16[32,6,64,128]{3,2,1,0:T(8,128)(2,1)} %get-tuple-element.16), calls=%async_computation.1 | async-start | bytes 6291456 | tf_op jit(solution)/shard_map/all_to_all | solution.py:390
  13.4 21.7 %reduce-precision_convert_fusion = (bf16[5,1,1024,256]{3,2,1,0:T(8,128)(2,1)S(1)}, bf16[5,1,1024,256]{3,2,1,0:T(8,128)(2,1)S(1)}) fusion(f32[5,256]{1,0:T(8,128)S(1)} %rsqrt_multiply_fusion, s32[5,256]{1,0:T(8,128)S(1)} %add_select_fusion.1, pred[5,256]{1,0:T(8,128)(4,1)S(1)} %fusion.7), kind=kLoop, calls=%fused_computation.4 | loop fusion | flops 26214400 | bytes 5254400 | tf_op jit(solution)/shard_map/convert_element_type | solution.py:121
  35.2 2.8 %pad_maximum_fusion.refs_2_ = bf16[5,2,1024,256]{3,2,1,0:T(8,128)(2,1)} fusion(bf16[5,1,1024,256]{3,2,1,0:T(8,128)(2,1)S(1)} %get-tuple-element.22, bf16[5,1,1024,256]{3,2,1,0:T(8,128)(2,1)S(1)} %get-tuple-element.21), kind=kLoop, calls=%fused_computation.9 | loop fusion | flops 2621440 | bytes 10485760 | tf_op jit(solution)/shard_map/stack | solution.py:121
  37.9 46.7 %all-to-all-done.1 = bf16[32,6,64,128]{3,2,1,0:T(8,128)(2,1)S(1)} async-done(((bf16[32,6,64,128]{3,2,1,0:T(8,128)(2,1)}), bf16[32,6,64,128]{3,2,1,0:T(8,128)(2,1)S(1)}, u32[]{:S(2)}, u32[]{:S(2)}) %all-to-all-start.1) | async-done | bytes 3145760 | tf_op jit(solution)/shard_map/all_to_all | solution.py:390
  84.6 4.1 %all-to-all-start = ((bf16[32,2,64,128]{3,2,1,0:T(8,128)(2,1)}), bf16[32,2,64,128]{3,2,1,0:T(8,128)(2,1)}, u32[]{:S(2)}, u32[]{:S(2)}) async-start(bf16[32,2,64,128]{3,2,1,0:T(8,128)(2,1)} %get-tuple-element.14), calls=%async_computation | async-start | bytes 2097152 | tf_op jit(solution)/shard_map/all_to_all | solution.py:390
  88.8 15.2 %shard_map.29 = (bf16[6,256,1280]{2,1,0:T(8,128)(2,1)}, f32[96,128]{1,0:T(8,128)S(1)}) custom-call(f32[1,8]{1,0:T(1,128)S(1)} %sine_sqrt_fusion.refs_0_, bf16[16,2,6,64,128]{4,3,2,1,0:T(8,128)(2,1)S(1)} %bitcast.3, bf16[5,2,1024,256]{3,2,1,0:T(8,128)(2,1)} %pad_maximum_fusion.refs_2_), custom_call_target="tpu_custom_call" | custom-call | flops 8053063680 | bytes 12320768 | tf_op jit(solution)/shard_map/pallas_call | solution.py:211
  104.1 0.0 copy-start
  104.1 10.9 %all-to-all-done = bf16[32,2,64,128]{3,2,1,0:T(8,128)(2,1)} async-done(((bf16[32,2,64,128]{3,2,1,0:T(8,128)(2,1)}), bf16[32,2,64,128]{3,2,1,0:T(8,128)(2,1)}, u32[]{:S(2)}, u32[]{:S(2)}) %all-to-all-start) | async-done | bytes 1048608 | tf_op jit(solution)/shard_map/all_to_all | solution.py:390
  115.0 7.7 %shard_map.30 = (bf16[2,256,1280]{2,1,0:T(8,128)(2,1)S(1)}, f32[96,128]{1,0:T(8,128)S(1)}) custom-call(f32[1,8]{1,0:T(1,128)S(1)} %sine_sqrt_fusion.refs_0_, bf16[16,2,2,64,128]{4,3,2,1,0:T(8,128)(2,1)} %bitcast.refs_1_, bf16[5,2,1024,256]{3,2,1,0:T(8,128)(2,1)} %pad_maximum_fusion.refs_2_, f32[96,128]{1,0:T(8,128)S(1)} %get-tuple-element.17.refs_3_), custom_call_target="tpu_custom_call" | custom-call | flops 2684354560 | bytes 7602176 | tf_op jit(solution)/shard_map/pallas_call | solution.py:211
  122.7 0.1 collective-permute-start
  122.8 1.2 collective-permute-done
  124.0 1.5 %collective-permute-start.1 = (f32[96,128]{1,0:T(8,128)S(1)}, f32[96,128]{1,0:T(8,128)S(1)}, u32[]{:S(2)}, u32[]{:S(2)}) collective-permute-start(f32[96,128]{1,0:T(8,128)S(1)} %add.104), channel_id=1, source_target_pairs={{0,2},{1,3},{2,0},{3,1},{4,6},{5,7},{6,4},{7,5},{8,10},{9,11},{10,... | collective-permute-start | bytes 147464 | tf_op jit(solution)/shard_map/ppermute | solution.py:366
  125.5 1.5 collective-permute-start.2
  127.0 0.5 collective-permute-start.3
  127.5 0.6 collective-permute-done.1
  128.1 2.0 %collective-permute-done.2 = f32[96,128]{1,0:T(8,128)S(1)} collective-permute-done((f32[96,128]{1,0:T(8,128)S(1)}, f32[96,128]{1,0:T(8,128)S(1)}, u32[]{:S(2)}, u32[]{:S(2)}) %collective-permute-start.2) | collective-permute-done | bytes 49184 | tf_op jit(solution)/shard_map/ppermute | solution.py:366
  130.1 1.9 %collective-permute-done.3 = f32[96,128]{1,0:T(8,128)S(1)} collective-permute-done((f32[96,128]{1,0:T(8,128)S(1)}, f32[96,128]{1,0:T(8,128)S(1)}, u32[]{:S(2)}, u32[]{:S(2)}) %collective-permute-start.3) | collective-permute-done | bytes 49184 | tf_op jit(solution)/shard_map/ppermute | solution.py:366
  132.0 0.1 collective-permute-start.4
  132.1 2.0 %collective-permute-start.5 = (f32[96,128]{1,0:T(8,128)S(1)}, f32[96,128]{1,0:T(8,128)S(1)}, u32[]{:S(2)}, u32[]{:S(2)}) collective-permute-start(f32[96,128]{1,0:T(8,128)S(1)} %add_add_fusion.refs_0_), channel_id=1, source_target_pairs={{0,8},{1,9},{2,10},{3,11},{4,12},{5,13},{6,14},{7,15},{8,0},{9,1},... | collective-permute-start | bytes 147464 | tf_op jit(solution)/shard_map/ppermute | solution.py:366
  134.1 2.4 %collective-permute-start.6 = (f32[96,128]{1,0:T(8,128)S(1)}, f32[96,128]{1,0:T(8,128)S(1)}, u32[]{:S(2)}, u32[]{:S(2)}) collective-permute-start(f32[96,128]{1,0:T(8,128)S(1)} %add_add_fusion.refs_0_), channel_id=1, source_target_pairs={{0,12},{1,13},{2,14},{3,15},{4,8},{5,9},{6,10},{7,11},{8,4},{9,5},... | collective-permute-start | bytes 147464 | tf_op jit(solution)/shard_map/ppermute | solution.py:366
  136.5 0.0 collective-permute-done.4.refs_1_
  136.5 0.9 collective-permute-done.5.refs_2_
  137.4 2.6 %collective-permute-done.6.refs_3_ = f32[96,128]{1,0:T(8,128)S(1)} collective-permute-done((f32[96,128]{1,0:T(8,128)S(1)}, f32[96,128]{1,0:T(8,128)S(1)}, u32[]{:S(2)}, u32[]{:S(2)}) %collective-permute-start.6) | collective-permute-done | bytes 49184 | tf_op jit(solution)/shard_map/ppermute | solution.py:366
  140.0 0.0 copy-done
  140.0 9.7 %shard_map.31 = f32[64,10240]{1,0:T(8,128)} custom-call(f32[96,128]{1,0:T(8,128)S(1)} %add_add_fusion.refs_0_, f32[96,128]{1,0:T(8,128)S(1)} %collective-permute-done.4.refs_1_, f32[96,128]{1,0:T(8,128)S(1)} %collective-permute-done.5.refs_2_, f32[96,128]{1,0:T(8,128)S(1)} %collective-permute-done.6.refs_3_, f32[64,128]{1,0:T(8,128)S(1)} %bitcast.4, ...), custom_call_target="tpu_custom_call" | custom-call | tf_op jit(solution)/shard_map/pallas_call | solution.py:338
  (6 shorter events, 0.1 us)
Async XLA Ops:
  6.1 78.5 %all-to-all-start.1 = ((bf16[32,6,64,128]{3,2,1,0:T(8,128)(2,1)}), bf16[32,6,64,128]{3,2,1,0:T(8,128)(2,1)S(1)}, u32[]{:S(2)}, u32[]{:S(2)}) async-start(bf16[32,6,64,128]{3,2,1,0:T(8,128)(2,1)} %get-tuple-element.16), calls=%async_computation.1 | async-start | bytes 6291456 | tf_op jit(solution)/shard_map/all_to_all | solution.py:390
  84.6 30.4 %all-to-all-start = ((bf16[32,2,64,128]{3,2,1,0:T(8,128)(2,1)}), bf16[32,2,64,128]{3,2,1,0:T(8,128)(2,1)}, u32[]{:S(2)}, u32[]{:S(2)}) async-start(bf16[32,2,64,128]{3,2,1,0:T(8,128)(2,1)} %get-tuple-element.14), calls=%async_computation | async-start | bytes 2097152 | tf_op jit(solution)/shard_map/all_to_all | solution.py:390
  104.1 35.9 %copy-start = (f32[128,64]{0,1:T(8,128)S(1)}, f32[128,64]{0,1:T(8,128)}, u32[]{:S(2)}) copy-start(f32[128,64]{0,1:T(8,128)} %param.3) | copy-start | bytes 98308
  122.7 1.3 collective-permute-start
  124.0 4.2 %collective-permute-start.1 = (f32[96,128]{1,0:T(8,128)S(1)}, f32[96,128]{1,0:T(8,128)S(1)}, u32[]{:S(2)}, u32[]{:S(2)}) collective-permute-start(f32[96,128]{1,0:T(8,128)S(1)} %add.104), channel_id=1, source_target_pairs={{0,2},{1,3},{2,0},{3,1},{4,6},{5,7},{6,4},{7,5},{8,10},{9,11},{10,... | collective-permute-start | bytes 147464 | tf_op jit(solution)/shard_map/ppermute | solution.py:366
  125.5 4.6 %collective-permute-start.2 = (f32[96,128]{1,0:T(8,128)S(1)}, f32[96,128]{1,0:T(8,128)S(1)}, u32[]{:S(2)}, u32[]{:S(2)}) collective-permute-start(f32[96,128]{1,0:T(8,128)S(1)} %add.104), channel_id=1, source_target_pairs={{0,16},{1,17},{2,18},{3,19},{4,20},{5,21},{6,22},{7,23},{8,24},{9,... | collective-permute-start | bytes 147464 | tf_op jit(solution)/shard_map/ppermute | solution.py:366
  127.0 5.0 %collective-permute-start.3 = (f32[96,128]{1,0:T(8,128)S(1)}, f32[96,128]{1,0:T(8,128)S(1)}, u32[]{:S(2)}, u32[]{:S(2)}) collective-permute-start(f32[96,128]{1,0:T(8,128)S(1)} %add.104), channel_id=1, source_target_pairs={{0,18},{1,19},{2,16},{3,17},{4,22},{5,23},{6,20},{7,21},{8,26},{9,... | collective-permute-start | bytes 147464 | tf_op jit(solution)/shard_map/ppermute | solution.py:366
  132.0 4.5 %collective-permute-start.4 = (f32[96,128]{1,0:T(8,128)S(1)}, f32[96,128]{1,0:T(8,128)S(1)}, u32[]{:S(2)}, u32[]{:S(2)}) collective-permute-start(f32[96,128]{1,0:T(8,128)S(1)} %add_add_fusion.refs_0_), channel_id=1, source_target_pairs={{0,4},{1,5},{2,6},{3,7},{4,0},{5,1},{6,2},{7,3},{8,12},{9,13},{10,... | collective-permute-start | bytes 147464 | tf_op jit(solution)/shard_map/ppermute | solution.py:366
  132.1 5.3 %collective-permute-start.5 = (f32[96,128]{1,0:T(8,128)S(1)}, f32[96,128]{1,0:T(8,128)S(1)}, u32[]{:S(2)}, u32[]{:S(2)}) collective-permute-start(f32[96,128]{1,0:T(8,128)S(1)} %add_add_fusion.refs_0_), channel_id=1, source_target_pairs={{0,8},{1,9},{2,10},{3,11},{4,12},{5,13},{6,14},{7,15},{8,0},{9,1},... | collective-permute-start | bytes 147464 | tf_op jit(solution)/shard_map/ppermute | solution.py:366
  134.1 5.9 %collective-permute-start.6 = (f32[96,128]{1,0:T(8,128)S(1)}, f32[96,128]{1,0:T(8,128)S(1)}, u32[]{:S(2)}, u32[]{:S(2)}) collective-permute-start(f32[96,128]{1,0:T(8,128)S(1)} %add_add_fusion.refs_0_), channel_id=1, source_target_pairs={{0,12},{1,13},{2,14},{3,15},{4,8},{5,9},{6,10},{7,11},{8,4},{9,5},... | collective-permute-start | bytes 147464 | tf_op jit(solution)/shard_map/ppermute | solution.py:366

commit v6 on v5

--- a/solution.py
+++ b/solution.py
@@ -121,6 +121,32 @@
     return jnp.stack([high.astype(jnp.bfloat16), (table - high).astype(jnp.bfloat16)], axis=1)
 
 
+def ids(shape):
+    return lax.broadcasted_iota(jnp.int32, shape, 0), lax.broadcasted_iota(jnp.int32, shape, 1)
+
+
+def packed_gram(gram):
+    rank = gram.shape[0] // 2
+    high, cross, low = gram[:rank, :rank], gram[:rank, rank:], gram[rank:, rank:]
+    row_ids, col_ids = ids(high.shape)
+    both = jnp.where(col_ids >= row_ids, high, low)
+    diagonal = jnp.sum(jnp.where(col_ids == row_ids, low, 0.0), axis=0, keepdims=True)
+    diagonal = jnp.broadcast_to(jnp.concatenate([diagonal, diagonal], axis=1), (8, 2 * rank))
+    return jnp.concatenate([jnp.concatenate([both, cross], axis=1), diagonal], axis=0)
+
+
+def unpacked_gram(packed):
+    rank = packed.shape[1] // 2
+    both, cross, diagonal = packed[:rank, :rank], packed[:rank, rank:], packed[rank : rank + 1, :rank]
+    row_ids, col_ids = ids(both.shape)
+    turned = both.T
+    high = jnp.where(col_ids >= row_ids, both, turned)
+    low = jnp.where(col_ids < row_ids, both, turned)
+    low = jnp.where(col_ids == row_ids, jnp.broadcast_to(diagonal, low.shape), low)
+    top = jnp.concatenate([high, cross], axis=1)
+    return jnp.concatenate([top, jnp.concatenate([cross.T, low], axis=1)], axis=0)
+
+
 def relayout_kernel(x_ref, first_ref, last_ref):
     points, some, total = x_ref.shape
     devices, split = first_ref.shape[:2]
@@ -148,7 +174,7 @@
 
 
 def spectra_kernel(*refs, first_row):
-    weight_ref, x_ref, table_ref, *before, modes_ref, gram_ref, lhs, acc, held, sems = refs
+    weight_ref, x_ref, table_ref, *before, modes_ref, gram_ref, lhs, acc, held, sems, own, own_sems = refs
     sources, groups, rows, rank_rows, points = x_ref.shape
     tiles = table_ref.shape[0]
     span = groups * rank_rows
@@ -156,15 +182,24 @@
     def fetch(step):
         return pltpu.make_async_copy(table_ref.at[step], held.at[step], sems.at[step])
 
-    for step in range(tiles):
-        fetch(step).start()
+    takes = []
+    for half in range(2):
+        part = pl.ds(half * sources // 2, sources // 2)
+        takes.append(pltpu.make_async_copy(x_ref.at[part], own.at[part], own_sems.at[half]))
+    for take in takes:
+        take.start()
+    fetch(0).start()
     acc[...] = jnp.zeros_like(acc)
     for src in range(sources):
         half, place = divmod(src, sources // 2)
+        if place == 0:
+            takes[half].wait()
+            for step in range(1 + half, tiles, 2):
+                fetch(step).start()
         for row in range(rows):
             for grp in range(groups):
                 start = ((half * rows + row) * groups + grp) * rank_rows
-                lhs[start : start + rank_rows, place * points : (place + 1) * points] = x_ref[
+                lhs[start : start + rank_rows, place * points : (place + 1) * points] = own[
                     src, grp, row
                 ]
 
@@ -194,9 +229,7 @@
 
     cross = acc[span:, :]
     gram = acc[:span, :] + (cross + cross.T)
-    low = gram[rank_rows:, rank_rows:]
-    low = jnp.concatenate([low[: rank_rows // 2], low[rank_rows // 2 :]], axis=1)
-    packed = jnp.concatenate([gram[:rank_rows], low], axis=0)
+    packed = packed_gram(gram)
     for ref in before:
         packed += ref[...]
     gram_ref[...] = packed
@@ -207,12 +240,12 @@
     tiles, _, half_lons, _ = table.shape
     cols = tiles * COL_TILE
     span = groups * rank_rows
-    packed = (rank_rows + rank_rows // 2, span)
+    packed = (rank_rows + 8, span)
     return pl.pallas_call(
         functools.partial(spectra_kernel, first_row=first_row),
         in_specs=[
             pl.BlockSpec(memory_space=pltpu.SMEM),
-            pl.BlockSpec(memory_space=pltpu.VMEM),
+            pl.BlockSpec(memory_space=pl.ANY),
             pl.BlockSpec(memory_space=pl.ANY),
             *[pl.BlockSpec(memory_space=pltpu.VMEM) for _ in before],
         ],
@@ -226,6 +259,8 @@
             pltpu.VMEM((2 * span, span), jnp.float32),
             pltpu.VMEM(table.shape, table.dtype),
             pltpu.SemaphoreType.DMA((tiles,)),
+            pltpu.VMEM(blocks.shape, blocks.dtype),
+            pltpu.SemaphoreType.DMA((2,)),
         ],
         compiler_params=pltpu.CompilerParams(vmem_limit_bytes=VMEM_BYTES),
         cost_estimate=pl.CostEstimate(
@@ -274,18 +309,6 @@
     return parts[0]
 
 
-def unpacked(packed):
-    span = packed.shape[1]
-    rank = span // 2
-    low = jnp.concatenate([packed[rank:, :rank], packed[rank:, rank:]], axis=0)
-    square = jnp.concatenate(
-        [packed[:rank], jnp.concatenate([jnp.zeros_like(low), low], axis=1)], axis=0
-    )
-    row_ids = lax.broadcasted_iota(jnp.int32, square.shape, 0)
-    col_ids = lax.broadcasted_iota(jnp.int32, square.shape, 1)
-    return jnp.where((row_ids >= rank) & (col_ids < rank), square.T, square)
-
-
 def merge_kernel(*refs, split):
     *part_refs, test_ref, early_ref, late_ref, out_ref, mix_ref, first_ref, second_ref, held, sems = refs
     rank = test_ref.shape[0]
@@ -299,7 +322,7 @@
     def _():
         for fetch in fetches:
             fetch.start()
-        gram = unpacked(add_up([part[...] for part in part_refs]))
+        gram = unpacked_gram(add_up([part[...] for part in part_refs]))
         test_t = test_ref[...]
         sketch = dot_full(gram, test_t, NT_DIMS)
         sketch_t = dot_full(test_t, gram)
@@ -314,8 +337,7 @@
         inner = 0.5 * (inner + inner.T)
         eliminate(jnp.concatenate([inner, pad], axis=1), rank, second_ref)
         upper = second_ref[:, :rank]
-        col_ids = lax.broadcasted_iota(jnp.int32, upper.shape, 1)
-        row_ids = lax.broadcasted_iota(jnp.int32, upper.shape, 0)
+        row_ids, col_ids = ids(upper.shape)
         mixing = dot_full(jnp.where(col_ids >= row_ids, upper, 0.0), unmixed)
         top = mixing.astype(jnp.bfloat16)
         rest = (mixing - top.astype(jnp.float32)).astype(jnp.bfloat16)

time: 150 us -> 149 us (level)
  no operation moved by 1% of the time
where the time goes in v6:
time: 149 us
  waiting for transfers between devices  66.2 us (44%)
  Pallas kernels  38.7 us (26%)
  other arithmetic  24.6 us (17%)
  starting transfers between devices  19.5 us (13%)
    all_to_all x2, waiting for transfers between devices, local_pair(): lax.all_to_all(part, ('lon', 'tm'), split_axis=0, concat_axis=0, tiled=True)  57.3 us
    pallas_call x2, Pallas kernels, spectra_and_gram(): pl.pallas_call(functools.partial(spectra_kernel, first_row=first_row), in...  22.9 us
    convert_element_type x1, other arithmetic, split_table(): high.astype(jnp.bfloat16)  21.7 us
    all_to_all x2, starting transfers between devices, local_pair(): lax.all_to_all(part, ('lon', 'tm'), split_axis=0, concat_axis=0, tiled=True)  11.4 us
    pallas_call x1, Pallas kernels, merge_and_mix(): pl.pallas_call(functools.partial(merge_kernel, split=split), grid=(rows,)...  9.72 us
    ppermute x7, waiting for transfers between devices, exchanged(): lax.ppermute(array, axes, [(i, i ^ mask) for i in range(count)])  8.88 us
    ppermute x7, starting transfers between devices, exchanged(): lax.ppermute(array, axes, [(i, i ^ mask) for i in range(count)])  8.02 us
    pallas_call x1, Pallas kernels, relayout(): pl.pallas_call(relayout_kernel, grid=(rank_rows // some,), in_specs=[pl.B...  6.06 us
  transfers between devices with their start and end apart: 9, of which 8 were waited for; matrix products, arithmetic and copies ran while one was open for 16% of the time, Pallas kernels for 10%

profile of v6, /device:TPU:0, one launch (start us, length us, event | category | flops | bytes accessed | tf_op | source)
XLA Modules:
  0.0 149.1 jit_solution(1996270201599036902)
XLA Ops:
  0.0 6.1 %shard_map.28 = (bf16[32,6,64,128]{3,2,1,0:T(8,128)(2,1)}, bf16[32,2,64,128]{3,2,1,0:T(8,128)(2,1)}) custom-call(bf16[128,64,256]{2,1,0:T(8,128)(2,1)} %x_ref.1), custom_call_target="tpu_custom_call" | custom-call | tf_op jit(solution)/shard_map/pallas_call | solution.py:164
  6.1 7.3 %all-to-all-start.1 = ((bf16[32,6,64,128]{3,2,1,0:T(8,128)(2,1)}), bf16[32,6,64,128]{3,2,1,0:T(8,128)(2,1)S(1)}, u32[]{:S(2)}, u32[]{:S(2)}) async-start(bf16[32,6,64,128]{3,2,1,0:T(8,128)(2,1)} %get-tuple-element.16), calls=%async_computation.1 | async-start | bytes 6291456 | tf_op jit(solution)/shard_map/all_to_all | solution.py:412
  13.4 21.7 %reduce-precision_convert_fusion = (bf16[5,1,1024,256]{3,2,1,0:T(8,128)(2,1)S(1)}, bf16[5,1,1024,256]{3,2,1,0:T(8,128)(2,1)S(1)}) fusion(f32[5,256]{1,0:T(8,128)S(1)} %rsqrt_multiply_fusion, s32[5,256]{1,0:T(8,128)S(1)} %add_select_fusion.1, pred[5,256]{1,0:T(8,128)(4,1)S(1)} %fusion.7), kind=kLoop, calls=%fused_computation.4 | loop fusion | flops 26214400 | bytes 5254400 | tf_op jit(solution)/shard_map/convert_element_type | solution.py:121
  35.2 2.8 %pad_maximum_fusion.refs_2_ = bf16[5,2,1024,256]{3,2,1,0:T(8,128)(2,1)} fusion(bf16[5,1,1024,256]{3,2,1,0:T(8,128)(2,1)S(1)} %get-tuple-element.22, bf16[5,1,1024,256]{3,2,1,0:T(8,128)(2,1)S(1)} %get-tuple-element.21), kind=kLoop, calls=%fused_computation.9 | loop fusion | flops 2621440 | bytes 10485760 | tf_op jit(solution)/shard_map/stack | solution.py:121
  37.9 46.7 %all-to-all-done.1 = bf16[32,6,64,128]{3,2,1,0:T(8,128)(2,1)S(1)} async-done(((bf16[32,6,64,128]{3,2,1,0:T(8,128)(2,1)}), bf16[32,6,64,128]{3,2,1,0:T(8,128)(2,1)S(1)}, u32[]{:S(2)}, u32[]{:S(2)}) %all-to-all-start.1) | async-done | bytes 3145760 | tf_op jit(solution)/shard_map/all_to_all | solution.py:412
  84.6 4.1 %all-to-all-start = ((bf16[32,2,64,128]{3,2,1,0:T(8,128)(2,1)}), bf16[32,2,64,128]{3,2,1,0:T(8,128)(2,1)}, u32[]{:S(2)}, u32[]{:S(2)}) async-start(bf16[32,2,64,128]{3,2,1,0:T(8,128)(2,1)} %get-tuple-element.14), calls=%async_computation | async-start | bytes 2097152 | tf_op jit(solution)/shard_map/all_to_all | solution.py:412
  88.8 15.5 %shard_map.29 = (bf16[6,256,1280]{2,1,0:T(8,128)(2,1)}, f32[72,128]{1,0:T(8,128)S(1)}) custom-call(f32[1,8]{1,0:T(1,128)S(1)} %sine_sqrt_fusion.refs_0_, bf16[16,2,6,64,128]{4,3,2,1,0:T(8,128)(2,1)S(1)} %bitcast.3, bf16[5,2,1024,256]{3,2,1,0:T(8,128)(2,1)} %pad_maximum_fusion.refs_2_), custom_call_target="tpu_custom_call" | custom-call | flops 8053063680 | bytes 12320768 | tf_op jit(solution)/shard_map/pallas_call | solution.py:244
  104.3 0.0 copy-start
  104.3 10.7 %all-to-all-done = bf16[32,2,64,128]{3,2,1,0:T(8,128)(2,1)} async-done(((bf16[32,2,64,128]{3,2,1,0:T(8,128)(2,1)}), bf16[32,2,64,128]{3,2,1,0:T(8,128)(2,1)}, u32[]{:S(2)}, u32[]{:S(2)}) %all-to-all-start) | async-done | bytes 1048608 | tf_op jit(solution)/shard_map/all_to_all | solution.py:412
  115.0 7.5 %shard_map.30 = (bf16[2,256,1280]{2,1,0:T(8,128)(2,1)S(1)}, f32[72,128]{1,0:T(8,128)S(1)}) custom-call(f32[1,8]{1,0:T(1,128)S(1)} %sine_sqrt_fusion.refs_0_, bf16[16,2,2,64,128]{4,3,2,1,0:T(8,128)(2,1)} %bitcast.refs_1_, bf16[5,2,1024,256]{3,2,1,0:T(8,128)(2,1)} %pad_maximum_fusion.refs_2_, f32[72,128]{1,0:T(8,128)S(1)} %get-tuple-element.17.refs_3_), custom_call_target="tpu_custom_call" | custom-call | flops 2684354560 | bytes 7602176 | tf_op jit(solution)/shard_map/pallas_call | solution.py:244
  122.4 0.1 collective-permute-start
  122.5 1.2 collective-permute-done
  123.7 1.5 collective-permute-start.1
  125.2 1.5 collective-permute-start.2
  126.7 0.5 collective-permute-start.3
  127.2 0.5 collective-permute-done.1
  127.7 1.8 %collective-permute-done.2 = f32[72,128]{1,0:T(8,128)S(1)} collective-permute-done((f32[72,128]{1,0:T(8,128)S(1)}, f32[72,128]{1,0:T(8,128)S(1)}, u32[]{:S(2)}, u32[]{:S(2)}) %collective-permute-start.2) | collective-permute-done | bytes 36896 | tf_op jit(solution)/shard_map/ppermute | solution.py:388
  129.5 2.1 %collective-permute-done.3 = f32[72,128]{1,0:T(8,128)S(1)} collective-permute-done((f32[72,128]{1,0:T(8,128)S(1)}, f32[72,128]{1,0:T(8,128)S(1)}, u32[]{:S(2)}, u32[]{:S(2)}) %collective-permute-start.3) | collective-permute-done | bytes 36896 | tf_op jit(solution)/shard_map/ppermute | solution.py:388
  131.5 0.1 collective-permute-start.4
  131.6 2.0 %collective-permute-start.5 = (f32[72,128]{1,0:T(8,128)S(1)}, f32[72,128]{1,0:T(8,128)S(1)}, u32[]{:S(2)}, u32[]{:S(2)}) collective-permute-start(f32[72,128]{1,0:T(8,128)S(1)} %add_add_fusion.refs_0_), channel_id=1, source_target_pairs={{0,8},{1,9},{2,10},{3,11},{4,12},{5,13},{6,14},{7,15},{8,0},{9,1},... | collective-permute-start | bytes 110600 | tf_op jit(solution)/shard_map/ppermute | solution.py:388
  133.6 2.4 %collective-permute-start.6 = (f32[72,128]{1,0:T(8,128)S(1)}, f32[72,128]{1,0:T(8,128)S(1)}, u32[]{:S(2)}, u32[]{:S(2)}) collective-permute-start(f32[72,128]{1,0:T(8,128)S(1)} %add_add_fusion.refs_0_), channel_id=1, source_target_pairs={{0,12},{1,13},{2,14},{3,15},{4,8},{5,9},{6,10},{7,11},{8,4},{9,5},... | collective-permute-start | bytes 110600 | tf_op jit(solution)/shard_map/ppermute | solution.py:388
  136.0 0.0 collective-permute-done.4.refs_1_
  136.0 0.7 collective-permute-done.5.refs_2_
  136.7 2.7 %collective-permute-done.6.refs_3_ = f32[72,128]{1,0:T(8,128)S(1)} collective-permute-done((f32[72,128]{1,0:T(8,128)S(1)}, f32[72,128]{1,0:T(8,128)S(1)}, u32[]{:S(2)}, u32[]{:S(2)}) %collective-permute-start.6) | collective-permute-done | bytes 36896 | tf_op jit(solution)/shard_map/ppermute | solution.py:388
  139.3 0.0 copy-done
  139.4 9.7 %shard_map.31 = f32[64,10240]{1,0:T(8,128)} custom-call(f32[72,128]{1,0:T(8,128)S(1)} %add_add_fusion.refs_0_, f32[72,128]{1,0:T(8,128)S(1)} %collective-permute-done.4.refs_1_, f32[72,128]{1,0:T(8,128)S(1)} %collective-permute-done.5.refs_2_, f32[72,128]{1,0:T(8,128)S(1)} %collective-permute-done.6.refs_3_, f32[64,128]{1,0:T(8,128)S(1)} %bitcast.4, ...), custom_call_target="tpu_custom_call" | custom-call | tf_op jit(solution)/shard_map/pallas_call | solution.py:360
  (6 shorter events, 0.1 us)
Async XLA Ops:
  6.1 78.5 %all-to-all-start.1 = ((bf16[32,6,64,128]{3,2,1,0:T(8,128)(2,1)}), bf16[32,6,64,128]{3,2,1,0:T(8,128)(2,1)S(1)}, u32[]{:S(2)}, u32[]{:S(2)}) async-start(bf16[32,6,64,128]{3,2,1,0:T(8,128)(2,1)} %get-tuple-element.16), calls=%async_computation.1 | async-start | bytes 6291456 | tf_op jit(solution)/shard_map/all_to_all | solution.py:412
  84.6 30.4 %all-to-all-start = ((bf16[32,2,64,128]{3,2,1,0:T(8,128)(2,1)}), bf16[32,2,64,128]{3,2,1,0:T(8,128)(2,1)}, u32[]{:S(2)}, u32[]{:S(2)}) async-start(bf16[32,2,64,128]{3,2,1,0:T(8,128)(2,1)} %get-tuple-element.14), calls=%async_computation | async-start | bytes 2097152 | tf_op jit(solution)/shard_map/all_to_all | solution.py:412
  104.3 35.1 %copy-start = (f32[128,64]{0,1:T(8,128)S(1)}, f32[128,64]{0,1:T(8,128)}, u32[]{:S(2)}) copy-start(f32[128,64]{0,1:T(8,128)} %param.3) | copy-start | bytes 98308
  122.4 1.3 collective-permute-start
  123.7 4.0 %collective-permute-start.1 = (f32[72,128]{1,0:T(8,128)S(1)}, f32[72,128]{1,0:T(8,128)S(1)}, u32[]{:S(2)}, u32[]{:S(2)}) collective-permute-start(f32[72,128]{1,0:T(8,128)S(1)} %add.104), channel_id=1, source_target_pairs={{0,2},{1,3},{2,0},{3,1},{4,6},{5,7},{6,4},{7,5},{8,10},{9,11},{10,... | collective-permute-start | bytes 110600 | tf_op jit(solution)/shard_map/ppermute | solution.py:388
  125.2 4.3 %collective-permute-start.2 = (f32[72,128]{1,0:T(8,128)S(1)}, f32[72,128]{1,0:T(8,128)S(1)}, u32[]{:S(2)}, u32[]{:S(2)}) collective-permute-start(f32[72,128]{1,0:T(8,128)S(1)} %add.104), channel_id=1, source_target_pairs={{0,16},{1,17},{2,18},{3,19},{4,20},{5,21},{6,22},{7,23},{8,24},{9,... | collective-permute-start | bytes 110600 | tf_op jit(solution)/shard_map/ppermute | solution.py:388
  126.7 4.9 %collective-permute-start.3 = (f32[72,128]{1,0:T(8,128)S(1)}, f32[72,128]{1,0:T(8,128)S(1)}, u32[]{:S(2)}, u32[]{:S(2)}) collective-permute-start(f32[72,128]{1,0:T(8,128)S(1)} %add.104), channel_id=1, source_target_pairs={{0,18},{1,19},{2,16},{3,17},{4,22},{5,23},{6,20},{7,21},{8,26},{9,... | collective-permute-start | bytes 110600 | tf_op jit(solution)/shard_map/ppermute | solution.py:388
  131.5 4.5 %collective-permute-start.4 = (f32[72,128]{1,0:T(8,128)S(1)}, f32[72,128]{1,0:T(8,128)S(1)}, u32[]{:S(2)}, u32[]{:S(2)}) collective-permute-start(f32[72,128]{1,0:T(8,128)S(1)} %add_add_fusion.refs_0_), channel_id=1, source_target_pairs={{0,4},{1,5},{2,6},{3,7},{4,0},{5,1},{6,2},{7,3},{8,12},{9,13},{10,... | collective-permute-start | bytes 110600 | tf_op jit(solution)/shard_map/ppermute | solution.py:388
  131.6 5.1 %collective-permute-start.5 = (f32[72,128]{1,0:T(8,128)S(1)}, f32[72,128]{1,0:T(8,128)S(1)}, u32[]{:S(2)}, u32[]{:S(2)}) collective-permute-start(f32[72,128]{1,0:T(8,128)S(1)} %add_add_fusion.refs_0_), channel_id=1, source_target_pairs={{0,8},{1,9},{2,10},{3,11},{4,12},{5,13},{6,14},{7,15},{8,0},{9,1},... | collective-permute-start | bytes 110600 | tf_op jit(solution)/shard_map/ppermute | solution.py:388
  133.6 5.8 %collective-permute-start.6 = (f32[72,128]{1,0:T(8,128)S(1)}, f32[72,128]{1,0:T(8,128)S(1)}, u32[]{:S(2)}, u32[]{:S(2)}) collective-permute-start(f32[72,128]{1,0:T(8,128)S(1)} %add_add_fusion.refs_0_), channel_id=1, source_target_pairs={{0,12},{1,13},{2,14},{3,15},{4,8},{5,9},{6,10},{7,11},{8,4},{9,5},... | collective-permute-start | bytes 110600 | tf_op jit(solution)/shard_map/ppermute | solution.py:388

commit v7 on v6

--- a/solution.py
+++ b/solution.py
@@ -13,7 +13,7 @@
 NTH = 256
 COL_TILE = 256
 LANES = 128
-PIVOTS = 4
+PIVOTS = 16
 SNAPSHOT_TILE = 16
 EARLY_ROWS = 6
 VMEM_BYTES = 50 * 2**20
@@ -349,24 +349,28 @@
         for fetch in fetches:
             fetch.wait()
 
-    both = jnp.dot(mix_ref[...], held[row], preferred_element_type=jnp.float32)
-    out_ref[...] = both[:rank] + both[rank:]
+    cols = held.shape[2]
+    for i in range(out_ref.shape[1] // cols):
+        modes = held[row * (out_ref.shape[1] // cols) + i]
+        both = jnp.dot(mix_ref[...], modes, preferred_element_type=jnp.float32)
+        out_ref[:, i * cols : (i + 1) * cols] = both[:rank] + both[rank:]
 
 
 def merge_and_mix(gram_parts, test_matrix, early, late):
     split, height, cols = early.shape
     rows = split + late.shape[0]
+    some = rows if rows % 2 else rows // 2
     rank = test_matrix.shape[1]
     return pl.pallas_call(
         functools.partial(merge_kernel, split=split),
-        grid=(rows,),
+        grid=(rows // some,),
         in_specs=[
             *[pl.BlockSpec(part.shape, lambda i: (0, 0)) for part in gram_parts],
             pl.BlockSpec((rank, 2 * rank), lambda i: (0, 0)),
             pl.BlockSpec(memory_space=pl.ANY),
             pl.BlockSpec(memory_space=pl.ANY),
         ],
-        out_specs=pl.BlockSpec((rank, cols), lambda i: (0, i)),
+        out_specs=pl.BlockSpec((rank, some * cols), lambda i: (0, i)),
         out_shape=jax.ShapeDtypeStruct((rank, rows * cols), jnp.float32),
         scratch_shapes=[
             pltpu.VMEM((2 * rank, height), jnp.bfloat16),
@@ -419,7 +423,8 @@
 def solution(mesh):
     lon_count, group_count = mesh.shape["lon"], mesh.shape["tm"]
     device_count = lon_count * group_count
-    whole_rows = NTH % device_count == 0 and device_count & (device_count - 1) == 0
+    whole_rows = NTH % device_count == 0 and NTH >= 2 * device_count
+    whole_rows = whole_rows and device_count & (device_count - 1) == 0
     return jax.shard_map(
         local_pair if group_count == 2 and whole_rows else local_tree,
         mesh=mesh,

time: 149 us -> 146 us (0.980)
  Pallas kernels: 38.7 us -> 35.6 us
    pallas_call x1, Pallas kernels: 9.72 us -> 6.64 us  [merge_and_mix(): pl.pallas_call(functools.partial(merge_kernel, split=split), grid=(rows /...]
  transfers between devices with their start and end apart: 9 -> 9, of which waited for: 8 -> 8; matrix products, arithmetic and copies ran while one was open for 16% -> 17% of each run, Pallas kernels for 10% -> 11%
where the time goes in v7:
time: 146 us
  waiting for transfers between devices  66 us (45%)
  Pallas kernels  35.6 us (24%)
  other arithmetic  24.6 us (17%)
  starting transfers between devices  19.6 us (13%)
    all_to_all x2, waiting for transfers between devices, local_pair(): lax.all_to_all(part, ('lon', 'tm'), split_axis=0, concat_axis=0, tiled=True)  57.1 us
    pallas_call x2, Pallas kernels, spectra_and_gram(): pl.pallas_call(functools.partial(spectra_kernel, first_row=first_row), in...  22.9 us
    convert_element_type x1, other arithmetic, split_table(): high.astype(jnp.bfloat16)  21.7 us
    all_to_all x2, starting transfers between devices, local_pair(): lax.all_to_all(part, ('lon', 'tm'), split_axis=0, concat_axis=0, tiled=True)  11.6 us
    ppermute x7, waiting for transfers between devices, exchanged(): lax.ppermute(array, axes, [(i, i ^ mask) for i in range(count)])  8.88 us
    ppermute x7, starting transfers between devices, exchanged(): lax.ppermute(array, axes, [(i, i ^ mask) for i in range(count)])  8.01 us
    pallas_call x1, Pallas kernels, merge_and_mix(): pl.pallas_call(functools.partial(merge_kernel, split=split), grid=(rows /...  6.64 us
    pallas_call x1, Pallas kernels, relayout(): pl.pallas_call(relayout_kernel, grid=(rank_rows // some,), in_specs=[pl.B...  6.06 us
  transfers between devices with their start and end apart: 9, of which 8 were waited for; matrix products, arithmetic and copies ran while one was open for 17% of the time, Pallas kernels for 11%

profile of v7, /device:TPU:0, one launch (start us, length us, event | category | flops | bytes accessed | tf_op | source)
XLA Modules:
  0.0 146.1 jit_solution(10024066042021202505)
XLA Ops:
  0.0 6.1 %shard_map.28 = (bf16[32,6,64,128]{3,2,1,0:T(8,128)(2,1)}, bf16[32,2,64,128]{3,2,1,0:T(8,128)(2,1)}) custom-call(bf16[128,64,256]{2,1,0:T(8,128)(2,1)} %x_ref.1), custom_call_target="tpu_custom_call" | custom-call | tf_op jit(solution)/shard_map/pallas_call | solution.py:164
  6.1 7.3 %all-to-all-start.1 = ((bf16[32,6,64,128]{3,2,1,0:T(8,128)(2,1)}), bf16[32,6,64,128]{3,2,1,0:T(8,128)(2,1)S(1)}, u32[]{:S(2)}, u32[]{:S(2)}) async-start(bf16[32,6,64,128]{3,2,1,0:T(8,128)(2,1)} %get-tuple-element.16), calls=%async_computation.1 | async-start | bytes 6291456 | tf_op jit(solution)/shard_map/all_to_all | solution.py:416
  13.4 21.7 %reduce-precision_convert_fusion = (bf16[5,1,1024,256]{3,2,1,0:T(8,128)(2,1)S(1)}, bf16[5,1,1024,256]{3,2,1,0:T(8,128)(2,1)S(1)}) fusion(f32[5,256]{1,0:T(8,128)S(1)} %rsqrt_multiply_fusion, s32[5,256]{1,0:T(8,128)S(1)} %add_select_fusion.1, pred[5,256]{1,0:T(8,128)(4,1)S(1)} %fusion.7), kind=kLoop, calls=%fused_computation.4 | loop fusion | flops 26214400 | bytes 5254400 | tf_op jit(solution)/shard_map/convert_element_type | solution.py:121
  35.2 2.8 %pad_maximum_fusion.refs_2_ = bf16[5,2,1024,256]{3,2,1,0:T(8,128)(2,1)} fusion(bf16[5,1,1024,256]{3,2,1,0:T(8,128)(2,1)S(1)} %get-tuple-element.22, bf16[5,1,1024,256]{3,2,1,0:T(8,128)(2,1)S(1)} %get-tuple-element.21), kind=kLoop, calls=%fused_computation.9 | loop fusion | flops 2621440 | bytes 10485760 | tf_op jit(solution)/shard_map/stack | solution.py:121
  37.9 46.7 %all-to-all-done.1 = bf16[32,6,64,128]{3,2,1,0:T(8,128)(2,1)S(1)} async-done(((bf16[32,6,64,128]{3,2,1,0:T(8,128)(2,1)}), bf16[32,6,64,128]{3,2,1,0:T(8,128)(2,1)S(1)}, u32[]{:S(2)}, u32[]{:S(2)}) %all-to-all-start.1) | async-done | bytes 3145760 | tf_op jit(solution)/shard_map/all_to_all | solution.py:416
  84.6 4.3 %all-to-all-start = ((bf16[32,2,64,128]{3,2,1,0:T(8,128)(2,1)}), bf16[32,2,64,128]{3,2,1,0:T(8,128)(2,1)}, u32[]{:S(2)}, u32[]{:S(2)}) async-start(bf16[32,2,64,128]{3,2,1,0:T(8,128)(2,1)} %get-tuple-element.14), calls=%async_computation | async-start | bytes 2097152 | tf_op jit(solution)/shard_map/all_to_all | solution.py:416
  89.0 15.5 %shard_map.29 = (bf16[6,256,1280]{2,1,0:T(8,128)(2,1)}, f32[72,128]{1,0:T(8,128)S(1)}) custom-call(f32[1,8]{1,0:T(1,128)S(1)} %sine_sqrt_fusion.refs_0_, bf16[16,2,6,64,128]{4,3,2,1,0:T(8,128)(2,1)S(1)} %bitcast.3, bf16[5,2,1024,256]{3,2,1,0:T(8,128)(2,1)} %pad_maximum_fusion.refs_2_), custom_call_target="tpu_custom_call" | custom-call | flops 8053063680 | bytes 12320768 | tf_op jit(solution)/shard_map/pallas_call | solution.py:244
  104.5 0.0 copy-start
  104.5 10.5 %all-to-all-done = bf16[32,2,64,128]{3,2,1,0:T(8,128)(2,1)} async-done(((bf16[32,2,64,128]{3,2,1,0:T(8,128)(2,1)}), bf16[32,2,64,128]{3,2,1,0:T(8,128)(2,1)}, u32[]{:S(2)}, u32[]{:S(2)}) %all-to-all-start) | async-done | bytes 1048608 | tf_op jit(solution)/shard_map/all_to_all | solution.py:416
  115.0 7.5 %shard_map.30 = (bf16[2,256,1280]{2,1,0:T(8,128)(2,1)S(1)}, f32[72,128]{1,0:T(8,128)S(1)}) custom-call(f32[1,8]{1,0:T(1,128)S(1)} %sine_sqrt_fusion.refs_0_, bf16[16,2,2,64,128]{4,3,2,1,0:T(8,128)(2,1)} %bitcast.refs_1_, bf16[5,2,1024,256]{3,2,1,0:T(8,128)(2,1)} %pad_maximum_fusion.refs_2_, f32[72,128]{1,0:T(8,128)S(1)} %get-tuple-element.17.refs_3_), custom_call_target="tpu_custom_call" | custom-call | flops 2684354560 | bytes 7602176 | tf_op jit(solution)/shard_map/pallas_call | solution.py:244
  122.4 0.1 collective-permute-start
  122.5 1.2 collective-permute-done
  123.7 1.5 %collective-permute-start.1 = (f32[72,128]{1,0:T(8,128)S(1)}, f32[72,128]{1,0:T(8,128)S(1)}, u32[]{:S(2)}, u32[]{:S(2)}) collective-permute-start(f32[72,128]{1,0:T(8,128)S(1)} %add.104), channel_id=1, source_target_pairs={{0,2},{1,3},{2,0},{3,1},{4,6},{5,7},{6,4},{7,5},{8,10},{9,11},{10,... | collective-permute-start | bytes 110600 | tf_op jit(solution)/shard_map/ppermute | solution.py:392
  125.2 1.5 %collective-permute-start.2 = (f32[72,128]{1,0:T(8,128)S(1)}, f32[72,128]{1,0:T(8,128)S(1)}, u32[]{:S(2)}, u32[]{:S(2)}) collective-permute-start(f32[72,128]{1,0:T(8,128)S(1)} %add.104), channel_id=1, source_target_pairs={{0,16},{1,17},{2,18},{3,19},{4,20},{5,21},{6,22},{7,23},{8,24},{9,... | collective-permute-start | bytes 110600 | tf_op jit(solution)/shard_map/ppermute | solution.py:392
  126.7 0.5 collective-permute-start.3
  127.2 0.5 collective-permute-done.1
  127.7 1.8 %collective-permute-done.2 = f32[72,128]{1,0:T(8,128)S(1)} collective-permute-done((f32[72,128]{1,0:T(8,128)S(1)}, f32[72,128]{1,0:T(8,128)S(1)}, u32[]{:S(2)}, u32[]{:S(2)}) %collective-permute-start.2) | collective-permute-done | bytes 36896 | tf_op jit(solution)/shard_map/ppermute | solution.py:392
  129.5 2.1 %collective-permute-done.3 = f32[72,128]{1,0:T(8,128)S(1)} collective-permute-done((f32[72,128]{1,0:T(8,128)S(1)}, f32[72,128]{1,0:T(8,128)S(1)}, u32[]{:S(2)}, u32[]{:S(2)}) %collective-permute-start.3) | collective-permute-done | bytes 36896 | tf_op jit(solution)/shard_map/ppermute | solution.py:392
  131.5 0.1 collective-permute-start.4
  131.6 2.0 %collective-permute-start.5 = (f32[72,128]{1,0:T(8,128)S(1)}, f32[72,128]{1,0:T(8,128)S(1)}, u32[]{:S(2)}, u32[]{:S(2)}) collective-permute-start(f32[72,128]{1,0:T(8,128)S(1)} %add_add_fusion.refs_0_), channel_id=1, source_target_pairs={{0,8},{1,9},{2,10},{3,11},{4,12},{5,13},{6,14},{7,15},{8,0},{9,1},... | collective-permute-start | bytes 110600 | tf_op jit(solution)/shard_map/ppermute | solution.py:392
  133.6 2.4 %collective-permute-start.6 = (f32[72,128]{1,0:T(8,128)S(1)}, f32[72,128]{1,0:T(8,128)S(1)}, u32[]{:S(2)}, u32[]{:S(2)}) collective-permute-start(f32[72,128]{1,0:T(8,128)S(1)} %add_add_fusion.refs_0_), channel_id=1, source_target_pairs={{0,12},{1,13},{2,14},{3,15},{4,8},{5,9},{6,10},{7,11},{8,4},{9,5},... | collective-permute-start | bytes 110600 | tf_op jit(solution)/shard_map/ppermute | solution.py:392
  136.0 0.0 collective-permute-done.4.refs_1_
  136.0 0.7 collective-permute-done.5.refs_2_
  136.7 2.7 %collective-permute-done.6.refs_3_ = f32[72,128]{1,0:T(8,128)S(1)} collective-permute-done((f32[72,128]{1,0:T(8,128)S(1)}, f32[72,128]{1,0:T(8,128)S(1)}, u32[]{:S(2)}, u32[]{:S(2)}) %collective-permute-start.6) | collective-permute-done | bytes 36896 | tf_op jit(solution)/shard_map/ppermute | solution.py:392
  139.3 0.0 copy-done
  139.3 6.6 %shard_map.31 = f32[64,10240]{1,0:T(8,128)} custom-call(f32[72,128]{1,0:T(8,128)S(1)} %add_add_fusion.refs_0_, f32[72,128]{1,0:T(8,128)S(1)} %collective-permute-done.4.refs_1_, f32[72,128]{1,0:T(8,128)S(1)} %collective-permute-done.5.refs_2_, f32[72,128]{1,0:T(8,128)S(1)} %collective-permute-done.6.refs_3_, f32[64,128]{1,0:T(8,128)S(1)} %bitcast.4, ...), custom_call_target="tpu_custom_call" | custom-call | tf_op jit(solution)/shard_map/pallas_call | solution.py:364
  (6 shorter events, 0.1 us)
Async XLA Ops:
  6.1 78.5 %all-to-all-start.1 = ((bf16[32,6,64,128]{3,2,1,0:T(8,128)(2,1)}), bf16[32,6,64,128]{3,2,1,0:T(8,128)(2,1)S(1)}, u32[]{:S(2)}, u32[]{:S(2)}) async-start(bf16[32,6,64,128]{3,2,1,0:T(8,128)(2,1)} %get-tuple-element.16), calls=%async_computation.1 | async-start | bytes 6291456 | tf_op jit(solution)/shard_map/all_to_all | solution.py:416
  84.6 30.4 %all-to-all-start = ((bf16[32,2,64,128]{3,2,1,0:T(8,128)(2,1)}), bf16[32,2,64,128]{3,2,1,0:T(8,128)(2,1)}, u32[]{:S(2)}, u32[]{:S(2)}) async-start(bf16[32,2,64,128]{3,2,1,0:T(8,128)(2,1)} %get-tuple-element.14), calls=%async_computation | async-start | bytes 2097152 | tf_op jit(solution)/shard_map/all_to_all | solution.py:416
  104.5 34.9 %copy-start = (f32[128,64]{0,1:T(8,128)S(1)}, f32[128,64]{0,1:T(8,128)}, u32[]{:S(2)}) copy-start(f32[128,64]{0,1:T(8,128)} %param.3) | copy-start | bytes 98308
  122.4 1.3 collective-permute-start
  123.7 4.0 %collective-permute-start.1 = (f32[72,128]{1,0:T(8,128)S(1)}, f32[72,128]{1,0:T(8,128)S(1)}, u32[]{:S(2)}, u32[]{:S(2)}) collective-permute-start(f32[72,128]{1,0:T(8,128)S(1)} %add.104), channel_id=1, source_target_pairs={{0,2},{1,3},{2,0},{3,1},{4,6},{5,7},{6,4},{7,5},{8,10},{9,11},{10,... | collective-permute-start | bytes 110600 | tf_op jit(solution)/shard_map/ppermute | solution.py:392
  125.2 4.3 %collective-permute-start.2 = (f32[72,128]{1,0:T(8,128)S(1)}, f32[72,128]{1,0:T(8,128)S(1)}, u32[]{:S(2)}, u32[]{:S(2)}) collective-permute-start(f32[72,128]{1,0:T(8,128)S(1)} %add.104), channel_id=1, source_target_pairs={{0,16},{1,17},{2,18},{3,19},{4,20},{5,21},{6,22},{7,23},{8,24},{9,... | collective-permute-start | bytes 110600 | tf_op jit(solution)/shard_map/ppermute | solution.py:392
  126.7 4.9 %collective-permute-start.3 = (f32[72,128]{1,0:T(8,128)S(1)}, f32[72,128]{1,0:T(8,128)S(1)}, u32[]{:S(2)}, u32[]{:S(2)}) collective-permute-start(f32[72,128]{1,0:T(8,128)S(1)} %add.104), channel_id=1, source_target_pairs={{0,18},{1,19},{2,16},{3,17},{4,22},{5,23},{6,20},{7,21},{8,26},{9,... | collective-permute-start | bytes 110600 | tf_op jit(solution)/shard_map/ppermute | solution.py:392
  131.5 4.5 %collective-permute-start.4 = (f32[72,128]{1,0:T(8,128)S(1)}, f32[72,128]{1,0:T(8,128)S(1)}, u32[]{:S(2)}, u32[]{:S(2)}) collective-permute-start(f32[72,128]{1,0:T(8,128)S(1)} %add_add_fusion.refs_0_), channel_id=1, source_target_pairs={{0,4},{1,5},{2,6},{3,7},{4,0},{5,1},{6,2},{7,3},{8,12},{9,13},{10,... | collective-permute-start | bytes 110600 | tf_op jit(solution)/shard_map/ppermute | solution.py:392
  131.6 5.0 %collective-permute-start.5 = (f32[72,128]{1,0:T(8,128)S(1)}, f32[72,128]{1,0:T(8,128)S(1)}, u32[]{:S(2)}, u32[]{:S(2)}) collective-permute-start(f32[72,128]{1,0:T(8,128)S(1)} %add_add_fusion.refs_0_), channel_id=1, source_target_pairs={{0,8},{1,9},{2,10},{3,11},{4,12},{5,13},{6,14},{7,15},{8,0},{9,1},... | collective-permute-start | bytes 110600 | tf_op jit(solution)/shard_map/ppermute | solution.py:392
  133.6 5.8 %collective-permute-start.6 = (f32[72,128]{1,0:T(8,128)S(1)}, f32[72,128]{1,0:T(8,128)S(1)}, u32[]{:S(2)}, u32[]{:S(2)}) collective-permute-start(f32[72,128]{1,0:T(8,128)S(1)} %add_add_fusion.refs_0_), channel_id=1, source_target_pairs={{0,12},{1,13},{2,14},{3,15},{4,8},{5,9},{6,10},{7,11},{8,4},{9,5},... | collective-permute-start | bytes 110600 | tf_op jit(solution)/shard_map/ppermute | solution.py:392

commit v8 on v7

--- a/solution.py
+++ b/solution.py
@@ -174,7 +174,7 @@
 
 
 def spectra_kernel(*refs, first_row):
-    weight_ref, x_ref, table_ref, *before, modes_ref, gram_ref, lhs, acc, held, sems, own, own_sems = refs
+    weight_ref, x_ref, table_ref, *before, modes_ref, gram_ref, lhs, held, sems, own, own_sems = refs
     sources, groups, rows, rank_rows, points = x_ref.shape
     tiles = table_ref.shape[0]
     span = groups * rank_rows
@@ -189,7 +189,6 @@
     for take in takes:
         take.start()
     fetch(0).start()
-    acc[...] = jnp.zeros_like(acc)
     for src in range(sources):
         half, place = divmod(src, sources // 2)
         if place == 0:
@@ -214,21 +213,22 @@
         wavenumber = jnp.where(col_ids < MMAX, col_ids, col_ids - MMAX + 1)
         turned = (1 - 2 * (wavenumber & 1)).astype(jnp.float32)
         spectra = halves[: rows * span] + turned * halves[rows * span :]
-        tops, rests = [], []
         for row in range(rows):
             scaled = spectra[row * span : (row + 1) * span] * weight_ref[0, first_row + row]
             top = scaled.astype(jnp.bfloat16)
             rest = (scaled - top.astype(jnp.float32)).astype(jnp.bfloat16)
             modes_ref[row, :span, tile] = top
             modes_ref[row, span:, tile] = rest
-            tops.append(top)
-            rests.append(rest)
-        top = jnp.concatenate(tops, axis=1)
-        both = jnp.concatenate([top, jnp.concatenate(rests, axis=1)], axis=0)
-        acc[...] += lax.dot_general(both, top, NT_DIMS, preferred_element_type=jnp.float32)
-
-    cross = acc[span:, :]
-    gram = acc[:span, :] + (cross + cross.T)
+
+    products = [
+        lax.dot_general(
+            modes_ref[row], modes_ref[row, :span, :], NT_DIMS, preferred_element_type=jnp.float32
+        )
+        for row in range(rows)
+    ]
+    total = functools.reduce(jnp.add, products)
+    cross = total[span:]
+    gram = total[:span] + (cross + cross.T)
     packed = packed_gram(gram)
     for ref in before:
         packed += ref[...]
@@ -256,7 +256,6 @@
         ],
         scratch_shapes=[
             pltpu.VMEM((2 * rows * span, half_lons), jnp.bfloat16),
-            pltpu.VMEM((2 * span, span), jnp.float32),
             pltpu.VMEM(table.shape, table.dtype),
             pltpu.SemaphoreType.DMA((tiles,)),
             pltpu.VMEM(blocks.shape, blocks.dtype),

time: 146 us -> 146 us (level)
  Pallas kernels: 35.6 us -> 32.6 us
  waiting for transfers between devices: 66 us -> 68.1 us
    pallas_call x2, Pallas kernels: 22.9 us -> 19.9 us  [spectra_and_gram(): pl.pallas_call(functools.partial(spectra_kernel, first_row=first_row), in...]
    all_to_all x2, waiting for transfers between devices: 57.1 us -> 59.3 us  [local_pair(): lax.all_to_all(part, ('lon', 'tm'), split_axis=0, concat_axis=0, tiled=True)]
  transfers between devices with their start and end apart: 9 -> 9, of which waited for: 8 -> 8; matrix products, arithmetic and copies ran while one was open for 17% -> 17% of each run, Pallas kernels for 11% -> 9%
where the time goes in v8:
time: 146 us; the launch traced here: 145 us
  waiting for transfers between devices  68.1 us (47%)
  Pallas kernels  32.6 us (22%)
  other arithmetic  24.6 us (17%)
  starting transfers between devices  19.6 us (13%)
    all_to_all x2, waiting for transfers between devices, local_pair(): lax.all_to_all(part, ('lon', 'tm'), split_axis=0, concat_axis=0, tiled=True)  59.3 us
    convert_element_type x1, other arithmetic, split_table(): high.astype(jnp.bfloat16)  21.7 us
    pallas_call x2, Pallas kernels, spectra_and_gram(): pl.pallas_call(functools.partial(spectra_kernel, first_row=first_row), in...  19.9 us
    all_to_all x2, starting transfers between devices, local_pair(): lax.all_to_all(part, ('lon', 'tm'), split_axis=0, concat_axis=0, tiled=True)  11.6 us
    ppermute x7, waiting for transfers between devices, exchanged(): lax.ppermute(array, axes, [(i, i ^ mask) for i in range(count)])  8.88 us
    ppermute x7, starting transfers between devices, exchanged(): lax.ppermute(array, axes, [(i, i ^ mask) for i in range(count)])  8.01 us
    pallas_call x1, Pallas kernels, merge_and_mix(): pl.pallas_call(functools.partial(merge_kernel, split=split), grid=(rows /...  6.63 us
    pallas_call x1, Pallas kernels, relayout(): pl.pallas_call(relayout_kernel, grid=(rank_rows // some,), in_specs=[pl.B...  6.06 us
  transfers between devices with their start and end apart: 9, of which 8 were waited for; matrix products, arithmetic and copies ran while one was open for 17% of the time, Pallas kernels for 9%

profile of v8, /device:TPU:0, one launch (start us, length us, event | category | flops | bytes accessed | tf_op | source)
XLA Modules:
  0.0 145.3 jit_solution(18126519198316078702)
XLA Ops:
  0.0 6.1 %shard_map.28 = (bf16[32,6,64,128]{3,2,1,0:T(8,128)(2,1)}, bf16[32,2,64,128]{3,2,1,0:T(8,128)(2,1)}) custom-call(bf16[128,64,256]{2,1,0:T(8,128)(2,1)} %x_ref.1), custom_call_target="tpu_custom_call" | custom-call | tf_op jit(solution)/shard_map/pallas_call | solution.py:164
  6.1 7.3 %all-to-all-start.1 = ((bf16[32,6,64,128]{3,2,1,0:T(8,128)(2,1)}), bf16[32,6,64,128]{3,2,1,0:T(8,128)(2,1)S(1)}, u32[]{:S(2)}, u32[]{:S(2)}) async-start(bf16[32,6,64,128]{3,2,1,0:T(8,128)(2,1)} %get-tuple-element.16), calls=%async_computation.1 | async-start | bytes 6291456 | tf_op jit(solution)/shard_map/all_to_all | solution.py:415
  13.4 21.7 %reduce-precision_convert_fusion = (bf16[5,1,1024,256]{3,2,1,0:T(8,128)(2,1)S(1)}, bf16[5,1,1024,256]{3,2,1,0:T(8,128)(2,1)S(1)}) fusion(f32[5,256]{1,0:T(8,128)S(1)} %rsqrt_multiply_fusion, s32[5,256]{1,0:T(8,128)S(1)} %add_select_fusion.1, pred[5,256]{1,0:T(8,128)(4,1)S(1)} %fusion.7), kind=kLoop, calls=%fused_computation.4 | loop fusion | flops 26214400 | bytes 5254400 | tf_op jit(solution)/shard_map/convert_element_type | solution.py:121
  35.2 2.8 %pad_maximum_fusion.refs_2_ = bf16[5,2,1024,256]{3,2,1,0:T(8,128)(2,1)} fusion(bf16[5,1,1024,256]{3,2,1,0:T(8,128)(2,1)S(1)} %get-tuple-element.22, bf16[5,1,1024,256]{3,2,1,0:T(8,128)(2,1)S(1)} %get-tuple-element.21), kind=kLoop, calls=%fused_computation.9 | loop fusion | flops 2621440 | bytes 10485760 | tf_op jit(solution)/shard_map/stack | solution.py:121
  37.9 46.7 %all-to-all-done.1 = bf16[32,6,64,128]{3,2,1,0:T(8,128)(2,1)S(1)} async-done(((bf16[32,6,64,128]{3,2,1,0:T(8,128)(2,1)}), bf16[32,6,64,128]{3,2,1,0:T(8,128)(2,1)S(1)}, u32[]{:S(2)}, u32[]{:S(2)}) %all-to-all-start.1) | async-done | bytes 3145760 | tf_op jit(solution)/shard_map/all_to_all | solution.py:415
  84.6 4.3 %all-to-all-start = ((bf16[32,2,64,128]{3,2,1,0:T(8,128)(2,1)}), bf16[32,2,64,128]{3,2,1,0:T(8,128)(2,1)}, u32[]{:S(2)}, u32[]{:S(2)}) async-start(bf16[32,2,64,128]{3,2,1,0:T(8,128)(2,1)} %get-tuple-element.14), calls=%async_computation | async-start | bytes 2097152 | tf_op jit(solution)/shard_map/all_to_all | solution.py:415
  89.0 13.4 %shard_map.29 = (bf16[6,256,1280]{2,1,0:T(8,128)(2,1)}, f32[72,128]{1,0:T(8,128)S(1)}) custom-call(f32[1,8]{1,0:T(1,128)S(1)} %sine_sqrt_fusion.refs_0_, bf16[16,2,6,64,128]{4,3,2,1,0:T(8,128)(2,1)S(1)} %bitcast.3, bf16[5,2,1024,256]{3,2,1,0:T(8,128)(2,1)} %pad_maximum_fusion.refs_2_), custom_call_target="tpu_custom_call" | custom-call | flops 8053063680 | bytes 12320768 | tf_op jit(solution)/shard_map/pallas_call | solution.py:244
  102.4 0.0 copy-start
  102.4 12.6 %all-to-all-done = bf16[32,2,64,128]{3,2,1,0:T(8,128)(2,1)} async-done(((bf16[32,2,64,128]{3,2,1,0:T(8,128)(2,1)}), bf16[32,2,64,128]{3,2,1,0:T(8,128)(2,1)}, u32[]{:S(2)}, u32[]{:S(2)}) %all-to-all-start) | async-done | bytes 1048608 | tf_op jit(solution)/shard_map/all_to_all | solution.py:415
  115.0 6.6 %shard_map.30 = (bf16[2,256,1280]{2,1,0:T(8,128)(2,1)S(1)}, f32[72,128]{1,0:T(8,128)S(1)}) custom-call(f32[1,8]{1,0:T(1,128)S(1)} %sine_sqrt_fusion.refs_0_, bf16[16,2,2,64,128]{4,3,2,1,0:T(8,128)(2,1)} %bitcast.refs_1_, bf16[5,2,1024,256]{3,2,1,0:T(8,128)(2,1)} %pad_maximum_fusion.refs_2_, f32[72,128]{1,0:T(8,128)S(1)} %get-tuple-element.17.refs_3_), custom_call_target="tpu_custom_call" | custom-call | flops 2684354560 | bytes 7602176 | tf_op jit(solution)/shard_map/pallas_call | solution.py:244
  121.6 0.1 collective-permute-start
  121.6 1.2 collective-permute-done
  122.8 1.5 %collective-permute-start.1 = (f32[72,128]{1,0:T(8,128)S(1)}, f32[72,128]{1,0:T(8,128)S(1)}, u32[]{:S(2)}, u32[]{:S(2)}) collective-permute-start(f32[72,128]{1,0:T(8,128)S(1)} %add.104), channel_id=1, source_target_pairs={{0,2},{1,3},{2,0},{3,1},{4,6},{5,7},{6,4},{7,5},{8,10},{9,11},{10,... | collective-permute-start | bytes 110600 | tf_op jit(solution)/shard_map/ppermute | solution.py:391
  124.3 1.5 %collective-permute-start.2 = (f32[72,128]{1,0:T(8,128)S(1)}, f32[72,128]{1,0:T(8,128)S(1)}, u32[]{:S(2)}, u32[]{:S(2)}) collective-permute-start(f32[72,128]{1,0:T(8,128)S(1)} %add.104), channel_id=1, source_target_pairs={{0,16},{1,17},{2,18},{3,19},{4,20},{5,21},{6,22},{7,23},{8,24},{9,... | collective-permute-start | bytes 110600 | tf_op jit(solution)/shard_map/ppermute | solution.py:391
  125.8 0.5 collective-permute-start.3
  126.3 0.5 collective-permute-done.1
  126.8 1.8 %collective-permute-done.2 = f32[72,128]{1,0:T(8,128)S(1)} collective-permute-done((f32[72,128]{1,0:T(8,128)S(1)}, f32[72,128]{1,0:T(8,128)S(1)}, u32[]{:S(2)}, u32[]{:S(2)}) %collective-permute-start.2) | collective-permute-done | bytes 36896 | tf_op jit(solution)/shard_map/ppermute | solution.py:391
  128.6 2.0 %collective-permute-done.3 = f32[72,128]{1,0:T(8,128)S(1)} collective-permute-done((f32[72,128]{1,0:T(8,128)S(1)}, f32[72,128]{1,0:T(8,128)S(1)}, u32[]{:S(2)}, u32[]{:S(2)}) %collective-permute-start.3) | collective-permute-done | bytes 36896 | tf_op jit(solution)/shard_map/ppermute | solution.py:391
  130.7 0.1 collective-permute-start.4
  130.7 2.0 %collective-permute-start.5 = (f32[72,128]{1,0:T(8,128)S(1)}, f32[72,128]{1,0:T(8,128)S(1)}, u32[]{:S(2)}, u32[]{:S(2)}) collective-permute-start(f32[72,128]{1,0:T(8,128)S(1)} %add_add_fusion.refs_0_), channel_id=1, source_target_pairs={{0,8},{1,9},{2,10},{3,11},{4,12},{5,13},{6,14},{7,15},{8,0},{9,1},... | collective-permute-start | bytes 110600 | tf_op jit(solution)/shard_map/ppermute | solution.py:391
  132.7 2.4 %collective-permute-start.6 = (f32[72,128]{1,0:T(8,128)S(1)}, f32[72,128]{1,0:T(8,128)S(1)}, u32[]{:S(2)}, u32[]{:S(2)}) collective-permute-start(f32[72,128]{1,0:T(8,128)S(1)} %add_add_fusion.refs_0_), channel_id=1, source_target_pairs={{0,12},{1,13},{2,14},{3,15},{4,8},{5,9},{6,10},{7,11},{8,4},{9,5},... | collective-permute-start | bytes 110600 | tf_op jit(solution)/shard_map/ppermute | solution.py:391
  135.1 0.0 collective-permute-done.4.refs_1_
  135.1 0.7 collective-permute-done.5.refs_2_
  135.8 2.7 %collective-permute-done.6.refs_3_ = f32[72,128]{1,0:T(8,128)S(1)} collective-permute-done((f32[72,128]{1,0:T(8,128)S(1)}, f32[72,128]{1,0:T(8,128)S(1)}, u32[]{:S(2)}, u32[]{:S(2)}) %collective-permute-start.6) | collective-permute-done | bytes 36896 | tf_op jit(solution)/shard_map/ppermute | solution.py:391
  138.5 0.0 copy-done
  138.5 6.6 %shard_map.31 = f32[64,10240]{1,0:T(8,128)} custom-call(f32[72,128]{1,0:T(8,128)S(1)} %add_add_fusion.refs_0_, f32[72,128]{1,0:T(8,128)S(1)} %collective-permute-done.4.refs_1_, f32[72,128]{1,0:T(8,128)S(1)} %collective-permute-done.5.refs_2_, f32[72,128]{1,0:T(8,128)S(1)} %collective-permute-done.6.refs_3_, f32[64,128]{1,0:T(8,128)S(1)} %bitcast.4, ...), custom_call_target="tpu_custom_call" | custom-call | tf_op jit(solution)/shard_map/pallas_call | solution.py:363
  (6 shorter events, 0.1 us)
Async XLA Ops:
  6.1 78.5 %all-to-all-start.1 = ((bf16[32,6,64,128]{3,2,1,0:T(8,128)(2,1)}), bf16[32,6,64,128]{3,2,1,0:T(8,128)(2,1)S(1)}, u32[]{:S(2)}, u32[]{:S(2)}) async-start(bf16[32,6,64,128]{3,2,1,0:T(8,128)(2,1)} %get-tuple-element.16), calls=%async_computation.1 | async-start | bytes 6291456 | tf_op jit(solution)/shard_map/all_to_all | solution.py:415
  84.6 30.4 %all-to-all-start = ((bf16[32,2,64,128]{3,2,1,0:T(8,128)(2,1)}), bf16[32,2,64,128]{3,2,1,0:T(8,128)(2,1)}, u32[]{:S(2)}, u32[]{:S(2)}) async-start(bf16[32,2,64,128]{3,2,1,0:T(8,128)(2,1)} %get-tuple-element.14), calls=%async_computation | async-start | bytes 2097152 | tf_op jit(solution)/shard_map/all_to_all | solution.py:415
  102.4 36.1 %copy-start = (f32[128,64]{0,1:T(8,128)S(1)}, f32[128,64]{0,1:T(8,128)}, u32[]{:S(2)}) copy-start(f32[128,64]{0,1:T(8,128)} %param.3) | copy-start | bytes 98308
  121.6 1.3 collective-permute-start
  122.8 4.0 %collective-permute-start.1 = (f32[72,128]{1,0:T(8,128)S(1)}, f32[72,128]{1,0:T(8,128)S(1)}, u32[]{:S(2)}, u32[]{:S(2)}) collective-permute-start(f32[72,128]{1,0:T(8,128)S(1)} %add.104), channel_id=1, source_target_pairs={{0,2},{1,3},{2,0},{3,1},{4,6},{5,7},{6,4},{7,5},{8,10},{9,11},{10,... | collective-permute-start | bytes 110600 | tf_op jit(solution)/shard_map/ppermute | solution.py:391
  124.3 4.3 %collective-permute-start.2 = (f32[72,128]{1,0:T(8,128)S(1)}, f32[72,128]{1,0:T(8,128)S(1)}, u32[]{:S(2)}, u32[]{:S(2)}) collective-permute-start(f32[72,128]{1,0:T(8,128)S(1)} %add.104), channel_id=1, source_target_pairs={{0,16},{1,17},{2,18},{3,19},{4,20},{5,21},{6,22},{7,23},{8,24},{9,... | collective-permute-start | bytes 110600 | tf_op jit(solution)/shard_map/ppermute | solution.py:391
  125.8 4.9 %collective-permute-start.3 = (f32[72,128]{1,0:T(8,128)S(1)}, f32[72,128]{1,0:T(8,128)S(1)}, u32[]{:S(2)}, u32[]{:S(2)}) collective-permute-start(f32[72,128]{1,0:T(8,128)S(1)} %add.104), channel_id=1, source_target_pairs={{0,18},{1,19},{2,16},{3,17},{4,22},{5,23},{6,20},{7,21},{8,26},{9,... | collective-permute-start | bytes 110600 | tf_op jit(solution)/shard_map/ppermute | solution.py:391
  130.7 4.5 %collective-permute-start.4 = (f32[72,128]{1,0:T(8,128)S(1)}, f32[72,128]{1,0:T(8,128)S(1)}, u32[]{:S(2)}, u32[]{:S(2)}) collective-permute-start(f32[72,128]{1,0:T(8,128)S(1)} %add_add_fusion.refs_0_), channel_id=1, source_target_pairs={{0,4},{1,5},{2,6},{3,7},{4,0},{5,1},{6,2},{7,3},{8,12},{9,13},{10,... | collective-permute-start | bytes 110600 | tf_op jit(solution)/shard_map/ppermute | solution.py:391
  130.7 5.0 %collective-permute-start.5 = (f32[72,128]{1,0:T(8,128)S(1)}, f32[72,128]{1,0:T(8,128)S(1)}, u32[]{:S(2)}, u32[]{:S(2)}) collective-permute-start(f32[72,128]{1,0:T(8,128)S(1)} %add_add_fusion.refs_0_), channel_id=1, source_target_pairs={{0,8},{1,9},{2,10},{3,11},{4,12},{5,13},{6,14},{7,15},{8,0},{9,1},... | collective-permute-start | bytes 110600 | tf_op jit(solution)/shard_map/ppermute | solution.py:391
  132.7 5.8 %collective-permute-start.6 = (f32[72,128]{1,0:T(8,128)S(1)}, f32[72,128]{1,0:T(8,128)S(1)}, u32[]{:S(2)}, u32[]{:S(2)}) collective-permute-start(f32[72,128]{1,0:T(8,128)S(1)} %add_add_fusion.refs_0_), channel_id=1, source_target_pairs={{0,12},{1,13},{2,14},{3,15},{4,8},{5,9},{6,10},{7,11},{8,4},{9,5},... | collective-permute-start | bytes 110600 | tf_op jit(solution)/shard_map/ppermute | solution.py:391

commit v9 on v8

--- a/solution.py
+++ b/solution.py
@@ -14,7 +14,7 @@
 COL_TILE = 256
 LANES = 128
 PIVOTS = 16
-SNAPSHOT_TILE = 16
+SNAPSHOT_TILE = 32
 EARLY_ROWS = 6
 VMEM_BYTES = 50 * 2**20
 RELAYOUT_VMEM_BYTES = 58 * 2**20

time: 146 us -> 145 us (level)
  no operation moved by 1% of the time
where the time goes in v9:
time: 145 us
  waiting for transfers between devices  68.1 us (47%)
  Pallas kernels  32.2 us (22%)
  other arithmetic  24.6 us (17%)
  starting transfers between devices  19.6 us (14%)
    all_to_all x2, waiting for transfers between devices, local_pair(): lax.all_to_all(part, ('lon', 'tm'), split_axis=0, concat_axis=0, tiled=True)  59.3 us
    convert_element_type x1, other arithmetic, split_table(): high.astype(jnp.bfloat16)  21.7 us
    pallas_call x2, Pallas kernels, spectra_and_gram(): pl.pallas_call(functools.partial(spectra_kernel, first_row=first_row), in...  19.9 us
    all_to_all x2, starting transfers between devices, local_pair(): lax.all_to_all(part, ('lon', 'tm'), split_axis=0, concat_axis=0, tiled=True)  11.6 us
    ppermute x7, waiting for transfers between devices, exchanged(): lax.ppermute(array, axes, [(i, i ^ mask) for i in range(count)])  8.88 us
    ppermute x7, starting transfers between devices, exchanged(): lax.ppermute(array, axes, [(i, i ^ mask) for i in range(count)])  8.01 us
    pallas_call x1, Pallas kernels, merge_and_mix(): pl.pallas_call(functools.partial(merge_kernel, split=split), grid=(rows /...  6.63 us
    pallas_call x1, Pallas kernels, relayout(): pl.pallas_call(relayout_kernel, grid=(rank_rows // some,), in_specs=[pl.B...  5.62 us
  transfers between devices with their start and end apart: 9, of which 8 were waited for; matrix products, arithmetic and copies ran while one was open for 17% of the time, Pallas kernels for 9%

profile of v9, /device:TPU:0, one launch (start us, length us, event | category | flops | bytes accessed | tf_op | source)
XLA Modules:
  0.0 144.8 jit_solution(6251865415566266384)
XLA Ops:
  0.0 5.6 %shard_map.28 = (bf16[32,6,64,128]{3,2,1,0:T(8,128)(2,1)}, bf16[32,2,64,128]{3,2,1,0:T(8,128)(2,1)}) custom-call(bf16[128,64,256]{2,1,0:T(8,128)(2,1)} %x_ref.1), custom_call_target="tpu_custom_call" | custom-call | tf_op jit(solution)/shard_map/pallas_call | solution.py:164
  5.6 7.3 %all-to-all-start.1 = ((bf16[32,6,64,128]{3,2,1,0:T(8,128)(2,1)}), bf16[32,6,64,128]{3,2,1,0:T(8,128)(2,1)S(1)}, u32[]{:S(2)}, u32[]{:S(2)}) async-start(bf16[32,6,64,128]{3,2,1,0:T(8,128)(2,1)} %get-tuple-element.16), calls=%async_computation.1 | async-start | bytes 6291456 | tf_op jit(solution)/shard_map/all_to_all | solution.py:415
  13.0 21.7 %reduce-precision_convert_fusion = (bf16[5,1,1024,256]{3,2,1,0:T(8,128)(2,1)S(1)}, bf16[5,1,1024,256]{3,2,1,0:T(8,128)(2,1)S(1)}) fusion(f32[5,256]{1,0:T(8,128)S(1)} %rsqrt_multiply_fusion, s32[5,256]{1,0:T(8,128)S(1)} %add_select_fusion.1, pred[5,256]{1,0:T(8,128)(4,1)S(1)} %fusion.7), kind=kLoop, calls=%fused_computation.4 | loop fusion | flops 26214400 | bytes 5254400 | tf_op jit(solution)/shard_map/convert_element_type | solution.py:121
  34.7 2.8 %pad_maximum_fusion.refs_2_ = bf16[5,2,1024,256]{3,2,1,0:T(8,128)(2,1)} fusion(bf16[5,1,1024,256]{3,2,1,0:T(8,128)(2,1)S(1)} %get-tuple-element.22, bf16[5,1,1024,256]{3,2,1,0:T(8,128)(2,1)S(1)} %get-tuple-element.21), kind=kLoop, calls=%fused_computation.9 | loop fusion | flops 2621440 | bytes 10485760 | tf_op jit(solution)/shard_map/stack | solution.py:121
  37.5 46.7 %all-to-all-done.1 = bf16[32,6,64,128]{3,2,1,0:T(8,128)(2,1)S(1)} async-done(((bf16[32,6,64,128]{3,2,1,0:T(8,128)(2,1)}), bf16[32,6,64,128]{3,2,1,0:T(8,128)(2,1)S(1)}, u32[]{:S(2)}, u32[]{:S(2)}) %all-to-all-start.1) | async-done | bytes 3145760 | tf_op jit(solution)/shard_map/all_to_all | solution.py:415
  84.1 4.3 %all-to-all-start = ((bf16[32,2,64,128]{3,2,1,0:T(8,128)(2,1)}), bf16[32,2,64,128]{3,2,1,0:T(8,128)(2,1)}, u32[]{:S(2)}, u32[]{:S(2)}) async-start(bf16[32,2,64,128]{3,2,1,0:T(8,128)(2,1)} %get-tuple-element.14), calls=%async_computation | async-start | bytes 2097152 | tf_op jit(solution)/shard_map/all_to_all | solution.py:415
  88.5 13.4 %shard_map.29 = (bf16[6,256,1280]{2,1,0:T(8,128)(2,1)}, f32[72,128]{1,0:T(8,128)S(1)}) custom-call(f32[1,8]{1,0:T(1,128)S(1)} %sine_sqrt_fusion.refs_0_, bf16[16,2,6,64,128]{4,3,2,1,0:T(8,128)(2,1)S(1)} %bitcast.3, bf16[5,2,1024,256]{3,2,1,0:T(8,128)(2,1)} %pad_maximum_fusion.refs_2_), custom_call_target="tpu_custom_call" | custom-call | flops 8053063680 | bytes 12320768 | tf_op jit(solution)/shard_map/pallas_call | solution.py:244
  101.9 0.0 copy-start
  101.9 12.6 %all-to-all-done = bf16[32,2,64,128]{3,2,1,0:T(8,128)(2,1)} async-done(((bf16[32,2,64,128]{3,2,1,0:T(8,128)(2,1)}), bf16[32,2,64,128]{3,2,1,0:T(8,128)(2,1)}, u32[]{:S(2)}, u32[]{:S(2)}) %all-to-all-start) | async-done | bytes 1048608 | tf_op jit(solution)/shard_map/all_to_all | solution.py:415
  114.5 6.6 %shard_map.30 = (bf16[2,256,1280]{2,1,0:T(8,128)(2,1)S(1)}, f32[72,128]{1,0:T(8,128)S(1)}) custom-call(f32[1,8]{1,0:T(1,128)S(1)} %sine_sqrt_fusion.refs_0_, bf16[16,2,2,64,128]{4,3,2,1,0:T(8,128)(2,1)} %bitcast.refs_1_, bf16[5,2,1024,256]{3,2,1,0:T(8,128)(2,1)} %pad_maximum_fusion.refs_2_, f32[72,128]{1,0:T(8,128)S(1)} %get-tuple-element.17.refs_3_), custom_call_target="tpu_custom_call" | custom-call | flops 2684354560 | bytes 7602176 | tf_op jit(solution)/shard_map/pallas_call | solution.py:244
  121.1 0.1 collective-permute-start
  121.2 1.2 collective-permute-done
  122.4 1.5 %collective-permute-start.1 = (f32[72,128]{1,0:T(8,128)S(1)}, f32[72,128]{1,0:T(8,128)S(1)}, u32[]{:S(2)}, u32[]{:S(2)}) collective-permute-start(f32[72,128]{1,0:T(8,128)S(1)} %add.104), channel_id=1, source_target_pairs={{0,2},{1,3},{2,0},{3,1},{4,6},{5,7},{6,4},{7,5},{8,10},{9,11},{10,... | collective-permute-start | bytes 110600 | tf_op jit(solution)/shard_map/ppermute | solution.py:391
  123.9 1.5 %collective-permute-start.2 = (f32[72,128]{1,0:T(8,128)S(1)}, f32[72,128]{1,0:T(8,128)S(1)}, u32[]{:S(2)}, u32[]{:S(2)}) collective-permute-start(f32[72,128]{1,0:T(8,128)S(1)} %add.104), channel_id=1, source_target_pairs={{0,16},{1,17},{2,18},{3,19},{4,20},{5,21},{6,22},{7,23},{8,24},{9,... | collective-permute-start | bytes 110600 | tf_op jit(solution)/shard_map/ppermute | solution.py:391
  125.3 0.5 collective-permute-start.3
  125.9 0.5 collective-permute-done.1
  126.3 1.8 %collective-permute-done.2 = f32[72,128]{1,0:T(8,128)S(1)} collective-permute-done((f32[72,128]{1,0:T(8,128)S(1)}, f32[72,128]{1,0:T(8,128)S(1)}, u32[]{:S(2)}, u32[]{:S(2)}) %collective-permute-start.2) | collective-permute-done | bytes 36896 | tf_op jit(solution)/shard_map/ppermute | solution.py:391
  128.2 2.0 %collective-permute-done.3 = f32[72,128]{1,0:T(8,128)S(1)} collective-permute-done((f32[72,128]{1,0:T(8,128)S(1)}, f32[72,128]{1,0:T(8,128)S(1)}, u32[]{:S(2)}, u32[]{:S(2)}) %collective-permute-start.3) | collective-permute-done | bytes 36896 | tf_op jit(solution)/shard_map/ppermute | solution.py:391
  130.2 0.1 collective-permute-start.4
  130.3 2.0 %collective-permute-start.5 = (f32[72,128]{1,0:T(8,128)S(1)}, f32[72,128]{1,0:T(8,128)S(1)}, u32[]{:S(2)}, u32[]{:S(2)}) collective-permute-start(f32[72,128]{1,0:T(8,128)S(1)} %add_add_fusion.refs_0_), channel_id=1, source_target_pairs={{0,8},{1,9},{2,10},{3,11},{4,12},{5,13},{6,14},{7,15},{8,0},{9,1},... | collective-permute-start | bytes 110600 | tf_op jit(solution)/shard_map/ppermute | solution.py:391
  132.3 2.4 %collective-permute-start.6 = (f32[72,128]{1,0:T(8,128)S(1)}, f32[72,128]{1,0:T(8,128)S(1)}, u32[]{:S(2)}, u32[]{:S(2)}) collective-permute-start(f32[72,128]{1,0:T(8,128)S(1)} %add_add_fusion.refs_0_), channel_id=1, source_target_pairs={{0,12},{1,13},{2,14},{3,15},{4,8},{5,9},{6,10},{7,11},{8,4},{9,5},... | collective-permute-start | bytes 110600 | tf_op jit(solution)/shard_map/ppermute | solution.py:391
  134.7 0.0 collective-permute-done.4.refs_1_
  134.7 0.7 collective-permute-done.5.refs_2_
  135.3 2.7 %collective-permute-done.6.refs_3_ = f32[72,128]{1,0:T(8,128)S(1)} collective-permute-done((f32[72,128]{1,0:T(8,128)S(1)}, f32[72,128]{1,0:T(8,128)S(1)}, u32[]{:S(2)}, u32[]{:S(2)}) %collective-permute-start.6) | collective-permute-done | bytes 36896 | tf_op jit(solution)/shard_map/ppermute | solution.py:391
  138.0 0.0 copy-done
  138.0 6.6 %shard_map.31 = f32[64,10240]{1,0:T(8,128)} custom-call(f32[72,128]{1,0:T(8,128)S(1)} %add_add_fusion.refs_0_, f32[72,128]{1,0:T(8,128)S(1)} %collective-permute-done.4.refs_1_, f32[72,128]{1,0:T(8,128)S(1)} %collective-permute-done.5.refs_2_, f32[72,128]{1,0:T(8,128)S(1)} %collective-permute-done.6.refs_3_, f32[64,128]{1,0:T(8,128)S(1)} %bitcast.4, ...), custom_call_target="tpu_custom_call" | custom-call | tf_op jit(solution)/shard_map/pallas_call | solution.py:363
  (6 shorter events, 0.1 us)
Async XLA Ops:
  5.6 78.5 %all-to-all-start.1 = ((bf16[32,6,64,128]{3,2,1,0:T(8,128)(2,1)}), bf16[32,6,64,128]{3,2,1,0:T(8,128)(2,1)S(1)}, u32[]{:S(2)}, u32[]{:S(2)}) async-start(bf16[32,6,64,128]{3,2,1,0:T(8,128)(2,1)} %get-tuple-element.16), calls=%async_computation.1 | async-start | bytes 6291456 | tf_op jit(solution)/shard_map/all_to_all | solution.py:415
  84.1 30.4 %all-to-all-start = ((bf16[32,2,64,128]{3,2,1,0:T(8,128)(2,1)}), bf16[32,2,64,128]{3,2,1,0:T(8,128)(2,1)}, u32[]{:S(2)}, u32[]{:S(2)}) async-start(bf16[32,2,64,128]{3,2,1,0:T(8,128)(2,1)} %get-tuple-element.14), calls=%async_computation | async-start | bytes 2097152 | tf_op jit(solution)/shard_map/all_to_all | solution.py:415
  101.9 36.1 %copy-start = (f32[128,64]{0,1:T(8,128)S(1)}, f32[128,64]{0,1:T(8,128)}, u32[]{:S(2)}) copy-start(f32[128,64]{0,1:T(8,128)} %param.3) | copy-start | bytes 98308
  121.1 1.3 collective-permute-start
  122.4 4.0 %collective-permute-start.1 = (f32[72,128]{1,0:T(8,128)S(1)}, f32[72,128]{1,0:T(8,128)S(1)}, u32[]{:S(2)}, u32[]{:S(2)}) collective-permute-start(f32[72,128]{1,0:T(8,128)S(1)} %add.104), channel_id=1, source_target_pairs={{0,2},{1,3},{2,0},{3,1},{4,6},{5,7},{6,4},{7,5},{8,10},{9,11},{10,... | collective-permute-start | bytes 110600 | tf_op jit(solution)/shard_map/ppermute | solution.py:391
  123.9 4.3 %collective-permute-start.2 = (f32[72,128]{1,0:T(8,128)S(1)}, f32[72,128]{1,0:T(8,128)S(1)}, u32[]{:S(2)}, u32[]{:S(2)}) collective-permute-start(f32[72,128]{1,0:T(8,128)S(1)} %add.104), channel_id=1, source_target_pairs={{0,16},{1,17},{2,18},{3,19},{4,20},{5,21},{6,22},{7,23},{8,24},{9,... | collective-permute-start | bytes 110600 | tf_op jit(solution)/shard_map/ppermute | solution.py:391
  125.3 4.9 %collective-permute-start.3 = (f32[72,128]{1,0:T(8,128)S(1)}, f32[72,128]{1,0:T(8,128)S(1)}, u32[]{:S(2)}, u32[]{:S(2)}) collective-permute-start(f32[72,128]{1,0:T(8,128)S(1)} %add.104), channel_id=1, source_target_pairs={{0,18},{1,19},{2,16},{3,17},{4,22},{5,23},{6,20},{7,21},{8,26},{9,... | collective-permute-start | bytes 110600 | tf_op jit(solution)/shard_map/ppermute | solution.py:391
  130.2 4.5 %collective-permute-start.4 = (f32[72,128]{1,0:T(8,128)S(1)}, f32[72,128]{1,0:T(8,128)S(1)}, u32[]{:S(2)}, u32[]{:S(2)}) collective-permute-start(f32[72,128]{1,0:T(8,128)S(1)} %add_add_fusion.refs_0_), channel_id=1, source_target_pairs={{0,4},{1,5},{2,6},{3,7},{4,0},{5,1},{6,2},{7,3},{8,12},{9,13},{10,... | collective-permute-start | bytes 110600 | tf_op jit(solution)/shard_map/ppermute | solution.py:391
  130.3 5.0 %collective-permute-start.5 = (f32[72,128]{1,0:T(8,128)S(1)}, f32[72,128]{1,0:T(8,128)S(1)}, u32[]{:S(2)}, u32[]{:S(2)}) collective-permute-start(f32[72,128]{1,0:T(8,128)S(1)} %add_add_fusion.refs_0_), channel_id=1, source_target_pairs={{0,8},{1,9},{2,10},{3,11},{4,12},{5,13},{6,14},{7,15},{8,0},{9,1},... | collective-permute-start | bytes 110600 | tf_op jit(solution)/shard_map/ppermute | solution.py:391
  132.3 5.8 %collective-permute-start.6 = (f32[72,128]{1,0:T(8,128)S(1)}, f32[72,128]{1,0:T(8,128)S(1)}, u32[]{:S(2)}, u32[]{:S(2)}) collective-permute-start(f32[72,128]{1,0:T(8,128)S(1)} %add_add_fusion.refs_0_), channel_id=1, source_target_pairs={{0,12},{1,13},{2,14},{3,15},{4,8},{5,9},{6,10},{7,11},{8,4},{9,5},... | collective-permute-start | bytes 110600 | tf_op jit(solution)/shard_map/ppermute | solution.py:391

commit v10 on v9

--- a/solution.py
+++ b/solution.py
@@ -13,7 +13,7 @@
 NTH = 256
 COL_TILE = 256
 LANES = 128
-PIVOTS = 16
+PIVOTS = 32
 SNAPSHOT_TILE = 32
 EARLY_ROWS = 6
 VMEM_BYTES = 50 * 2**20

time: 145 us -> 147 us (1.014)
  Pallas kernels: 32.2 us -> 34 us
    pallas_call x1, Pallas kernels: 6.63 us -> 8.45 us  [merge_and_mix(): pl.pallas_call(functools.partial(merge_kernel, split=split), grid=(rows /...]
where the time goes in v10:
time: 147 us
  waiting for transfers between devices  68.1 us (46%)
  Pallas kernels  34 us (23%)
  other arithmetic  24.6 us (17%)
  starting transfers between devices  19.6 us (13%)
    all_to_all x2, waiting for transfers between devices, local_pair(): lax.all_to_all(part, ('lon', 'tm'), split_axis=0, concat_axis=0, tiled=True)  59.3 us
    convert_element_type x1, other arithmetic, split_table(): high.astype(jnp.bfloat16)  21.7 us
    pallas_call x2, Pallas kernels, spectra_and_gram(): pl.pallas_call(functools.partial(spectra_kernel, first_row=first_row), in...  19.9 us
    all_to_all x2, starting transfers between devices, local_pair(): lax.all_to_all(part, ('lon', 'tm'), split_axis=0, concat_axis=0, tiled=True)  11.6 us
    ppermute x7, waiting for transfers between devices, exchanged(): lax.ppermute(array, axes, [(i, i ^ mask) for i in range(count)])  8.88 us
    pallas_call x1, Pallas kernels, merge_and_mix(): pl.pallas_call(functools.partial(merge_kernel, split=split), grid=(rows /...  8.45 us
    ppermute x7, starting transfers between devices, exchanged(): lax.ppermute(array, axes, [(i, i ^ mask) for i in range(count)])  8.01 us
    pallas_call x1, Pallas kernels, relayout(): pl.pallas_call(relayout_kernel, grid=(rank_rows // some,), in_specs=[pl.B...  5.62 us
  transfers between devices with their start and end apart: 9, of which 8 were waited for; matrix products, arithmetic and copies ran while one was open for 17% of the time, Pallas kernels for 9%

profile of v10, /device:TPU:0, one launch (start us, length us, event | category | flops | bytes accessed | tf_op | source)
XLA Modules:
  0.0 146.6 jit_solution(14035524225212405916)
XLA Ops:
  0.0 5.6 %shard_map.28 = (bf16[32,6,64,128]{3,2,1,0:T(8,128)(2,1)}, bf16[32,2,64,128]{3,2,1,0:T(8,128)(2,1)}) custom-call(bf16[128,64,256]{2,1,0:T(8,128)(2,1)} %x_ref.1), custom_call_target="tpu_custom_call" | custom-call | tf_op jit(solution)/shard_map/pallas_call | solution.py:164
  5.6 7.3 %all-to-all-start.1 = ((bf16[32,6,64,128]{3,2,1,0:T(8,128)(2,1)}), bf16[32,6,64,128]{3,2,1,0:T(8,128)(2,1)S(1)}, u32[]{:S(2)}, u32[]{:S(2)}) async-start(bf16[32,6,64,128]{3,2,1,0:T(8,128)(2,1)} %get-tuple-element.16), calls=%async_computation.1 | async-start | bytes 6291456 | tf_op jit(solution)/shard_map/all_to_all | solution.py:415
  13.0 21.7 %reduce-precision_convert_fusion = (bf16[5,1,1024,256]{3,2,1,0:T(8,128)(2,1)S(1)}, bf16[5,1,1024,256]{3,2,1,0:T(8,128)(2,1)S(1)}) fusion(f32[5,256]{1,0:T(8,128)S(1)} %rsqrt_multiply_fusion, s32[5,256]{1,0:T(8,128)S(1)} %add_select_fusion.1, pred[5,256]{1,0:T(8,128)(4,1)S(1)} %fusion.7), kind=kLoop, calls=%fused_computation.4 | loop fusion | flops 26214400 | bytes 5254400 | tf_op jit(solution)/shard_map/convert_element_type | solution.py:121
  34.7 2.8 %pad_maximum_fusion.refs_2_ = bf16[5,2,1024,256]{3,2,1,0:T(8,128)(2,1)} fusion(bf16[5,1,1024,256]{3,2,1,0:T(8,128)(2,1)S(1)} %get-tuple-element.22, bf16[5,1,1024,256]{3,2,1,0:T(8,128)(2,1)S(1)} %get-tuple-element.21), kind=kLoop, calls=%fused_computation.9 | loop fusion | flops 2621440 | bytes 10485760 | tf_op jit(solution)/shard_map/stack | solution.py:121
  37.5 46.7 %all-to-all-done.1 = bf16[32,6,64,128]{3,2,1,0:T(8,128)(2,1)S(1)} async-done(((bf16[32,6,64,128]{3,2,1,0:T(8,128)(2,1)}), bf16[32,6,64,128]{3,2,1,0:T(8,128)(2,1)S(1)}, u32[]{:S(2)}, u32[]{:S(2)}) %all-to-all-start.1) | async-done | bytes 3145760 | tf_op jit(solution)/shard_map/all_to_all | solution.py:415
  84.1 4.3 %all-to-all-start = ((bf16[32,2,64,128]{3,2,1,0:T(8,128)(2,1)}), bf16[32,2,64,128]{3,2,1,0:T(8,128)(2,1)}, u32[]{:S(2)}, u32[]{:S(2)}) async-start(bf16[32,2,64,128]{3,2,1,0:T(8,128)(2,1)} %get-tuple-element.14), calls=%async_computation | async-start | bytes 2097152 | tf_op jit(solution)/shard_map/all_to_all | solution.py:415
  88.5 13.4 %shard_map.29 = (bf16[6,256,1280]{2,1,0:T(8,128)(2,1)}, f32[72,128]{1,0:T(8,128)S(1)}) custom-call(f32[1,8]{1,0:T(1,128)S(1)} %sine_sqrt_fusion.refs_0_, bf16[16,2,6,64,128]{4,3,2,1,0:T(8,128)(2,1)S(1)} %bitcast.3, bf16[5,2,1024,256]{3,2,1,0:T(8,128)(2,1)} %pad_maximum_fusion.refs_2_), custom_call_target="tpu_custom_call" | custom-call | flops 8053063680 | bytes 12320768 | tf_op jit(solution)/shard_map/pallas_call | solution.py:244
  101.9 0.0 copy-start
  101.9 12.6 %all-to-all-done = bf16[32,2,64,128]{3,2,1,0:T(8,128)(2,1)} async-done(((bf16[32,2,64,128]{3,2,1,0:T(8,128)(2,1)}), bf16[32,2,64,128]{3,2,1,0:T(8,128)(2,1)}, u32[]{:S(2)}, u32[]{:S(2)}) %all-to-all-start) | async-done | bytes 1048608 | tf_op jit(solution)/shard_map/all_to_all | solution.py:415
  114.5 6.6 %shard_map.30 = (bf16[2,256,1280]{2,1,0:T(8,128)(2,1)S(1)}, f32[72,128]{1,0:T(8,128)S(1)}) custom-call(f32[1,8]{1,0:T(1,128)S(1)} %sine_sqrt_fusion.refs_0_, bf16[16,2,2,64,128]{4,3,2,1,0:T(8,128)(2,1)} %bitcast.refs_1_, bf16[5,2,1024,256]{3,2,1,0:T(8,128)(2,1)} %pad_maximum_fusion.refs_2_, f32[72,128]{1,0:T(8,128)S(1)} %get-tuple-element.17.refs_3_), custom_call_target="tpu_custom_call" | custom-call | flops 2684354560 | bytes 7602176 | tf_op jit(solution)/shard_map/pallas_call | solution.py:244
  121.1 0.1 collective-permute-start
  121.2 1.2 collective-permute-done
  122.4 1.5 %collective-permute-start.1 = (f32[72,128]{1,0:T(8,128)S(1)}, f32[72,128]{1,0:T(8,128)S(1)}, u32[]{:S(2)}, u32[]{:S(2)}) collective-permute-start(f32[72,128]{1,0:T(8,128)S(1)} %add.104), channel_id=1, source_target_pairs={{0,2},{1,3},{2,0},{3,1},{4,6},{5,7},{6,4},{7,5},{8,10},{9,11},{10,... | collective-permute-start | bytes 110600 | tf_op jit(solution)/shard_map/ppermute | solution.py:391
  123.9 1.5 %collective-permute-start.2 = (f32[72,128]{1,0:T(8,128)S(1)}, f32[72,128]{1,0:T(8,128)S(1)}, u32[]{:S(2)}, u32[]{:S(2)}) collective-permute-start(f32[72,128]{1,0:T(8,128)S(1)} %add.104), channel_id=1, source_target_pairs={{0,16},{1,17},{2,18},{3,19},{4,20},{5,21},{6,22},{7,23},{8,24},{9,... | collective-permute-start | bytes 110600 | tf_op jit(solution)/shard_map/ppermute | solution.py:391
  125.3 0.5 collective-permute-start.3
  125.9 0.5 collective-permute-done.1
  126.3 1.8 %collective-permute-done.2 = f32[72,128]{1,0:T(8,128)S(1)} collective-permute-done((f32[72,128]{1,0:T(8,128)S(1)}, f32[72,128]{1,0:T(8,128)S(1)}, u32[]{:S(2)}, u32[]{:S(2)}) %collective-permute-start.2) | collective-permute-done | bytes 36896 | tf_op jit(solution)/shard_map/ppermute | solution.py:391
  128.2 2.0 %collective-permute-done.3 = f32[72,128]{1,0:T(8,128)S(1)} collective-permute-done((f32[72,128]{1,0:T(8,128)S(1)}, f32[72,128]{1,0:T(8,128)S(1)}, u32[]{:S(2)}, u32[]{:S(2)}) %collective-permute-start.3) | collective-permute-done | bytes 36896 | tf_op jit(solution)/shard_map/ppermute | solution.py:391
  130.2 0.1 collective-permute-start.4
  130.3 2.0 %collective-permute-start.5 = (f32[72,128]{1,0:T(8,128)S(1)}, f32[72,128]{1,0:T(8,128)S(1)}, u32[]{:S(2)}, u32[]{:S(2)}) collective-permute-start(f32[72,128]{1,0:T(8,128)S(1)} %add_add_fusion.refs_0_), channel_id=1, source_target_pairs={{0,8},{1,9},{2,10},{3,11},{4,12},{5,13},{6,14},{7,15},{8,0},{9,1},... | collective-permute-start | bytes 110600 | tf_op jit(solution)/shard_map/ppermute | solution.py:391
  132.3 2.4 %collective-permute-start.6 = (f32[72,128]{1,0:T(8,128)S(1)}, f32[72,128]{1,0:T(8,128)S(1)}, u32[]{:S(2)}, u32[]{:S(2)}) collective-permute-start(f32[72,128]{1,0:T(8,128)S(1)} %add_add_fusion.refs_0_), channel_id=1, source_target_pairs={{0,12},{1,13},{2,14},{3,15},{4,8},{5,9},{6,10},{7,11},{8,4},{9,5},... | collective-permute-start | bytes 110600 | tf_op jit(solution)/shard_map/ppermute | solution.py:391
  134.7 0.0 collective-permute-done.4.refs_1_
  134.7 0.7 collective-permute-done.5.refs_2_
  135.3 2.7 %collective-permute-done.6.refs_3_ = f32[72,128]{1,0:T(8,128)S(1)} collective-permute-done((f32[72,128]{1,0:T(8,128)S(1)}, f32[72,128]{1,0:T(8,128)S(1)}, u32[]{:S(2)}, u32[]{:S(2)}) %collective-permute-start.6) | collective-permute-done | bytes 36896 | tf_op jit(solution)/shard_map/ppermute | solution.py:391
  138.0 0.0 copy-done
  138.0 8.4 %shard_map.31 = f32[64,10240]{1,0:T(8,128)} custom-call(f32[72,128]{1,0:T(8,128)S(1)} %add_add_fusion.refs_0_, f32[72,128]{1,0:T(8,128)S(1)} %collective-permute-done.4.refs_1_, f32[72,128]{1,0:T(8,128)S(1)} %collective-permute-done.5.refs_2_, f32[72,128]{1,0:T(8,128)S(1)} %collective-permute-done.6.refs_3_, f32[64,128]{1,0:T(8,128)S(1)} %bitcast.4, ...), custom_call_target="tpu_custom_call" | custom-call | tf_op jit(solution)/shard_map/pallas_call | solution.py:363
  (6 shorter events, 0.1 us)
Async XLA Ops:
  5.6 78.5 %all-to-all-start.1 = ((bf16[32,6,64,128]{3,2,1,0:T(8,128)(2,1)}), bf16[32,6,64,128]{3,2,1,0:T(8,128)(2,1)S(1)}, u32[]{:S(2)}, u32[]{:S(2)}) async-start(bf16[32,6,64,128]{3,2,1,0:T(8,128)(2,1)} %get-tuple-element.16), calls=%async_computation.1 | async-start | bytes 6291456 | tf_op jit(solution)/shard_map/all_to_all | solution.py:415
  84.1 30.4 %all-to-all-start = ((bf16[32,2,64,128]{3,2,1,0:T(8,128)(2,1)}), bf16[32,2,64,128]{3,2,1,0:T(8,128)(2,1)}, u32[]{:S(2)}, u32[]{:S(2)}) async-start(bf16[32,2,64,128]{3,2,1,0:T(8,128)(2,1)} %get-tuple-element.14), calls=%async_computation | async-start | bytes 2097152 | tf_op jit(solution)/shard_map/all_to_all | solution.py:415
  101.9 36.1 %copy-start = (f32[128,64]{0,1:T(8,128)S(1)}, f32[128,64]{0,1:T(8,128)}, u32[]{:S(2)}) copy-start(f32[128,64]{0,1:T(8,128)} %param.3) | copy-start | bytes 98308
  121.1 1.3 collective-permute-start
  122.4 4.0 %collective-permute-start.1 = (f32[72,128]{1,0:T(8,128)S(1)}, f32[72,128]{1,0:T(8,128)S(1)}, u32[]{:S(2)}, u32[]{:S(2)}) collective-permute-start(f32[72,128]{1,0:T(8,128)S(1)} %add.104), channel_id=1, source_target_pairs={{0,2},{1,3},{2,0},{3,1},{4,6},{5,7},{6,4},{7,5},{8,10},{9,11},{10,... | collective-permute-start | bytes 110600 | tf_op jit(solution)/shard_map/ppermute | solution.py:391
  123.9 4.3 %collective-permute-start.2 = (f32[72,128]{1,0:T(8,128)S(1)}, f32[72,128]{1,0:T(8,128)S(1)}, u32[]{:S(2)}, u32[]{:S(2)}) collective-permute-start(f32[72,128]{1,0:T(8,128)S(1)} %add.104), channel_id=1, source_target_pairs={{0,16},{1,17},{2,18},{3,19},{4,20},{5,21},{6,22},{7,23},{8,24},{9,... | collective-permute-start | bytes 110600 | tf_op jit(solution)/shard_map/ppermute | solution.py:391
  125.3 4.9 %collective-permute-start.3 = (f32[72,128]{1,0:T(8,128)S(1)}, f32[72,128]{1,0:T(8,128)S(1)}, u32[]{:S(2)}, u32[]{:S(2)}) collective-permute-start(f32[72,128]{1,0:T(8,128)S(1)} %add.104), channel_id=1, source_target_pairs={{0,18},{1,19},{2,16},{3,17},{4,22},{5,23},{6,20},{7,21},{8,26},{9,... | collective-permute-start | bytes 110600 | tf_op jit(solution)/shard_map/ppermute | solution.py:391
  130.2 4.5 %collective-permute-start.4 = (f32[72,128]{1,0:T(8,128)S(1)}, f32[72,128]{1,0:T(8,128)S(1)}, u32[]{:S(2)}, u32[]{:S(2)}) collective-permute-start(f32[72,128]{1,0:T(8,128)S(1)} %add_add_fusion.refs_0_), channel_id=1, source_target_pairs={{0,4},{1,5},{2,6},{3,7},{4,0},{5,1},{6,2},{7,3},{8,12},{9,13},{10,... | collective-permute-start | bytes 110600 | tf_op jit(solution)/shard_map/ppermute | solution.py:391
  130.3 5.0 %collective-permute-start.5 = (f32[72,128]{1,0:T(8,128)S(1)}, f32[72,128]{1,0:T(8,128)S(1)}, u32[]{:S(2)}, u32[]{:S(2)}) collective-permute-start(f32[72,128]{1,0:T(8,128)S(1)} %add_add_fusion.refs_0_), channel_id=1, source_target_pairs={{0,8},{1,9},{2,10},{3,11},{4,12},{5,13},{6,14},{7,15},{8,0},{9,1},... | collective-permute-start | bytes 110600 | tf_op jit(solution)/shard_map/ppermute | solution.py:391
  132.3 5.8 %collective-permute-start.6 = (f32[72,128]{1,0:T(8,128)S(1)}, f32[72,128]{1,0:T(8,128)S(1)}, u32[]{:S(2)}, u32[]{:S(2)}) collective-permute-start(f32[72,128]{1,0:T(8,128)S(1)} %add_add_fusion.refs_0_), channel_id=1, source_target_pairs={{0,12},{1,13},{2,14},{3,15},{4,8},{5,9},{6,10},{7,11},{8,4},{9,5},... | collective-permute-start | bytes 110600 | tf_op jit(solution)/shard_map/ppermute | solution.py:391
